TPU v7x, 1024 devices: a whole 4x8x16 slice. The times are simulated.
1024 devices in a mesh: region: 128 (over z, y), mp: 8 (over x, core).
Axes of the slice: x: 4, y: 8, z: 16, core: 2. Of those that a mesh axis runs over, the one named last changes fastest.
Arguments:
- grid: bfloat16 [262144, 1024], P('region', 'mp'), may hold values from -6 to 6
- g2m_weight: float32 [262144], P('region'), may hold values from 0.3 to 1
- g2m_slot: int32 [262144], P('region'), may hold values from 0 to 511
- slot_node: int32 [128, 128, 4], P('region'), may hold values from 0 to 511, as said below
- peer_mask: int32 [128, 4], P('region'), may hold values 0 or 1
- norm_gain: float32 [1024], replicated, may hold values from 0.25 to 1.75
- w_qkv: bfloat16 [3, 1024, 1024], P(None, None, 'mp')
- w_out: bfloat16 [1024, 1024], P('mp'), may hold values from -0.1875 to 0.1875
Outputs:
- mesh_state: float32 [65536, 1024], P('region', 'mp')
- grid_out: bfloat16 [262144, 1024], P('region', 'mp')
Inputs may be any that keep to these rules, and one draw needn't show every extreme that they name: `slot_node`: for each mesh tile o and lane c, the entries over all grid tiles r lie in one range b * (128) to (b + 1) * 128 - 1 and name every node of that range, where the range b depends on o and c and different lanes of one mesh tile take different ranges; so every mesh node is named by some send slot, and the 4 slots of one grid tile for one mesh tile name different nodes.
All inputs are finite; a program needn't handle non-finite values. No bound on the sum of `peer_mask` on one device may be relied on, other than what follows from the above.
Results may differ from a plain program's by a relative error of at most 0.006.
Values may be sent and summed in bfloat16 or wider, within the bound.
No kernel may reach another device: no remote copies, remote signals or barrier semaphores. Data moves between devices by JAX's collectives and lax.ppermute only.
A program may use at most 64 MiB of HBM per device.

v0:
```python
import jax
import jax.numpy as jnp
from jax import lax
from jax.sharding import PartitionSpec as P

HEAD_DIM = 64
MESH_DEV = 512


OFFSETS = (-2, -1, 1, 2)


def from_everyone(array, axis):
    copies = jnp.broadcast_to(array, (lax.axis_size(axis), *array.shape))
    return lax.all_to_all(copies, axis, split_axis=0, concat_axis=0, tiled=True)


def joined_along(parts, dim):
    dims = list(parts.shape[1:])
    dims[dim] *= parts.shape[0]
    return jnp.moveaxis(parts, 0, dim).reshape(dims)


def gathered_copies(array, axis, dim):
    parts = from_everyone(array, axis)
    return joined_along(parts, dim)


def from_behind(value, axis, steps):
    count = lax.axis_size(axis)
    pairs = [(source, (source + steps) % count) for source in range(count)]
    return lax.ppermute(value, axis, pairs)


def cut_along(array, dim, devices):
    dims = array.shape
    parts = array.reshape(*dims[:dim], devices, dims[dim] // devices, *dims[dim + 1 :])
    return jnp.moveaxis(parts, dim, 0)


def sum_at_owner(array, axis, dim):
    parts = cut_along(array, dim, lax.axis_size(axis))
    arrived = lax.all_to_all(parts, axis, split_axis=0, concat_axis=0, tiled=True)
    return arrived.sum(axis=0)


def project(normed, weight):
    return jnp.dot(normed, weight, preferred_element_type=jnp.float32).astype(jnp.bfloat16)


def block_scores(queries, key_block, heads):
    rows = queries.shape[0]
    query_heads = queries.reshape(rows, heads, HEAD_DIM)
    key_heads = key_block.reshape(key_block.shape[0], heads, HEAD_DIM)
    return jnp.einsum(
        "qhd,khd->hqk", query_heads, key_heads, preferred_element_type=jnp.float32
    ) * HEAD_DIM ** (-0.5)


def block_values(weights, val_block, heads):
    val_heads = val_block.reshape(val_block.shape[0], heads, HEAD_DIM)
    return jnp.einsum("hqk,khd->qhd", weights, val_heads, preferred_element_type=jnp.float32)


def on_device(grid, g2m_weight, g2m_slot, slot_node, peer_mask, norm_gain, w_qkv, w_out):
    regions = lax.axis_size("region")
    cap = slot_node.shape[2]
    slots = regions * cap
    local_width = grid.shape[1]
    heads = local_width // HEAD_DIM
    scaled = (g2m_weight[:, None] * grid.astype(jnp.float32)).astype(jnp.bfloat16)
    slot_hot = (g2m_slot[None, :] == jnp.arange(slots, dtype=jnp.int32)[:, None]).astype(
        jnp.bfloat16
    )
    partial_value = jnp.dot(slot_hot, scaled, preferred_element_type=jnp.float32).astype(
        jnp.bfloat16
    )
    received = lax.all_to_all(
        partial_value.reshape(regions, cap, local_width),
        "region",
        split_axis=0,
        concat_axis=0,
        tiled=True,
    )
    flat_nodes = slot_node[0].reshape(-1)
    node_hot = (jnp.arange(MESH_DEV, dtype=jnp.int32)[:, None] == flat_nodes[None, :]).astype(
        jnp.bfloat16
    )
    mesh_in = jnp.dot(
        node_hot, received.reshape(-1, local_width), preferred_element_type=jnp.float32
    )
    whole = gathered_copies(mesh_in.astype(jnp.bfloat16), "mp", 1).astype(jnp.float32)
    normed = (
        whole * lax.rsqrt(jnp.mean(whole * whole, axis=-1, keepdims=True) + 1e-05) * norm_gain
    ).astype(jnp.bfloat16)
    queries = project(normed, w_qkv[0])
    keys = project(normed, w_qkv[1])
    values = project(normed, w_qkv[2])
    key_list = [keys]
    val_list = [values]
    for offset in OFFSETS:
        peer_key, peer_val = from_behind((keys, values), "region", -offset)
        key_list.append(peer_key)
        val_list.append(peer_val)
    active = jnp.concatenate([jnp.ones((1,), jnp.int32), peer_mask[0]])
    rows = queries.shape[0]
    key_block = jnp.concatenate(key_list, axis=0)
    val_block = jnp.concatenate(val_list, axis=0)
    valid = jnp.repeat(active, rows)
    scores = jnp.where(valid[None, None, :] > 0, block_scores(queries, key_block, heads), -1e30)
    top = jnp.max(scores, axis=-1, keepdims=True)
    expd = jnp.exp(scores - top)
    weights = (expd / jnp.sum(expd, axis=-1, keepdims=True)).astype(jnp.bfloat16)
    mixed = block_values(weights, val_block, heads)
    attended = mixed.astype(jnp.bfloat16).reshape(rows, local_width)
    head_terms = jnp.dot(attended, w_out, preferred_element_type=jnp.float32)
    mesh_state = mesh_in + sum_at_owner(head_terms, "mp", 1)
    mesh_back = mesh_state.astype(jnp.bfloat16)
    requested = mesh_back[flat_nodes].reshape(regions, cap, local_width)
    returned = lax.all_to_all(requested, "region", split_axis=0, concat_axis=0, tiled=True).reshape(
        slots, local_width
    )
    gathered = jnp.dot(slot_hot.T, returned, preferred_element_type=jnp.float32)
    grid_out = (grid.astype(jnp.float32) + gathered).astype(jnp.bfloat16)
    return (mesh_state, grid_out)


def solution(mesh):
    return jax.shard_map(
        on_device,
        mesh=mesh,
        in_specs=(
            P("region", "mp"),
            P("region"),
            P("region"),
            P("region", None, None),
            P("region", None),
            P(),
            P(None, None, "mp"),
            P("mp", None),
        ),
        out_specs=(P("region", "mp"), P("region", "mp")),
        check_vma=False,
    )
```

profile of v0, /device:TPU:6, one launch (start us, length us, event | category | flops | bytes accessed | tf_op | source)
XLA Modules:
  0.0 188.8 jit_solution(14086322247905275904)
XLA Ops:
  0.6 2.7 %fusion.15 = bf16[512,128]{1,0:T(8,128)(2,1)} fusion(s32[2048]{0:T(1024)} %param.10, bf16[2048,128]{1,0:T(8,128)(2,1)} %param.8, f32[2048]{0:T(1024)} %param.9), kind=kOutput, calls=%fused_computation.24 | convolution fusion | flops 270336000 | bytes 671744 | tf_op jit(solution)/shard_map/dot_general | solution.py:75
  3.4 26.3 %all-to-all-start = ((bf16[128,4,128]{2,1,0:T(4,128)(2,1)}), bf16[128,4,128]{2,1,0:T(4,128)(2,1)S(1)}, u32[]{:S(2)}, u32[]{:S(2)}) async-start(bf16[128,4,128]{2,1,0:T(4,128)(2,1)} %bitcast), calls=%async_computation | async-start | bytes 262144 | tf_op jit(solution)/shard_map/all_to_all | solution.py:78
  29.6 0.8 copy.14
  30.5 16.9 %all-to-all-done = bf16[128,4,128]{2,1,0:T(4,128)(2,1)S(1)} async-done(((bf16[128,4,128]{2,1,0:T(4,128)(2,1)}), bf16[128,4,128]{2,1,0:T(4,128)(2,1)S(1)}, u32[]{:S(2)}, u32[]{:S(2)}) %all-to-all-start) | async-done | bytes 131104 | tf_op jit(solution)/shard_map/all_to_all | solution.py:78
  47.8 1.1 broadcast_in_dim.16
  48.9 4.8 %all-to-all-start.1 = ((bf16[8,512,128]{1,2,0:T(8,128)(2,1)}), bf16[8,512,128]{1,2,0:T(8,128)(2,1)S(1)}, u32[]{:S(2)}, u32[]{:S(2)}) async-start(bf16[8,512,128]{1,2,0:T(8,128)(2,1)} %broadcast_in_dim.16), calls=%async_computation.1 | async-start | bytes 2097152 | tf_op jit(solution)/shard_map/all_to_all | solution.py:15
  53.6 0.7 add_compare_fusion
  54.5 1.1 copy.23
  55.6 11.9 %all-to-all-done.1 = bf16[8,512,128]{1,2,0:T(8,128)(2,1)S(1)} async-done(((bf16[8,512,128]{1,2,0:T(8,128)(2,1)}), bf16[8,512,128]{1,2,0:T(8,128)(2,1)S(1)}, u32[]{:S(2)}, u32[]{:S(2)}) %all-to-all-start.1) | async-done | bytes 1048608 | tf_op jit(solution)/shard_map/all_to_all | solution.py:15
  67.8 1.0 fusion.12
  68.8 0.5 constant_dynamic-update-slice_fusion.4
  69.3 3.1 %collective-permute-start = (bf16[512,128]{1,0:T(8,128)(2,1)S(1)}, bf16[512,128]{1,0:T(8,128)(2,1)S(1)}, u32[]{:S(2)}, u32[]{:S(2)}) collective-permute-start(bf16[512,128]{1,0:T(8,128)(2,1)S(1)} %get-tuple-element.7), channel_id=1, source_target_pairs={{0,16},{8,24},{16,32},{24,40},{32,48},{40,56},{48,64},{56,72},{64,... | collective-permute-start | bytes 393224 | tf_op jit(solution)/shard_map/ppermute | solution.py:32
  72.5 2.7 %collective-permute-start.1 = (bf16[512,128]{1,0:T(8,128)(2,1)S(1)}, bf16[512,128]{1,0:T(8,128)(2,1)S(1)}, u32[]{:S(2)}, u32[]{:S(2)}) collective-permute-start(bf16[512,128]{1,0:T(8,128)(2,1)S(1)} %get-tuple-element.7), channel_id=1, source_target_pairs={{0,8},{8,16},{16,24},{24,32},{32,40},{40,48},{48,56},{56,64},{64,7... | collective-permute-start | bytes 393224 | tf_op jit(solution)/shard_map/ppermute | solution.py:32
  75.2 6.4 %collective-permute-start.2 = (bf16[512,128]{1,0:T(8,128)(2,1)S(1)}, bf16[512,128]{1,0:T(8,128)(2,1)S(1)}, u32[]{:S(2)}, u32[]{:S(2)}) collective-permute-start(bf16[512,128]{1,0:T(8,128)(2,1)S(1)} %get-tuple-element.7), channel_id=1, source_target_pairs={{0,1016},{8,0},{16,8},{24,16},{32,24},{40,32},{48,40},{56,48},{64,... | collective-permute-start | bytes 393224 | tf_op jit(solution)/shard_map/ppermute | solution.py:32
  81.6 3.6 %collective-permute-start.3 = (bf16[512,128]{1,0:T(8,128)(2,1)S(1)}, bf16[512,128]{1,0:T(8,128)(2,1)S(1)}, u32[]{:S(2)}, u32[]{:S(2)}) collective-permute-start(bf16[512,128]{1,0:T(8,128)(2,1)S(1)} %get-tuple-element.7), channel_id=1, source_target_pairs={{0,1008},{8,1016},{16,0},{24,8},{32,16},{40,24},{48,32},{56,40},{6... | collective-permute-start | bytes 393224 | tf_op jit(solution)/shard_map/ppermute | solution.py:32
  85.3 0.5 constant_dynamic-update-slice_fusion.9
  85.8 0.3 convolution_convert_fusion.1
  86.1 3.1 %collective-permute-start.4 = (bf16[512,128]{1,0:T(8,128)(2,1)S(1)}, bf16[512,128]{1,0:T(8,128)(2,1)S(1)}, u32[]{:S(2)}, u32[]{:S(2)}) collective-permute-start(bf16[512,128]{1,0:T(8,128)(2,1)S(1)} %get-tuple-element.9), channel_id=1, source_target_pairs={{0,16},{8,24},{16,32},{24,40},{32,48},{40,56},{48,64},{56,72},{64,... | collective-permute-start | bytes 393224 | tf_op jit(solution)/shard_map/ppermute | solution.py:32
  89.2 1.9 %collective-permute-start.5 = (bf16[512,128]{1,0:T(8,128)(2,1)S(1)}, bf16[512,128]{1,0:T(8,128)(2,1)S(1)}, u32[]{:S(2)}, u32[]{:S(2)}) collective-permute-start(bf16[512,128]{1,0:T(8,128)(2,1)S(1)} %get-tuple-element.9), channel_id=1, source_target_pairs={{0,8},{8,16},{16,24},{24,32},{32,40},{40,48},{48,56},{56,64},{64,7... | collective-permute-start | bytes 393224 | tf_op jit(solution)/shard_map/ppermute | solution.py:32
  91.2 7.2 %collective-permute-start.6 = (bf16[512,128]{1,0:T(8,128)(2,1)S(1)}, bf16[512,128]{1,0:T(8,128)(2,1)S(1)}, u32[]{:S(2)}, u32[]{:S(2)}) collective-permute-start(bf16[512,128]{1,0:T(8,128)(2,1)S(1)} %get-tuple-element.9), channel_id=1, source_target_pairs={{0,1016},{8,0},{16,8},{24,16},{32,24},{40,32},{48,40},{56,48},{64,... | collective-permute-start | bytes 393224 | tf_op jit(solution)/shard_map/ppermute | solution.py:32
  98.5 3.8 %collective-permute-start.7 = (bf16[512,128]{1,0:T(8,128)(2,1)S(1)}, bf16[512,128]{1,0:T(8,128)(2,1)S(1)}, u32[]{:S(2)}, u32[]{:S(2)}) collective-permute-start(bf16[512,128]{1,0:T(8,128)(2,1)S(1)} %get-tuple-element.9), channel_id=1, source_target_pairs={{0,1008},{8,1016},{16,0},{24,8},{32,16},{40,24},{48,32},{56,40},{6... | collective-permute-start | bytes 393224 | tf_op jit(solution)/shard_map/ppermute | solution.py:32
  102.7 4.0 %collective-permute-done.7 = bf16[512,128]{1,0:T(8,128)(2,1)S(1)} collective-permute-done((bf16[512,128]{1,0:T(8,128)(2,1)S(1)}, bf16[512,128]{1,0:T(8,128)(2,1)S(1)}, u32[]{:S(2)}, u32[]{:S(2)}) %collective-permute-start.7) | collective-permute-done | bytes 131104 | tf_op jit(solution)/shard_map/ppermute | solution.py:32
  107.0 5.5 %fusion.40 = f32[2,512,2560]{2,1,0:T(8,128)} fusion(bf16[512,2,64]{0,2,1:T(8,128)(2,1)S(1)} %bitcast.56, bf16[2560,2,64]{0,2,1:T(8,128)(2,1)S(1)} %bitcast.47), kind=kOutput, calls=%fused_computation.63 | convolution fusion | flops 335544320 | bytes 11272192 | tf_op jit(solution)/shard_map/qhd,khd->hqk/dot_general | solution.py:55
  112.5 3.7 %fusion.39 = f32[2,512]{1,0:T(2,128)S(1)} fusion(pred[2560]{0:T(1024)(128)(4,1)S(1)} %gt.17, bf16[512,2,64]{0,2,1:T(8,128)(2,1)S(1)} %bitcast.57, bf16[2560,2,64]{0,2,1:T(8,128)(2,1)S(1)} %bitcast.48), kind=kOutput, calls=%fused_computation.62 | convolution fusion | flops 346032640 | bytes 793088 | tf_op jit(solution)/shard_map/sub | solution.py:112
  116.3 7.1 %fusion.16 = bf16[2,64,512]{2,1,0:T(8,128)(2,1)S(1)} fusion(bf16[2560,2,64]{0,2,1:T(8,128)(2,1)S(1)} %bitcast.53, f32[2,512]{1,0:T(2,128)S(1)} %fusion.39, f32[2,512,2560]{2,1,0:T(8,128)} %fusion.40, pred[2560]{0:T(1024)(128)(4,1)S(1)} %gt.17), kind=kOutput, calls=%fused_computation.28 | convolution fusion | flops 348720640 | bytes 11278848 | tf_op jit(solution)/shard_map/hqk,khd->qhd/dot_general | solution.py:62
  123.4 1.8 convolution_bitcast_fusion
  125.2 5.6 %all-to-all-start.2 = ((f32[8,512,128]{2,1,0:T(8,128)}), f32[8,512,128]{2,1,0:T(8,128)S(1)}, u32[]{:S(2)}, u32[]{:S(2)}) async-start(f32[8,512,128]{2,1,0:T(8,128)} %convolution_bitcast_fusion), calls=%async_computation.2 | async-start | bytes 4194304 | tf_op jit(solution)/shard_map/all_to_all | solution.py:43
  131.0 25.0 %all-to-all-done.2 = f32[8,512,128]{2,1,0:T(8,128)S(1)} async-done(((f32[8,512,128]{2,1,0:T(8,128)}), f32[8,512,128]{2,1,0:T(8,128)S(1)}, u32[]{:S(2)}, u32[]{:S(2)}) %all-to-all-start.2) | async-done | bytes 2097184 | tf_op jit(solution)/shard_map/all_to_all | solution.py:43
  156.1 0.8 fusion.37
  156.9 1.3 gather_fusion
  158.2 28.6 %all_to_all.20 = bf16[128,4,128]{2,1,0:T(4,128)(2,1)S(1)} all-to-all(bf16[128,4,128]{2,1,0:T(4,128)(2,1)S(1)} %bitcast.54), channel_id=1, replica_groups=mesh['region'=128,'mp'=8] {'region'}, dimensions={0} | all-to-all | bytes 262144 | tf_op jit(solution)/shard_map/all_to_all | solution.py:120
  186.8 2.1 %fusion.9 = bf16[2048,128]{1,0:T(8,128)(2,1)} fusion(bf16[512,128]{1,0:T(8,128)(2,1)S(1)} %bitcast.60, s32[2048]{0:T(1024)S(1)} %copy-done.2, bf16[2048,128]{1,0:T(8,128)(2,1)S(1)} %copy-done.1), kind=kOutput, calls=%fused_computation.16 | convolution fusion | flops 270270464 | bytes 1187840 | tf_op jit(solution)/shard_map/dot_general | solution.py:123
  (34 shorter events, 1.9 us)
Async XLA Ops:
  0.6 68.2 %copy-start = (bf16[3,1024,128]{2,1,0:T(8,128)(2,1)S(1)}, bf16[3,1024,128]{2,1,0:T(8,128)(2,1)}, u32[]{:S(2)}) copy-start(bf16[3,1024,128]{2,1,0:T(8,128)(2,1)} %param.14) | copy-start | bytes 2359300
  3.4 44.0 %all-to-all-start = ((bf16[128,4,128]{2,1,0:T(4,128)(2,1)}), bf16[128,4,128]{2,1,0:T(4,128)(2,1)S(1)}, u32[]{:S(2)}, u32[]{:S(2)}) async-start(bf16[128,4,128]{2,1,0:T(4,128)(2,1)} %bitcast), calls=%async_computation | async-start | bytes 262144 | tf_op jit(solution)/shard_map/all_to_all | solution.py:78
  48.9 18.7 %all-to-all-start.1 = ((bf16[8,512,128]{1,2,0:T(8,128)(2,1)}), bf16[8,512,128]{1,2,0:T(8,128)(2,1)S(1)}, u32[]{:S(2)}, u32[]{:S(2)}) async-start(bf16[8,512,128]{1,2,0:T(8,128)(2,1)} %broadcast_in_dim.16), calls=%async_computation.1 | async-start | bytes 2097152 | tf_op jit(solution)/shard_map/all_to_all | solution.py:15
  69.3 19.9 %collective-permute-start = (bf16[512,128]{1,0:T(8,128)(2,1)S(1)}, bf16[512,128]{1,0:T(8,128)(2,1)S(1)}, u32[]{:S(2)}, u32[]{:S(2)}) collective-permute-start(bf16[512,128]{1,0:T(8,128)(2,1)S(1)} %get-tuple-element.7), channel_id=1, source_target_pairs={{0,16},{8,24},{16,32},{24,40},{32,48},{40,56},{48,64},{56,72},{64,... | collective-permute-start | bytes 393224 | tf_op jit(solution)/shard_map/ppermute | solution.py:32
  72.5 18.7 %collective-permute-start.1 = (bf16[512,128]{1,0:T(8,128)(2,1)S(1)}, bf16[512,128]{1,0:T(8,128)(2,1)S(1)}, u32[]{:S(2)}, u32[]{:S(2)}) collective-permute-start(bf16[512,128]{1,0:T(8,128)(2,1)S(1)} %get-tuple-element.7), channel_id=1, source_target_pairs={{0,8},{8,16},{16,24},{24,32},{32,40},{40,48},{48,56},{56,64},{64,7... | collective-permute-start | bytes 393224 | tf_op jit(solution)/shard_map/ppermute | solution.py:32
  75.2 23.3 %collective-permute-start.2 = (bf16[512,128]{1,0:T(8,128)(2,1)S(1)}, bf16[512,128]{1,0:T(8,128)(2,1)S(1)}, u32[]{:S(2)}, u32[]{:S(2)}) collective-permute-start(bf16[512,128]{1,0:T(8,128)(2,1)S(1)} %get-tuple-element.7), channel_id=1, source_target_pairs={{0,1016},{8,0},{16,8},{24,16},{32,24},{40,32},{48,40},{56,48},{64,... | collective-permute-start | bytes 393224 | tf_op jit(solution)/shard_map/ppermute | solution.py:32
  81.6 20.7 %collective-permute-start.3 = (bf16[512,128]{1,0:T(8,128)(2,1)S(1)}, bf16[512,128]{1,0:T(8,128)(2,1)S(1)}, u32[]{:S(2)}, u32[]{:S(2)}) collective-permute-start(bf16[512,128]{1,0:T(8,128)(2,1)S(1)} %get-tuple-element.7), channel_id=1, source_target_pairs={{0,1008},{8,1016},{16,0},{24,8},{32,16},{40,24},{48,32},{56,40},{6... | collective-permute-start | bytes 393224 | tf_op jit(solution)/shard_map/ppermute | solution.py:32
  86.1 16.3 %collective-permute-start.4 = (bf16[512,128]{1,0:T(8,128)(2,1)S(1)}, bf16[512,128]{1,0:T(8,128)(2,1)S(1)}, u32[]{:S(2)}, u32[]{:S(2)}) collective-permute-start(bf16[512,128]{1,0:T(8,128)(2,1)S(1)} %get-tuple-element.9), channel_id=1, source_target_pairs={{0,16},{8,24},{16,32},{24,40},{32,48},{40,56},{48,64},{56,72},{64,... | collective-permute-start | bytes 393224 | tf_op jit(solution)/shard_map/ppermute | solution.py:32
  89.2 13.2 %collective-permute-start.5 = (bf16[512,128]{1,0:T(8,128)(2,1)S(1)}, bf16[512,128]{1,0:T(8,128)(2,1)S(1)}, u32[]{:S(2)}, u32[]{:S(2)}) collective-permute-start(bf16[512,128]{1,0:T(8,128)(2,1)S(1)} %get-tuple-element.9), channel_id=1, source_target_pairs={{0,8},{8,16},{16,24},{24,32},{32,40},{40,48},{48,56},{56,64},{64,7... | collective-permute-start | bytes 393224 | tf_op jit(solution)/shard_map/ppermute | solution.py:32
  91.2 11.5 %collective-permute-start.6 = (bf16[512,128]{1,0:T(8,128)(2,1)S(1)}, bf16[512,128]{1,0:T(8,128)(2,1)S(1)}, u32[]{:S(2)}, u32[]{:S(2)}) collective-permute-start(bf16[512,128]{1,0:T(8,128)(2,1)S(1)} %get-tuple-element.9), channel_id=1, source_target_pairs={{0,1016},{8,0},{16,8},{24,16},{32,24},{40,32},{48,40},{56,48},{64,... | collective-permute-start | bytes 393224 | tf_op jit(solution)/shard_map/ppermute | solution.py:32
  98.5 8.2 %collective-permute-start.7 = (bf16[512,128]{1,0:T(8,128)(2,1)S(1)}, bf16[512,128]{1,0:T(8,128)(2,1)S(1)}, u32[]{:S(2)}, u32[]{:S(2)}) collective-permute-start(bf16[512,128]{1,0:T(8,128)(2,1)S(1)} %get-tuple-element.9), channel_id=1, source_target_pairs={{0,1008},{8,1016},{16,0},{24,8},{32,16},{40,24},{48,32},{56,40},{6... | collective-permute-start | bytes 393224 | tf_op jit(solution)/shard_map/ppermute | solution.py:32
  123.4 63.4 %copy-start.1 = (bf16[2048,128]{1,0:T(8,128)(2,1)S(1)}, bf16[2048,128]{1,0:T(8,128)(2,1)}, u32[]{:S(2)}) copy-start(bf16[2048,128]{1,0:T(8,128)(2,1)} %param.8) | copy-start | bytes 1572868
  123.4 63.4 %copy-start.2 = (s32[2048]{0:T(1024)S(1)}, s32[2048]{0:T(1024)}, u32[]{:S(2)}) copy-start(s32[2048]{0:T(1024)} %param.10) | copy-start | bytes 24580
  125.2 30.7 %all-to-all-start.2 = ((f32[8,512,128]{2,1,0:T(8,128)}), f32[8,512,128]{2,1,0:T(8,128)S(1)}, u32[]{:S(2)}, u32[]{:S(2)}) async-start(f32[8,512,128]{2,1,0:T(8,128)} %convolution_bitcast_fusion), calls=%async_computation.2 | async-start | bytes 4194304 | tf_op jit(solution)/shard_map/all_to_all | solution.py:43
where the time goes:
time: 190 us; the launch traced here: 189 us
  starting transfers between devices  68.6 us (36%)
  waiting for transfers between devices  57.7 us (30%)
  blocking collectives  28.6 us (15%)
  matrix products  24.6 us (13%)
  local copies, waits for them, and re-layouts  5.41 us (3%)
  other arithmetic  2.92 us (2%)
    ppermute x8, starting transfers between devices, from_behind(): return lax.ppermute(value, axis, pairs)  32 us
    all_to_all x1, blocking collectives, on_device(): lax.all_to_all(requested, 'region', split_axis=0, concat_axis=0, tiled=True)  28.6 us
    all_to_all x1, starting transfers between devices, on_device(): lax.all_to_all(partial_value.reshape(regions, cap, local_width), 'region'...  26.3 us
    all_to_all x1, waiting for transfers between devices, sum_at_owner(): lax.all_to_all(parts, axis, split_axis=0, concat_axis=0, tiled=True)  25 us
    all_to_all x1, waiting for transfers between devices, on_device(): lax.all_to_all(partial_value.reshape(regions, cap, local_width), 'region'...  16.9 us
    all_to_all x1, waiting for transfers between devices, from_everyone(): return lax.all_to_all(copies, axis, split_axis=0, concat_axis=0, tiled=True)  11.9 us
    dot_general x1, matrix products, block_values(): jnp.einsum('hqk,khd->qhd', weights, val_heads, preferred_element_type=jnp...  7.13 us
    all_to_all x1, starting transfers between devices, sum_at_owner(): lax.all_to_all(parts, axis, split_axis=0, concat_axis=0, tiled=True)  5.61 us
  transfers between devices with their start and end apart: 11, of which 4 were waited for; matrix products, arithmetic and copies ran while one was open for 2% of the time, Pallas kernels for 0%

commit v1 on v0

v1 whole, which is shorter than its diff:
```python
import jax
import jax.numpy as jnp
from jax import lax
from jax.experimental import pallas as pl
from jax.experimental.pallas import tpu as pltpu
from jax.sharding import Mesh
from jax.sharding import PartitionSpec as P

HEAD_DIM = 64
BF16 = jnp.bfloat16
F32 = jnp.float32
VMEM = pl.BlockSpec(memory_space=pltpu.VMEM)
SMEM = pl.BlockSpec(memory_space=pltpu.SMEM)
PARAMS = pltpu.CompilerParams(vmem_limit_bytes=32 * 1024 * 1024)


def exchange(array, axis):
    return lax.all_to_all(array, axis, split_axis=0, concat_axis=0, tiled=True)


def shifted(value, axis, steps):
    count = lax.axis_size(axis)
    pairs = [(source, (source + steps) % count) for source in range(count)]
    return lax.ppermute(value, axis, pairs)


def qkv_kernel(core_ref, own_ref, other_ref, gain_ref, w_ref, q_ref, kv_ref, normed_ref):
    core = core_ref[0]
    blocks, rows, width = own_ref.shape
    chunk = 128

    def normalise(step, _):
        at = pl.ds(pl.multiple_of(step * chunk, chunk), chunk)
        total = jnp.zeros((chunk, width), F32)
        for ref in (own_ref, other_ref):
            for block in range(blocks):
                value = ref[block, at, :].astype(F32)
                total = total + value * value
        mean = jnp.sum(total, axis=-1, keepdims=True) / (2 * blocks * width)
        factor = lax.rsqrt(mean + 1e-05)
        for ref, part in ((own_ref, core), (other_ref, 1 - core)):
            for block in range(blocks):
                index = 2 * block + part
                gain = gain_ref[pl.ds(index, 1), :]
                value = (ref[block, at, :].astype(F32) * factor * gain).astype(BF16)
                normed_ref[at, pl.ds(pl.multiple_of(index * width, width), width)] = value
        normed = normed_ref[at, :]
        queries = jnp.dot(normed, w_ref[0], preferred_element_type=F32).astype(BF16)
        q_ref[at, :] = queries
        kv_ref[at, :] = jnp.dot(normed, w_ref[1], preferred_element_type=F32).astype(BF16)
        later = pl.ds(pl.multiple_of(rows + step * chunk, chunk), chunk)
        kv_ref[later, :] = jnp.dot(normed, w_ref[2], preferred_element_type=F32).astype(BF16)
        return 0

    lax.fori_loop(0, rows // chunk, normalise, 0)


def attend_block(q_ref, kv_ref, top_ref, total_ref, mixed_ref, first):
    rows, width = q_ref.shape
    chunk = 256
    lane = lax.broadcasted_iota(jnp.int32, (1, width), 1)
    heads = width // HEAD_DIM
    keys = kv_ref[pl.ds(0, rows), :]
    values = kv_ref[pl.ds(rows, rows), :]
    for start in range(0, rows, chunk):
        at = pl.ds(start, chunk)
        queries = q_ref[at, :] * HEAD_DIM ** (-0.5)
        if first:
            tops, totals, mixed = None, None, None
        else:
            tops, totals, mixed = top_ref[at, :], total_ref[at, :], mixed_ref[at, :]
        new_tops = jnp.zeros((chunk, width), F32)
        expds = []
        for head in range(heads):
            mine = lane // HEAD_DIM == head
            scores = lax.dot_general(
                jnp.where(mine, queries, 0).astype(BF16),
                keys,
                (((1,), (1,)), ((), ())),
                preferred_element_type=F32,
            )
            top = jnp.max(scores, axis=-1, keepdims=True)
            if not first:
                top = jnp.maximum(top, tops[:, head * HEAD_DIM : head * HEAD_DIM + 1])
            expds.append(jnp.exp(scores - top).astype(BF16))
            new_tops = jnp.where(mine, top, new_tops)
        gained = jnp.zeros((chunk, 2 * width), F32)
        for head in range(heads):
            mine = lane // HEAD_DIM == head
            masked = jnp.where(mine, values, 0).astype(BF16)
            ones = jnp.broadcast_to(jnp.where(mine, 1.0, 0.0), values.shape).astype(BF16)
            gained = gained + jnp.dot(
                expds[head], jnp.concatenate([masked, ones], axis=1), preferred_element_type=F32
            )
        if first:
            mixed_ref[at, :] = gained[:, :width]
            total_ref[at, :] = gained[:, width:]
        else:
            shrink = jnp.exp(tops - new_tops)
            mixed_ref[at, :] = mixed * shrink + gained[:, :width]
            total_ref[at, :] = totals * shrink + gained[:, width:]
        top_ref[at, :] = new_tops


def own_kernel(q_ref, kv_ref, top_ref, total_ref, mixed_ref):
    attend_block(q_ref, kv_ref, top_ref, total_ref, mixed_ref, True)


def seen_blocks(mask_ref, picks, q_ref, kv_refs, top_ref, total_ref, mixed_ref):
    for pick, kv_ref in zip(picks, kv_refs):

        @pl.when(mask_ref[pick] > 0)
        def _(kv_ref=kv_ref):
            attend_block(q_ref, kv_ref, top_ref, total_ref, mixed_ref, False)


def near_kernel(
    mask_ref, q_ref, behind_ref, ahead_ref, top0_ref, total0_ref, mixed0_ref, top_ref, total_ref, mixed_ref
):
    top_ref[...] = top0_ref[...]
    total_ref[...] = total0_ref[...]
    mixed_ref[...] = mixed0_ref[...]
    seen_blocks(mask_ref, (1, 2), q_ref, (behind_ref, ahead_ref), top_ref, total_ref, mixed_ref)


def far_kernel(
    mask_ref,
    core_ref,
    q_ref,
    behind_ref,
    ahead_ref,
    top0_ref,
    total0_ref,
    mixed0_ref,
    w_ref,
    att_ref,
    out_ref,
    top_ref,
    total_ref,
    mixed_ref,
):
    top_ref[...] = top0_ref[...]
    total_ref[...] = total0_ref[...]
    mixed_ref[...] = mixed0_ref[...]
    seen_blocks(mask_ref, (0, 3), q_ref, (behind_ref, ahead_ref), top_ref, total_ref, mixed_ref)
    attended = (mixed_ref[...] / total_ref[...]).astype(BF16)
    att_ref[...] = attended
    blocks, _, width = out_ref.shape
    part = 1 - core_ref[0]
    for block in range(blocks):
        at = pl.ds(pl.multiple_of((2 * block + part) * width, width), width)
        out_ref[block] = jnp.dot(attended, w_ref[:, at], preferred_element_type=F32).astype(BF16)


def share_kernel(core_ref, att_ref, w_ref, arrived_ref, out_ref):
    blocks, _, width = out_ref.shape
    core = core_ref[0]
    for block in range(blocks):
        at = pl.ds(pl.multiple_of((2 * block + core) * width, width), width)
        share = jnp.dot(att_ref[...], w_ref[:, at], preferred_element_type=F32)
        out_ref[block] = (share + arrived_ref[block].astype(F32)).astype(BF16)


def call(kernel, outs, ins, name, scratch=(), flops=0, bytes_accessed=0, transcendentals=0):
    return pl.pallas_call(
        kernel,
        out_shape=outs,
        in_specs=ins,
        out_specs=jax.tree.map(lambda _: VMEM, outs),
        scratch_shapes=list(scratch),
        compiler_params=PARAMS,
        name=name,
        cost_estimate=pl.CostEstimate(
            flops=flops, bytes_accessed=bytes_accessed, transcendentals=transcendentals
        ),
    )


def on_device(grid, g2m_weight, g2m_slot, slot_node, peer_mask, norm_gain, w_qkv, w_out):
    regions = lax.axis_size("region")
    chips = lax.axis_size("x")
    cap = slot_node.shape[2]
    slots = regions * cap
    rows = slots
    width = grid.shape[1]
    core = lax.axis_index("core").astype(jnp.int32).reshape(1)
    sds = jax.ShapeDtypeStruct

    scaled = (g2m_weight[:, None] * grid.astype(F32)).astype(BF16)
    slot_hot = (g2m_slot[None, :] == jnp.arange(slots, dtype=jnp.int32)[:, None]).astype(BF16)
    partial_value = jnp.dot(slot_hot, scaled, preferred_element_type=F32).astype(BF16)
    mesh_low = exchange(partial_value.reshape(regions, cap, width), "region").reshape(rows, width)

    own = exchange(jnp.broadcast_to(mesh_low, (chips, rows, width)), "x")
    other = shifted(own, "core", 1)
    queries, kv = call(
        qkv_kernel,
        (sds((rows, width), BF16), sds((2 * rows, width), BF16)),
        [SMEM, VMEM, VMEM, VMEM, VMEM],
        "qkv",
        scratch=[pltpu.VMEM((rows, 2 * chips * width), BF16)],
        flops=2 * rows * 1024 * 384,
        bytes_accessed=3 << 20,
    )(core, own, other, norm_gain.reshape(2 * chips, width), w_qkv)

    state = sds((rows, width), F32)
    states = (state, state, state)
    mask = peer_mask.reshape(-1)
    block_cost = dict(flops=8 * rows * rows * width, transcendentals=2 * rows * rows)
    behind = shifted(kv, "region", 1)
    ahead = shifted(kv, "region", -1)
    top, total, mixed = call(own_kernel, states, [VMEM] * 2, "own", **block_cost)(queries, kv)
    behind2 = shifted(behind, "region", 1)
    ahead2 = shifted(ahead, "region", -1)
    twice = {key: 2 * value for key, value in block_cost.items()}
    top, total, mixed = call(near_kernel, states, [SMEM] + [VMEM] * 6, "near", **twice)(
        mask, queries, behind, ahead, top, total, mixed
    )
    shares = sds((chips, rows, width), BF16)
    attended, leaving = call(
        far_kernel,
        (sds((rows, width), BF16), shares),
        [SMEM, SMEM] + [VMEM] * 7,
        "far",
        scratch=[pltpu.VMEM((rows, width), F32)] * 3,
        **twice,
    )(mask, core, queries, behind2, ahead2, top, total, mixed, w_out)
    arrived = shifted(leaving, "core", 1)
    summed = call(share_kernel, shares, [SMEM] + [VMEM] * 3, "share")(core, attended, w_out, arrived)
    mesh_slots = mesh_low.astype(F32) + exchange(summed, "x").astype(F32).sum(axis=0)

    mesh_back = mesh_slots.astype(BF16)
    returned = exchange(mesh_back.reshape(regions, cap, width), "region").reshape(slots, width)
    flat_nodes = slot_node[0].reshape(-1)
    node_hot = (jnp.arange(rows, dtype=jnp.int32)[:, None] == flat_nodes[None, :]).astype(F32)
    mesh_state = jnp.dot(
        node_hot, mesh_slots, precision=lax.Precision.HIGHEST, preferred_element_type=F32
    )
    gathered = jnp.dot(slot_hot.T, returned, preferred_element_type=F32)
    grid_out = (grid.astype(F32) + gathered).astype(BF16)
    return (mesh_state, grid_out)


def solution(mesh):
    regions, model = mesh.devices.shape
    split = Mesh(mesh.devices.reshape(regions, model // 2, 2), ("region", "x", "core"))
    model = ("x", "core")
    return jax.shard_map(
        on_device,
        mesh=split,
        in_specs=(
            P("region", model),
            P("region"),
            P("region"),
            P("region", None, None),
            P("region", None),
            P(),
            P(None, None, model),
            P(model, None),
        ),
        out_specs=(P("region", model), P("region", model)),
        check_vma=False,
    )
```

time: 190 us -> 143 us (0.75)
  blocking collectives: 28.6 us -> 67 us
  starting transfers between devices: 68.6 us -> 32.3 us
  waiting for transfers between devices: 57.7 us -> 25.2 us
  matrix products: 24.6 us -> 5.41 us
  Pallas kernels: 0 us -> 9.64 us
  local copies, waits for them, and re-layouts: 5.41 us -> 0.32 us
  other arithmetic: 2.92 us -> 0.79 us
    all_to_all x1 -> x3, blocking collectives: 28.6 us -> 67 us  [exchange(): return lax.all_to_all(array, axis, split_axis=0, concat_axis=0, tiled=True)]
    all_to_all x3 -> x1, waiting for transfers between devices: 53.8 us -> 15.7 us  [exchange(): return lax.all_to_all(array, axis, split_axis=0, concat_axis=0, tiled=True)]
    all_to_all x3 -> x1, starting transfers between devices: 36.6 us -> 10.2 us  [exchange(): return lax.all_to_all(array, axis, split_axis=0, concat_axis=0, tiled=True)]
    dot_general x9 -> x3, matrix products: 20.9 us -> 5.41 us  [the longest x1 2.09 us: on_device(): gathered = jnp.dot(slot_hot.T, returned, preferred_element_type=F32)]
    ppermute x8 -> x6, starting transfers between devices: 32 us -> 22.1 us  [shifted(): return lax.ppermute(value, axis, pairs)]
    pallas_call x0 -> x5, Pallas kernels: none -> 9.64 us  [the longest x1 3.93 us: on_device(): call(far_kernel, (sds((rows, width), BF16), shares), [SMEM, SMEM] + [VMEM...]
    ppermute x8 -> x6, waiting for transfers between devices: 3.98 us -> 9.52 us  [shifted(): return lax.ppermute(value, axis, pairs)]
    sub x1 -> x0, matrix products: 3.74 us -> none  [on_device(): expd = jnp.exp(scores - top)]
  transfers between devices with their start and end apart: 11 -> 7, of which waited for: 4 -> 6; matrix products, arithmetic and copies ran while one was open for 2% -> 1% of each run, Pallas kernels for 0% -> 2%
where the time goes in v1:
time: 143 us; the launch traced here: 141 us
  blocking collectives  67 us (47%)
  starting transfers between devices  32.3 us (23%)
  waiting for transfers between devices  25.2 us (18%)
  Pallas kernels  9.64 us (7%)
  matrix products  5.41 us (4%)
    all_to_all x3, blocking collectives, exchange(): return lax.all_to_all(array, axis, split_axis=0, concat_axis=0, tiled=True)  67 us
    ppermute x6, starting transfers between devices, shifted(): return lax.ppermute(value, axis, pairs)  22.1 us
    all_to_all x1, waiting for transfers between devices, exchange(): return lax.all_to_all(array, axis, split_axis=0, concat_axis=0, tiled=True)  15.7 us
    all_to_all x1, starting transfers between devices, exchange(): return lax.all_to_all(array, axis, split_axis=0, concat_axis=0, tiled=True)  10.2 us
    ppermute x6, waiting for transfers between devices, shifted(): return lax.ppermute(value, axis, pairs)  9.52 us
    pallas_call x1, Pallas kernels, on_device(): call(far_kernel, (sds((rows, width), BF16), shares), [SMEM, SMEM] + [VMEM...  3.93 us
  transfers between devices with their start and end apart: 7, of which 6 were waited for; matrix products, arithmetic and copies ran while one was open for 1% of the time, Pallas kernels for 2%

profile of v1, /device:TPU:6, one launch (start us, length us, event | category | flops | bytes accessed | tf_op | source)
XLA Modules:
  0.0 141.5 jit_solution(933774461745891454)
XLA Ops:
  0.6 2.0 %fusion.6 = bf16[512,128]{1,0:T(8,128)(2,1)S(1)} fusion(s32[2048]{0:T(1024)} %param.10, bf16[2048,128]{1,0:T(8,128)(2,1)} %param.8, f32[2048]{0:T(1024)} %param.9), kind=kOutput, calls=%fused_computation.8 | convolution fusion | flops 270336000 | bytes 671744 | tf_op jit(solution)/shard_map/dot_general | solution.py:191
  2.6 43.8 %all_to_all.20 = bf16[128,4,128]{2,1,0:T(4,128)(2,1)S(1)} all-to-all(bf16[128,4,128]{2,1,0:T(4,128)(2,1)S(1)} %bitcast.15), channel_id=1, replica_groups=mesh['region'=128,'x'=4,'core'=2] {'region'}, dimensions={0} | all-to-all | bytes 262144 | tf_op jit(solution)/shard_map/all_to_all | solution.py:18
  46.4 0.1 broadcast_in_dim.2
  46.5 10.7 %all_to_all.21.own_ref = bf16[4,512,128]{2,1,0:T(8,128)(2,1)S(1)} all-to-all(bf16[4,512,128]{2,1,0:T(8,128)(2,1)S(1)} %broadcast_in_dim.2), channel_id=1, replica_groups=mesh['region'=128,'x'=4,'core'=2] {'x'}, dimensions={0} | all-to-all | bytes 1048576 | tf_op jit(solution)/shard_map/all_to_all | solution.py:18
  57.2 1.9 %collective-permute-start = (bf16[4,512,128]{2,1,0:T(8,128)(2,1)S(1)}, bf16[4,512,128]{2,1,0:T(8,128)(2,1)S(1)}, u32[]{:S(2)}, u32[]{:S(2)}) collective-permute-start(bf16[4,512,128]{2,1,0:T(8,128)(2,1)S(1)} %all_to_all.21.own_ref), channel_id=1, source_target_pairs={{0,1},{1,0},{2,3},{3,2},{4,5},{5,4},{6,7},{7,6},{8,9},{9,8},{10,11... | collective-permute-start | bytes 1572872 | tf_op jit(solution)/shard_map/ppermute | solution.py:24
  59.1 1.9 %collective-permute-done.other_ref = bf16[4,512,128]{2,1,0:T(8,128)(2,1)S(1)} collective-permute-done((bf16[4,512,128]{2,1,0:T(8,128)(2,1)S(1)}, bf16[4,512,128]{2,1,0:T(8,128)(2,1)S(1)}, u32[]{:S(2)}, u32[]{:S(2)}) %collective-permute-start) | collective-permute-done | bytes 524320 | tf_op jit(solution)/shard_map/ppermute | solution.py:24
  61.0 2.1 %qkv.1 = (bf16[512,128]{1,0:T(8,128)(2,1)S(1)}, bf16[1024,128]{1,0:T(8,128)(2,1)S(1)}) custom-call(s32[1]{0:T(128)} %bitcast.2.core_ref, bf16[4,512,128]{2,1,0:T(8,128)(2,1)S(1)} %all_to_all.21.own_ref, bf16[4,512,128]{2,1,0:T(8,128)(2,1)S(1)} %collective-permute-done.other_ref, f32[8,128]{1,0:T(8,128)S(1)} %bitcast.8, bf16[3,1024,128]{2,1,0:T(8,128)(2,1)S(1)} %copy-done), custom_call_target="tpu_custom_call" | custom-call | flops 402653184 | bytes 3145728 | tf_op jit(solution)/shard_map/qkv/pallas_call | solution.py:196
  63.1 0.0 copy-start.3
  63.1 2.9 %collective-permute-start.1 = (bf16[1024,128]{1,0:T(8,128)(2,1)S(1)}, bf16[1024,128]{1,0:T(8,128)(2,1)S(1)}, u32[]{:S(2)}, u32[]{:S(2)}) collective-permute-start(bf16[1024,128]{1,0:T(8,128)(2,1)S(1)} %get-tuple-element.13.kv_ref), channel_id=1, source_target_pairs={{0,8},{8,16},{16,24},{24,32},{32,40},{40,48},{48,56},{56,64},{64,7... | collective-permute-start | bytes 786440 | tf_op jit(solution)/shard_map/ppermute | solution.py:24
  66.0 6.3 %collective-permute-start.3 = (bf16[1024,128]{1,0:T(8,128)(2,1)S(1)}, bf16[1024,128]{1,0:T(8,128)(2,1)S(1)}, u32[]{:S(2)}, u32[]{:S(2)}) collective-permute-start(bf16[1024,128]{1,0:T(8,128)(2,1)S(1)} %get-tuple-element.13.kv_ref), channel_id=1, source_target_pairs={{0,1016},{8,0},{16,8},{24,16},{32,24},{40,32},{48,40},{56,48},{64,... | collective-permute-start | bytes 786440 | tf_op jit(solution)/shard_map/ppermute | solution.py:24
  72.3 4.4 %collective-permute-done.1.behind_ref = bf16[1024,128]{1,0:T(8,128)(2,1)S(1)} collective-permute-done((bf16[1024,128]{1,0:T(8,128)(2,1)S(1)}, bf16[1024,128]{1,0:T(8,128)(2,1)S(1)}, u32[]{:S(2)}, u32[]{:S(2)}) %collective-permute-start.1) | collective-permute-done | bytes 262176 | tf_op jit(solution)/shard_map/ppermute | solution.py:24
  76.7 1.9 %collective-permute-start.2 = (bf16[1024,128]{1,0:T(8,128)(2,1)S(1)}, bf16[1024,128]{1,0:T(8,128)(2,1)S(1)}, u32[]{:S(2)}, u32[]{:S(2)}) collective-permute-start(bf16[1024,128]{1,0:T(8,128)(2,1)S(1)} %collective-permute-done.1.behind_ref), channel_id=1, source_target_pairs={{0,8},{8,16},{16,24},{24,32},{32,40},{40,48},{48,56},{56,64},{64,7... | collective-permute-start | bytes 786440 | tf_op jit(solution)/shard_map/ppermute | solution.py:24
  78.6 7.2 %collective-permute-start.4 = (bf16[1024,128]{1,0:T(8,128)(2,1)S(1)}, bf16[1024,128]{1,0:T(8,128)(2,1)S(1)}, u32[]{:S(2)}, u32[]{:S(2)}) collective-permute-start(bf16[1024,128]{1,0:T(8,128)(2,1)S(1)} %collective-permute-done.3.ahead_ref), channel_id=1, source_target_pairs={{0,1016},{8,0},{16,8},{24,16},{32,24},{40,32},{48,40},{56,48},{64,... | collective-permute-start | bytes 786440 | tf_op jit(solution)/shard_map/ppermute | solution.py:24
  85.9 1.2 own.1
  87.1 0.0 copy-start.1
  87.1 2.1 %near.1 = (f32[512,128]{1,0:T(8,128)S(1)}, f32[512,128]{1,0:T(8,128)S(1)}, f32[512,128]{1,0:T(8,128)S(1)}) custom-call(s32[4]{0:T(128)S(1)} %bitcast.9, bf16[512,128]{1,0:T(8,128)(2,1)S(1)} %get-tuple-element.12.q_ref, bf16[1024,128]{1,0:T(8,128)(2,1)S(1)} %collective-permute-done.1.behind_ref, bf16[1024,128]{1,0:T(8,128)(2,1)S(1)} %collective-permute-done.3.ahead_ref, ...), custom_call_target="tpu_custom_call" | custom-call | flops 536870912 | tf_op jit(solution)/shard_map/near/pallas_call | solution.py:216
  89.2 0.2 collective-permute-done.2.behind_ref
  89.4 1.2 collective-permute-done.4.ahead_ref
  90.6 3.9 %far.1 = (bf16[512,128]{1,0:T(8,128)(2,1)S(1)}, bf16[4,512,128]{2,1,0:T(8,128)(2,1)S(1)}) custom-call(s32[4]{0:T(128)S(1)} %bitcast.10, s32[1]{0:T(128)} %bitcast.2.core_ref, bf16[512,128]{1,0:T(8,128)(2,1)S(1)} %get-tuple-element.12.q_ref, bf16[1024,128]{1,0:T(8,128)(2,1)S(1)} %collective-permute-done.2.behind_ref, ...), custom_call_target="tpu_custom_call" | custom-call | flops 536870912 | tf_op jit(solution)/shard_map/far/pallas_call | solution.py:220
  94.6 1.9 %collective-permute-start.5 = (bf16[4,512,128]{2,1,0:T(8,128)(2,1)S(1)}, bf16[4,512,128]{2,1,0:T(8,128)(2,1)S(1)}, u32[]{:S(2)}, u32[]{:S(2)}) collective-permute-start(bf16[4,512,128]{2,1,0:T(8,128)(2,1)S(1)} %get-tuple-element.21), channel_id=1, source_target_pairs={{0,1},{1,0},{2,3},{3,2},{4,5},{5,4},{6,7},{7,6},{8,9},{9,8},{10,11... | collective-permute-start | bytes 1572872 | tf_op jit(solution)/shard_map/ppermute | solution.py:24
  96.5 1.9 %collective-permute-done.5.arrived_ref = bf16[4,512,128]{2,1,0:T(8,128)(2,1)S(1)} collective-permute-done((bf16[4,512,128]{2,1,0:T(8,128)(2,1)S(1)}, bf16[4,512,128]{2,1,0:T(8,128)(2,1)S(1)}, u32[]{:S(2)}, u32[]{:S(2)}) %collective-permute-start.5) | collective-permute-done | bytes 524320 | tf_op jit(solution)/shard_map/ppermute | solution.py:24
  98.4 0.3 share.1
  98.7 12.5 %all_to_all.22 = bf16[4,512,128]{2,1,0:T(8,128)(2,1)S(1)} all-to-all(bf16[4,512,128]{2,1,0:T(8,128)(2,1)S(1)} %share.1), channel_id=1, replica_groups=mesh['region'=128,'x'=4,'core'=2] {'x'}, dimensions={0} | all-to-all | bytes 1048576 | tf_op jit(solution)/shard_map/all_to_all | solution.py:18
  111.1 0.1 convert_reduce_fusion
  111.2 0.0 copy-start.6
  111.2 0.7 add_convert_fusion
  111.9 10.2 %all-to-all-start.3 = ((bf16[128,4,128]{2,1,0:T(4,128)(2,1)}), bf16[128,4,128]{2,1,0:T(4,128)(2,1)S(1)}, u32[]{:S(2)}, u32[]{:S(2)}) async-start(bf16[128,4,128]{2,1,0:T(4,128)(2,1)} %add_convert_fusion), calls=%async_computation.3 | async-start | bytes 262144 | tf_op jit(solution)/shard_map/all_to_all | solution.py:18
  122.1 0.1 copy.10
  122.2 0.1 eq.29
  122.3 1.3 fusion.8
  123.7 15.7 %all-to-all-done.3 = bf16[128,4,128]{2,1,0:T(4,128)(2,1)S(1)} async-done(((bf16[128,4,128]{2,1,0:T(4,128)(2,1)}), bf16[128,4,128]{2,1,0:T(4,128)(2,1)S(1)}, u32[]{:S(2)}, u32[]{:S(2)}) %all-to-all-start.3) | async-done | bytes 131104 | tf_op jit(solution)/shard_map/all_to_all | solution.py:18
  139.4 2.1 %fusion.3 = bf16[2048,128]{1,0:T(8,128)(2,1)} fusion(bf16[512,128]{1,0:T(8,128)(2,1)S(1)} %bitcast.14, s32[2048]{0:T(1024)S(1)} %copy-done.6, bf16[2048,128]{1,0:T(8,128)(2,1)S(1)} %copy-done.5), kind=kOutput, calls=%fused_computation.4 | convolution fusion | flops 270270464 | bytes 1187840 | tf_op jit(solution)/shard_map/dot_general | solution.py:239
  (12 shorter events, 0.0 us)
Async XLA Ops:
  46.4 14.6 %copy-start = (bf16[3,1024,128]{2,1,0:T(8,128)(2,1)S(1)}, bf16[3,1024,128]{2,1,0:T(8,128)(2,1)}, u32[]{:S(2)}) copy-start(bf16[3,1024,128]{2,1,0:T(8,128)(2,1)} %w_ref.3) | copy-start | bytes 2359300
  46.4 14.6 %copy-start.2 = (f32[1024]{0:T(1024)S(1)}, f32[1024]{0:T(1024)}, u32[]{:S(2)}) copy-start(f32[1024]{0:T(1024)} %param.13) | copy-start | bytes 12292
  57.2 3.8 %collective-permute-start = (bf16[4,512,128]{2,1,0:T(8,128)(2,1)S(1)}, bf16[4,512,128]{2,1,0:T(8,128)(2,1)S(1)}, u32[]{:S(2)}, u32[]{:S(2)}) collective-permute-start(bf16[4,512,128]{2,1,0:T(8,128)(2,1)S(1)} %all_to_all.21.own_ref), channel_id=1, source_target_pairs={{0,1},{1,0},{2,3},{3,2},{4,5},{5,4},{6,7},{7,6},{8,9},{9,8},{10,11... | collective-permute-start | bytes 1572872 | tf_op jit(solution)/shard_map/ppermute | solution.py:24
  63.1 23.9 %copy-start.3 = (s32[1,4]{1,0:T(1,128)S(1)}, s32[1,4]{1,0:T(1,128)}, u32[]{:S(2)}) copy-start(s32[1,4]{1,0:T(1,128)} %param.12) | copy-start | bytes 52
  63.1 13.6 %collective-permute-start.1 = (bf16[1024,128]{1,0:T(8,128)(2,1)S(1)}, bf16[1024,128]{1,0:T(8,128)(2,1)S(1)}, u32[]{:S(2)}, u32[]{:S(2)}) collective-permute-start(bf16[1024,128]{1,0:T(8,128)(2,1)S(1)} %get-tuple-element.13.kv_ref), channel_id=1, source_target_pairs={{0,8},{8,16},{16,24},{24,32},{32,40},{40,48},{48,56},{56,64},{64,7... | collective-permute-start | bytes 786440 | tf_op jit(solution)/shard_map/ppermute | solution.py:24
  66.0 12.6 %collective-permute-start.3 = (bf16[1024,128]{1,0:T(8,128)(2,1)S(1)}, bf16[1024,128]{1,0:T(8,128)(2,1)S(1)}, u32[]{:S(2)}, u32[]{:S(2)}) collective-permute-start(bf16[1024,128]{1,0:T(8,128)(2,1)S(1)} %get-tuple-element.13.kv_ref), channel_id=1, source_target_pairs={{0,1016},{8,0},{16,8},{24,16},{32,24},{40,32},{48,40},{56,48},{64,... | collective-permute-start | bytes 786440 | tf_op jit(solution)/shard_map/ppermute | solution.py:24
  76.7 12.7 %collective-permute-start.2 = (bf16[1024,128]{1,0:T(8,128)(2,1)S(1)}, bf16[1024,128]{1,0:T(8,128)(2,1)S(1)}, u32[]{:S(2)}, u32[]{:S(2)}) collective-permute-start(bf16[1024,128]{1,0:T(8,128)(2,1)S(1)} %collective-permute-done.1.behind_ref), channel_id=1, source_target_pairs={{0,8},{8,16},{16,24},{24,32},{32,40},{40,48},{48,56},{56,64},{64,7... | collective-permute-start | bytes 786440 | tf_op jit(solution)/shard_map/ppermute | solution.py:24
  78.6 12.0 %collective-permute-start.4 = (bf16[1024,128]{1,0:T(8,128)(2,1)S(1)}, bf16[1024,128]{1,0:T(8,128)(2,1)S(1)}, u32[]{:S(2)}, u32[]{:S(2)}) collective-permute-start(bf16[1024,128]{1,0:T(8,128)(2,1)S(1)} %collective-permute-done.3.ahead_ref), channel_id=1, source_target_pairs={{0,1016},{8,0},{16,8},{24,16},{32,24},{40,32},{48,40},{56,48},{64,... | collective-permute-start | bytes 786440 | tf_op jit(solution)/shard_map/ppermute | solution.py:24
  87.1 3.6 %copy-start.1 = (bf16[128,1024]{1,0:T(8,128)(2,1)S(1)}, bf16[128,1024]{1,0:T(8,128)(2,1)}, u32[]{:S(2)}) copy-start(bf16[128,1024]{1,0:T(8,128)(2,1)} %w_ref.5) | copy-start | bytes 786436
  94.6 3.8 %collective-permute-start.5 = (bf16[4,512,128]{2,1,0:T(8,128)(2,1)S(1)}, bf16[4,512,128]{2,1,0:T(8,128)(2,1)S(1)}, u32[]{:S(2)}, u32[]{:S(2)}) collective-permute-start(bf16[4,512,128]{2,1,0:T(8,128)(2,1)S(1)} %get-tuple-element.21), channel_id=1, source_target_pairs={{0,1},{1,0},{2,3},{3,2},{4,5},{5,4},{6,7},{7,6},{8,9},{9,8},{10,11... | collective-permute-start | bytes 1572872 | tf_op jit(solution)/shard_map/ppermute | solution.py:24
  111.1 11.0 %copy-start.4 = (s32[1,128,4]{1,2,0:T(4,128)S(1)}, s32[1,128,4]{1,2,0:T(4,128)}, u32[]{:S(2)}) copy-start(s32[1,128,4]{1,2,0:T(4,128)} %param.11) | copy-start | bytes 6148
  111.2 28.2 %copy-start.5 = (bf16[2048,128]{1,0:T(8,128)(2,1)S(1)}, bf16[2048,128]{1,0:T(8,128)(2,1)}, u32[]{:S(2)}) copy-start(bf16[2048,128]{1,0:T(8,128)(2,1)} %param.8) | copy-start | bytes 1572868
  111.2 28.2 %copy-start.6 = (s32[2048]{0:T(1024)S(1)}, s32[2048]{0:T(1024)}, u32[]{:S(2)}) copy-start(s32[2048]{0:T(1024)} %param.10) | copy-start | bytes 24580
  111.9 27.4 %all-to-all-start.3 = ((bf16[128,4,128]{2,1,0:T(4,128)(2,1)}), bf16[128,4,128]{2,1,0:T(4,128)(2,1)S(1)}, u32[]{:S(2)}, u32[]{:S(2)}) async-start(bf16[128,4,128]{2,1,0:T(4,128)(2,1)} %add_convert_fusion), calls=%async_computation.3 | async-start | bytes 262144 | tf_op jit(solution)/shard_map/all_to_all | solution.py:18

commit v2 on v1

v2 whole, which is shorter than its diff:
```python
import jax
import jax.numpy as jnp
from jax import lax
from jax.experimental import pallas as pl
from jax.experimental.pallas import tpu as pltpu
from jax.sharding import Mesh
from jax.sharding import PartitionSpec as P

HEAD_DIM = 64
BF16 = jnp.bfloat16
F32 = jnp.float32
VMEM = pl.BlockSpec(memory_space=pltpu.VMEM)
SMEM = pl.BlockSpec(memory_space=pltpu.SMEM)
PARAMS = pltpu.CompilerParams(vmem_limit_bytes=32 * 1024 * 1024)


def exchange(array, axis):
    return lax.all_to_all(array, axis, split_axis=0, concat_axis=0, tiled=True)


def other_core(value):
    return lax.ppermute(value, "core", [(0, 1), (1, 0)])


def swapped(value, first):
    count = lax.axis_size("region")
    pairs = []
    for tile in range(count):
        ahead = (tile % 2 == 0) == first
        pairs.append((tile, (tile + (1 if ahead else -1)) % count))
    return lax.ppermute(value, "region", pairs)


def after(value, *earlier):
    return lax.optimization_barrier((value, *earlier))[0]


def half_product(part, x_ref, gain_ref, w_ref, scaled_ref, rows_ref, begin):
    blocks, rows, width = x_ref.shape
    for block in range(blocks):
        index = 2 * block + part
        at = pl.ds(block * width, width)
        source = pl.ds(pl.multiple_of(index * width, width), width)
        for third in range(3):
            rows_ref[at, third * width : (third + 1) * width] = w_ref[third, source, :]
    chunk = 128

    def step(i, _):
        at = pl.ds(pl.multiple_of(i * chunk, chunk), chunk)
        total = jnp.zeros((chunk, width), F32)
        for block in range(blocks):
            value = x_ref[block, at, :].astype(F32)
            total = total + value * value
            gain = gain_ref[pl.ds(2 * block + part, 1), :]
            scaled_ref[:, block * width : (block + 1) * width] = (value * gain).astype(BF16)
        square = jnp.sum(total, axis=-1, keepdims=True)
        begin(at, square, jnp.dot(scaled_ref[...], rows_ref[...], preferred_element_type=F32))
        return 0

    lax.fori_loop(0, rows // chunk, step, 0)


def own_half_kernel(core_ref, x_ref, gain_ref, w_ref, product_ref, square_ref, scaled_ref, rows_ref):
    def keep(at, square, product):
        product_ref[at, :] = product
        square_ref[at, :] = jnp.broadcast_to(square, (square.shape[0], square_ref.shape[1]))

    half_product(core_ref[0], x_ref, gain_ref, w_ref, scaled_ref, rows_ref, keep)


def other_half_kernel(
    core_ref, x_ref, gain_ref, w_ref, product_ref, square_ref, q_ref, kv_ref, scaled_ref, rows_ref
):
    blocks, rows, width = x_ref.shape

    def finish(at, square, product):
        mean = (square + square_ref[at, :]) / (2 * blocks * width)
        factor = lax.rsqrt(mean + 1e-05)
        for third in range(3):
            columns = slice(third * width, (third + 1) * width)
            whole = ((product[:, columns] + product_ref[at, columns]) * factor).astype(BF16)
            if third == 0:
                q_ref[at, :] = whole
            elif third == 1:
                kv_ref[at, :] = whole
            else:
                kv_ref[pl.ds(pl.multiple_of(rows + at.start, 128), at.size), :] = whole

    half_product(1 - core_ref[0], x_ref, gain_ref, w_ref, scaled_ref, rows_ref, finish)


def attend_block(q_ref, kv_ref, before, put):
    rows, width = q_ref.shape
    chunk = 256
    heads = width // HEAD_DIM
    lane = lax.broadcasted_iota(jnp.int32, (1, width), 1)
    keys = kv_ref[pl.ds(0, rows), :]
    values = kv_ref[pl.ds(rows, rows), :]
    summed = []
    for head in range(heads):
        mine = lane // HEAD_DIM == head
        ones = jnp.broadcast_to(jnp.where(mine, 1.0, 0.0), values.shape).astype(BF16)
        summed.append(jnp.concatenate([jnp.where(mine, values, 0).astype(BF16), ones], axis=1))
    for start in range(0, rows, chunk):
        at = pl.ds(start, chunk)
        queries = q_ref[at, :] * HEAD_DIM ** (-0.5)
        if before is not None:
            tops = before[0][at, :]
        new_tops = jnp.zeros((chunk, width), F32)
        gained = jnp.zeros((chunk, 2 * width), F32)
        for head in range(heads):
            mine = lane // HEAD_DIM == head
            scores = lax.dot_general(
                jnp.where(mine, queries, 0).astype(BF16),
                keys,
                (((1,), (1,)), ((), ())),
                preferred_element_type=F32,
            )
            top = jnp.max(scores, axis=-1, keepdims=True)
            if before is not None:
                top = jnp.maximum(top, tops[:, head * HEAD_DIM : head * HEAD_DIM + 1])
            expd = jnp.exp(scores - top).astype(BF16)
            gained = gained + jnp.dot(expd, summed[head], preferred_element_type=F32)
            new_tops = jnp.where(mine, top, new_tops)
        mixed, total = gained[:, :width], gained[:, width:]
        if before is not None:
            shrink = jnp.exp(tops - new_tops)
            mixed = before[2][at, :] * shrink + mixed
            total = before[1][at, :] * shrink + total
        put(at, new_tops, total, mixed)


def own_kernel(q_ref, kv_ref, top_ref, total_ref, mixed_ref):
    def put(at, top, total, mixed):
        top_ref[at, :] = top
        total_ref[at, :] = total
        mixed_ref[at, :] = mixed

    attend_block(q_ref, kv_ref, None, put)


PICKS = ((2, 1), (1, 2), (3, 0), (0, 3))


def is_seen(pick, mask_ref, odd_ref):
    even, odd = PICKS[pick]
    return mask_ref[0, jnp.where(odd_ref[0] == 0, even, odd)] > 0


def peer_kernel(
    pick, mask_ref, odd_ref, q_ref, kv_ref, top0_ref, total0_ref, mixed0_ref, top_ref, total_ref, mixed_ref
):
    before = (top0_ref, total0_ref, mixed0_ref)
    seen = is_seen(pick, mask_ref, odd_ref)

    def put(at, top, total, mixed):
        top_ref[at, :] = top
        total_ref[at, :] = total
        mixed_ref[at, :] = mixed

    @pl.when(seen)
    def _():
        attend_block(q_ref, kv_ref, before, put)

    @pl.when(jnp.logical_not(seen))
    def _():
        for old_ref, new_ref in zip(before, (top_ref, total_ref, mixed_ref)):
            new_ref[...] = old_ref[...]


def last_kernel(pick, mask_ref, odd_ref, q_ref, kv_ref, top0_ref, total0_ref, mixed0_ref, att_ref):
    before = (top0_ref, total0_ref, mixed0_ref)
    seen = is_seen(pick, mask_ref, odd_ref)

    def put(at, top, total, mixed):
        att_ref[at, :] = (mixed / total).astype(BF16)

    @pl.when(seen)
    def _():
        attend_block(q_ref, kv_ref, before, put)

    @pl.when(jnp.logical_not(seen))
    def _():
        att_ref[...] = (mixed0_ref[...] / total0_ref[...]).astype(BF16)


def share_kernel(core_ref, own_ref, other_ref, w_own_ref, w_other_ref, out_ref):
    blocks, _, width = out_ref.shape
    core = core_ref[0]
    both = jnp.concatenate([own_ref[...], other_ref[...]], axis=1)
    for block in range(blocks):
        at = pl.ds(pl.multiple_of((2 * block + core) * width, width), width)
        weight = jnp.concatenate([w_own_ref[:, at], w_other_ref[:, at]], axis=0)
        out_ref[block] = jnp.dot(both, weight, preferred_element_type=F32).astype(BF16)


def sum_kernel(base_ref, parts_ref, state_ref, back_ref):
    total = base_ref[...].astype(F32)
    for block in range(parts_ref.shape[0]):
        total = total + parts_ref[block].astype(F32)
    state_ref[...] = total
    back_ref[...] = total.astype(BF16)


def call(kernel, outs, scalars, arrays, name, scratch=(), flops=0, bytes_accessed=0, transcendentals=0):
    return pl.pallas_call(
        kernel,
        out_shape=outs,
        in_specs=[SMEM] * scalars + [VMEM] * arrays,
        out_specs=jax.tree.map(lambda _: VMEM, outs),
        scratch_shapes=list(scratch),
        compiler_params=PARAMS,
        name=name,
        cost_estimate=pl.CostEstimate(
            flops=flops, bytes_accessed=bytes_accessed, transcendentals=transcendentals
        ),
    )


def on_device(grid, g2m_weight, g2m_slot, slot_node, peer_mask, norm_gain, w_qkv, w_out):
    regions = lax.axis_size("region")
    chips = lax.axis_size("x")
    cap = slot_node.shape[2]
    slots = regions * cap
    rows = slots
    width = grid.shape[1]
    core = lax.axis_index("core").astype(jnp.int32).reshape(1)
    odd = (lax.axis_index("region") & 1).astype(jnp.int32).reshape(1)
    sds = jax.ShapeDtypeStruct

    scaled = (g2m_weight[:, None] * grid.astype(F32)).astype(BF16)
    slot_hot = (g2m_slot[None, :] == jnp.arange(slots, dtype=jnp.int32)[:, None]).astype(BF16)
    partial_value = jnp.dot(slot_hot, scaled, preferred_element_type=F32).astype(BF16)
    mesh_low = exchange(partial_value.reshape(regions, cap, width), "region").reshape(rows, width)

    own = exchange(jnp.broadcast_to(mesh_low, (chips, rows, width)), "x")
    other = other_core(own)
    gain = norm_gain.reshape(2 * chips, width)
    half = chips * width
    scratch = [pltpu.VMEM((128, half), BF16), pltpu.VMEM((half, 3 * width), BF16)]
    cost = dict(flops=2 * rows * half * 3 * width, bytes_accessed=2 << 20)
    product, square = call(
        own_half_kernel,
        (sds((rows, 3 * width), F32), sds((rows, width), F32)),
        1,
        3,
        "own_half",
        scratch,
        **cost,
    )(core, own, gain, w_qkv)
    queries, kv = call(
        other_half_kernel,
        (sds((rows, width), BF16), sds((2 * rows, width), BF16)),
        1,
        5,
        "other_half",
        scratch,
        **cost,
    )(core, other, gain, w_qkv, product, square)

    state = sds((rows, width), F32)
    states = (state, state, state)
    cost = dict(flops=8 * rows * rows * width, transcendentals=2 * rows * rows)

    def peer(pick, block, so_far):
        def kernel(*refs):
            peer_kernel(pick, *refs)

        return call(kernel, states, 2, 5, f"peer{pick}", **cost)(
            peer_mask, odd, queries, block, *so_far
        )

    def last(*refs):
        last_kernel(2, *refs)

    near1 = swapped(kv, True)
    near2 = swapped(kv, False)
    so_far = call(own_kernel, states, 0, 2, "own", **cost)(queries, kv)
    far2 = swapped(after(near1, so_far[0]), False)
    far1 = swapped(near2, True)
    w_other = other_core(after(w_out, so_far[0]))
    so_far = peer(0, near1, so_far)
    so_far = peer(1, near2, (after(so_far[0], w_other), *so_far[1:]))
    so_far = peer(3, far2, so_far)
    attended = call(last, sds((rows, width), BF16), 2, 5, "last", **cost)(
        peer_mask, odd, queries, far1, *so_far
    )

    attended_other = other_core(attended)
    summed = call(
        share_kernel,
        sds((chips, rows, width), BF16),
        1,
        4,
        "share",
        flops=2 * rows * 2 * width * half,
    )(core, attended, attended_other, w_out, w_other)
    mesh_slots, mesh_back = call(
        sum_kernel, (state, sds((rows, width), BF16)), 0, 2, "sum", bytes_accessed=1 << 20
    )(mesh_low, exchange(summed, "x"))

    returned = exchange(mesh_back.reshape(regions, cap, width), "region").reshape(slots, width)
    flat_nodes = slot_node[0].reshape(-1)
    node_hot = (jnp.arange(rows, dtype=jnp.int32)[:, None] == flat_nodes[None, :]).astype(F32)
    mesh_state = jnp.dot(
        node_hot, mesh_slots, precision=lax.Precision.HIGHEST, preferred_element_type=F32
    )
    gathered = jnp.dot(slot_hot.T, returned, preferred_element_type=F32)
    grid_out = (grid.astype(F32) + gathered).astype(BF16)
    return (mesh_state, grid_out)


def solution(mesh):
    regions, model = mesh.devices.shape
    split = Mesh(mesh.devices.reshape(regions, model // 2, 2), ("region", "x", "core"))
    model = ("x", "core")
    return jax.shard_map(
        on_device,
        mesh=split,
        in_specs=(
            P("region", model),
            P("region"),
            P("region"),
            P("region", None, None),
            P("region", None),
            P(),
            P(None, None, model),
            P(model, None),
        ),
        out_specs=(P("region", model), P("region", model)),
        check_vma=False,
    )
```

time: 143 us -> 136 us (0.951)
  starting transfers between devices: 32.3 us -> 26.9 us
    ppermute x6 -> x7, starting transfers between devices: 22.1 us -> 17.9 us  [the longest x4 12.2 us: swapped(): return lax.ppermute(value, 'region', pairs)]
    ppermute x6 -> x7, waiting for transfers between devices: 9.52 us -> 9.16 us  [the longest x4 6.99 us: swapped(): return lax.ppermute(value, 'region', pairs)]
    pallas_call x5 -> x9, Pallas kernels: 9.64 us -> 9.71 us  [the longest x3 3.27 us: peer(): call(kernel, states, 2, 5, f'peer{pick}', **cost)]
  transfers between devices with their start and end apart: 7 -> 8, of which waited for: 6 -> 7; matrix products, arithmetic and copies ran while one was open for 1% -> 1% of each run, Pallas kernels for 2% -> 4%
where the time goes in v2:
time: 136 us; the launch traced here: 135 us
  blocking collectives  67 us (49%)
  starting transfers between devices  26.9 us (20%)
  waiting for transfers between devices  24.9 us (18%)
  Pallas kernels  9.71 us (7%)
  matrix products  5.39 us (4%)
    all_to_all x3, blocking collectives, exchange(): return lax.all_to_all(array, axis, split_axis=0, concat_axis=0, tiled=True)  67 us
    all_to_all x1, waiting for transfers between devices, exchange(): return lax.all_to_all(array, axis, split_axis=0, concat_axis=0, tiled=True)  15.7 us
    ppermute x4, starting transfers between devices, swapped(): return lax.ppermute(value, 'region', pairs)  12.2 us
    all_to_all x1, starting transfers between devices, exchange(): return lax.all_to_all(array, axis, split_axis=0, concat_axis=0, tiled=True)  8.98 us
    ppermute x4, waiting for transfers between devices, swapped(): return lax.ppermute(value, 'region', pairs)  6.99 us
    ppermute x3, starting transfers between devices, other_core(): return lax.ppermute(value, 'core', [(0, 1), (1, 0)])  5.75 us
    pallas_call x3, Pallas kernels, peer(): call(kernel, states, 2, 5, f'peer{pick}', **cost)  3.27 us
  transfers between devices with their start and end apart: 8, of which 7 were waited for; matrix products, arithmetic and copies ran while one was open for 1% of the time, Pallas kernels for 4%

profile of v2, /device:TPU:6, one launch (start us, length us, event | category | flops | bytes accessed | tf_op | source)
XLA Modules:
  0.0 135.0 jit_solution(13089829660557897551)
XLA Ops:
  0.6 2.0 %fusion.6 = bf16[512,128]{1,0:T(8,128)(2,1)S(1)} fusion(s32[2048]{0:T(1024)} %param.10, bf16[2048,128]{1,0:T(8,128)(2,1)} %param.8, f32[2048]{0:T(1024)} %param.9), kind=kOutput, calls=%fused_computation.8 | convolution fusion | flops 270336000 | bytes 671744 | tf_op jit(solution)/shard_map/dot_general | solution.py:233
  2.6 43.8 %all_to_all.20 = bf16[128,4,128]{2,1,0:T(4,128)(2,1)S(1)} all-to-all(bf16[128,4,128]{2,1,0:T(4,128)(2,1)S(1)} %bitcast.14), channel_id=1, replica_groups=mesh['region'=128,'x'=4,'core'=2] {'region'}, dimensions={0} | all-to-all | bytes 262144 | tf_op jit(solution)/shard_map/all_to_all | solution.py:18
  46.5 10.7 %all_to_all.21.x_ref = bf16[4,512,128]{2,1,0:T(8,128)(2,1)S(1)} all-to-all(bf16[4,512,128]{2,1,0:T(8,128)(2,1)S(1)} %broadcast_in_dim.2), channel_id=1, replica_groups=mesh['region'=128,'x'=4,'core'=2] {'x'}, dimensions={0} | all-to-all | bytes 1048576 | tf_op jit(solution)/shard_map/all_to_all | solution.py:18
  57.2 1.9 %collective-permute-start = (bf16[4,512,128]{2,1,0:T(8,128)(2,1)S(1)}, bf16[4,512,128]{2,1,0:T(8,128)(2,1)S(1)}, u32[]{:S(2)}, u32[]{:S(2)}) collective-permute-start(bf16[4,512,128]{2,1,0:T(8,128)(2,1)S(1)} %all_to_all.21.x_ref), channel_id=1, source_target_pairs={{0,1},{1,0},{2,3},{3,2},{4,5},{5,4},{6,7},{7,6},{8,9},{9,8},{10,11... | collective-permute-start | bytes 1572872 | tf_op jit(solution)/shard_map/ppermute | solution.py:22
  59.2 1.0 own_half.1
  60.1 0.9 collective-permute-done.x_ref
  61.0 1.0 other_half.1
  62.0 3.0 %collective-permute-start.3 = (bf16[1024,128]{1,0:T(8,128)(2,1)S(1)}, bf16[1024,128]{1,0:T(8,128)(2,1)S(1)}, u32[]{:S(2)}, u32[]{:S(2)}) collective-permute-start(bf16[1024,128]{1,0:T(8,128)(2,1)S(1)} %get-tuple-element.26.kv_ref), channel_id=1, source_target_pairs={{0,8},{8,0},{16,24},{24,16},{32,40},{40,32},{48,56},{56,48},{64,72... | collective-permute-start | bytes 786440 | tf_op jit(solution)/shard_map/ppermute | solution.py:31
  65.0 2.4 %collective-permute-start.1 = (bf16[1024,128]{1,0:T(8,128)(2,1)S(1)}, bf16[1024,128]{1,0:T(8,128)(2,1)S(1)}, u32[]{:S(2)}, u32[]{:S(2)}) collective-permute-start(bf16[1024,128]{1,0:T(8,128)(2,1)S(1)} %get-tuple-element.26.kv_ref), channel_id=1, source_target_pairs={{0,1016},{8,16},{16,8},{24,32},{32,24},{40,48},{48,40},{56,64},{64... | collective-permute-start | bytes 786440 | tf_op jit(solution)/shard_map/ppermute | solution.py:31
  67.4 1.2 own.1
  68.6 1.9 %collective-permute-start.5 = (bf16[128,1024]{1,0:T(8,128)(2,1)S(1)}, bf16[128,1024]{1,0:T(8,128)(2,1)S(1)}, u32[]{:S(2)}, u32[]{:S(2)}) collective-permute-start(bf16[128,1024]{1,0:T(8,128)(2,1)S(1)} %copy-done.1), channel_id=1, source_target_pairs={{0,1},{1,0},{2,3},{3,2},{4,5},{5,4},{6,7},{7,6},{8,9},{9,8},{10,11... | collective-permute-start | bytes 786440 | tf_op jit(solution)/shard_map/ppermute | solution.py:22
  70.5 1.9 %collective-permute-done.3.refs_3_ = bf16[1024,128]{1,0:T(8,128)(2,1)S(1)} collective-permute-done((bf16[1024,128]{1,0:T(8,128)(2,1)S(1)}, bf16[1024,128]{1,0:T(8,128)(2,1)S(1)}, u32[]{:S(2)}, u32[]{:S(2)}) %collective-permute-start.3) | collective-permute-done | bytes 262176 | tf_op jit(solution)/shard_map/ppermute | solution.py:31
  72.4 4.9 %collective-permute-start.4 = (bf16[1024,128]{1,0:T(8,128)(2,1)S(1)}, bf16[1024,128]{1,0:T(8,128)(2,1)S(1)}, u32[]{:S(2)}, u32[]{:S(2)}) collective-permute-start(bf16[1024,128]{1,0:T(8,128)(2,1)S(1)} %collective-permute-done.3.refs_3_), channel_id=1, source_target_pairs={{0,1016},{8,16},{16,8},{24,32},{32,24},{40,48},{48,40},{56,64},{64... | collective-permute-start | bytes 786440 | tf_op jit(solution)/shard_map/ppermute | solution.py:31
  77.3 1.0 collective-permute-done.1.refs_3_
  78.3 1.9 %collective-permute-start.2 = (bf16[1024,128]{1,0:T(8,128)(2,1)S(1)}, bf16[1024,128]{1,0:T(8,128)(2,1)S(1)}, u32[]{:S(2)}, u32[]{:S(2)}) collective-permute-start(bf16[1024,128]{1,0:T(8,128)(2,1)S(1)} %collective-permute-done.1.refs_3_), channel_id=1, source_target_pairs={{0,8},{8,0},{16,24},{24,16},{32,40},{40,32},{48,56},{56,48},{64,72... | collective-permute-start | bytes 786440 | tf_op jit(solution)/shard_map/ppermute | solution.py:31
  80.3 0.6 peer0.1
  80.9 2.1 %peer1.1 = (f32[512,128]{1,0:T(8,128)S(1)}, f32[512,128]{1,0:T(8,128)S(1)}, f32[512,128]{1,0:T(8,128)S(1)}) custom-call(s32[1,4]{1,0:T(1,128)S(1)} %copy-done.3, s32[1]{0:T(128)} %bitcast.3.refs_1_, bf16[512,128]{1,0:T(8,128)(2,1)S(1)} %get-tuple-element.25.q_ref.refs_2_, bf16[1024,128]{1,0:T(8,128)(2,1)S(1)} %collective-permute-done.1.refs_3_, ...), custom_call_target="tpu_custom_call" | custom-call | flops 268435456 | tf_op jit(solution)/shard_map/peer1/pallas_call | solution.py:269
  83.0 2.2 %collective-permute-done.4.refs_3_ = bf16[1024,128]{1,0:T(8,128)(2,1)S(1)} collective-permute-done((bf16[1024,128]{1,0:T(8,128)(2,1)S(1)}, bf16[1024,128]{1,0:T(8,128)(2,1)S(1)}, u32[]{:S(2)}, u32[]{:S(2)}) %collective-permute-start.4) | collective-permute-done | bytes 262176 | tf_op jit(solution)/shard_map/ppermute | solution.py:31
  85.1 0.6 peer3.1
  85.7 1.9 %collective-permute-done.2.refs_3_ = bf16[1024,128]{1,0:T(8,128)(2,1)S(1)} collective-permute-done((bf16[1024,128]{1,0:T(8,128)(2,1)S(1)}, bf16[1024,128]{1,0:T(8,128)(2,1)S(1)}, u32[]{:S(2)}, u32[]{:S(2)}) %collective-permute-start.2) | collective-permute-done | bytes 262176 | tf_op jit(solution)/shard_map/ppermute | solution.py:31
  87.7 2.1 %last.1.own_ref = bf16[512,128]{1,0:T(8,128)(2,1)S(1)} custom-call(s32[1,4]{1,0:T(1,128)S(1)} %copy-done.3, s32[1]{0:T(128)} %bitcast.3.refs_1_, bf16[512,128]{1,0:T(8,128)(2,1)S(1)} %get-tuple-element.25.q_ref.refs_2_, bf16[1024,128]{1,0:T(8,128)(2,1)S(1)} %collective-permute-done.2.refs_3_, f32[512,128]{1,0:T(8,128)S(1)} %get-tuple-element.39.refs_4_, ...), custom_call_target="tpu_custom_call" | custom-call | flops 268435456 | tf_op jit(solution)/shard_map/last/pallas_call | solution.py:285
  89.8 1.9 %collective-permute-start.6 = (bf16[512,128]{1,0:T(8,128)(2,1)S(1)}, bf16[512,128]{1,0:T(8,128)(2,1)S(1)}, u32[]{:S(2)}, u32[]{:S(2)}) collective-permute-start(bf16[512,128]{1,0:T(8,128)(2,1)S(1)} %last.1.own_ref), channel_id=1, source_target_pairs={{0,1},{1,0},{2,3},{3,2},{4,5},{5,4},{6,7},{7,6},{8,9},{9,8},{10,11... | collective-permute-start | bytes 393224 | tf_op jit(solution)/shard_map/ppermute | solution.py:22
  91.7 1.3 collective-permute-done.6.other_ref
  93.0 0.4 share.1
  93.5 12.5 %all_to_all.22.parts_ref = bf16[4,512,128]{2,1,0:T(8,128)(2,1)S(1)} all-to-all(bf16[4,512,128]{2,1,0:T(8,128)(2,1)S(1)} %share.1), channel_id=1, replica_groups=mesh['region'=128,'x'=4,'core'=2] {'x'}, dimensions={0} | all-to-all | bytes 1048576 | tf_op jit(solution)/shard_map/all_to_all | solution.py:18
  106.0 0.7 sum.1
  106.7 9.0 %all-to-all-start.3 = ((bf16[128,4,128]{2,1,0:T(4,128)(2,1)}), bf16[128,4,128]{2,1,0:T(4,128)(2,1)S(1)}, u32[]{:S(2)}, u32[]{:S(2)}) async-start(bf16[128,4,128]{2,1,0:T(4,128)(2,1)} %bitcast.5), calls=%async_computation.3 | async-start | bytes 262144 | tf_op jit(solution)/shard_map/all_to_all | solution.py:18
  115.7 0.1 copy.10
  115.8 0.1 eq.29
  115.9 1.3 fusion.8
  117.2 15.7 %all-to-all-done.3 = bf16[128,4,128]{2,1,0:T(4,128)(2,1)S(1)} async-done(((bf16[128,4,128]{2,1,0:T(4,128)(2,1)}), bf16[128,4,128]{2,1,0:T(4,128)(2,1)S(1)}, u32[]{:S(2)}, u32[]{:S(2)}) %all-to-all-start.3) | async-done | bytes 131104 | tf_op jit(solution)/shard_map/all_to_all | solution.py:18
  133.0 2.1 %fusion.3 = bf16[2048,128]{1,0:T(8,128)(2,1)} fusion(bf16[512,128]{1,0:T(8,128)(2,1)S(1)} %bitcast.13, s32[2048]{0:T(1024)S(1)} %copy-done.6, bf16[2048,128]{1,0:T(8,128)(2,1)S(1)} %copy-done.5), kind=kOutput, calls=%fused_computation.4 | convolution fusion | flops 270270464 | bytes 1187840 | tf_op jit(solution)/shard_map/dot_general | solution.py:308
  (16 shorter events, 0.1 us)
Async XLA Ops:
  46.4 12.7 %copy-start = (bf16[3,1024,128]{2,1,0:T(8,128)(2,1)S(1)}, bf16[3,1024,128]{2,1,0:T(8,128)(2,1)}, u32[]{:S(2)}) copy-start(bf16[3,1024,128]{2,1,0:T(8,128)(2,1)} %w_ref.3) | copy-start | bytes 2359300
  46.4 12.7 %copy-start.2 = (f32[1024]{0:T(1024)S(1)}, f32[1024]{0:T(1024)}, u32[]{:S(2)}) copy-start(f32[1024]{0:T(1024)} %param.13) | copy-start | bytes 12292
  57.2 3.8 %collective-permute-start = (bf16[4,512,128]{2,1,0:T(8,128)(2,1)S(1)}, bf16[4,512,128]{2,1,0:T(8,128)(2,1)S(1)}, u32[]{:S(2)}, u32[]{:S(2)}) collective-permute-start(bf16[4,512,128]{2,1,0:T(8,128)(2,1)S(1)} %all_to_all.21.x_ref), channel_id=1, source_target_pairs={{0,1},{1,0},{2,3},{3,2},{4,5},{5,4},{6,7},{7,6},{8,9},{9,8},{10,11... | collective-permute-start | bytes 1572872 | tf_op jit(solution)/shard_map/ppermute | solution.py:22
  62.0 6.6 %copy-start.1 = (bf16[128,1024]{1,0:T(8,128)(2,1)S(1)}, bf16[128,1024]{1,0:T(8,128)(2,1)}, u32[]{:S(2)}) copy-start(bf16[128,1024]{1,0:T(8,128)(2,1)} %w_own_ref.1) | copy-start | bytes 786436
  62.0 18.2 %copy-start.3 = (s32[1,4]{1,0:T(1,128)S(1)}, s32[1,4]{1,0:T(1,128)}, u32[]{:S(2)}) copy-start(s32[1,4]{1,0:T(1,128)} %refs_0_.7) | copy-start | bytes 52
  62.0 10.4 %collective-permute-start.3 = (bf16[1024,128]{1,0:T(8,128)(2,1)S(1)}, bf16[1024,128]{1,0:T(8,128)(2,1)S(1)}, u32[]{:S(2)}, u32[]{:S(2)}) collective-permute-start(bf16[1024,128]{1,0:T(8,128)(2,1)S(1)} %get-tuple-element.26.kv_ref), channel_id=1, source_target_pairs={{0,8},{8,0},{16,24},{24,16},{32,40},{40,32},{48,56},{56,48},{64,72... | collective-permute-start | bytes 786440 | tf_op jit(solution)/shard_map/ppermute | solution.py:31
  65.0 13.3 %collective-permute-start.1 = (bf16[1024,128]{1,0:T(8,128)(2,1)S(1)}, bf16[1024,128]{1,0:T(8,128)(2,1)S(1)}, u32[]{:S(2)}, u32[]{:S(2)}) collective-permute-start(bf16[1024,128]{1,0:T(8,128)(2,1)S(1)} %get-tuple-element.26.kv_ref), channel_id=1, source_target_pairs={{0,1016},{8,16},{16,8},{24,32},{32,24},{40,48},{48,40},{56,64},{64... | collective-permute-start | bytes 786440 | tf_op jit(solution)/shard_map/ppermute | solution.py:31
  68.6 12.3 %collective-permute-start.5 = (bf16[128,1024]{1,0:T(8,128)(2,1)S(1)}, bf16[128,1024]{1,0:T(8,128)(2,1)S(1)}, u32[]{:S(2)}, u32[]{:S(2)}) collective-permute-start(bf16[128,1024]{1,0:T(8,128)(2,1)S(1)} %copy-done.1), channel_id=1, source_target_pairs={{0,1},{1,0},{2,3},{3,2},{4,5},{5,4},{6,7},{7,6},{8,9},{9,8},{10,11... | collective-permute-start | bytes 786440 | tf_op jit(solution)/shard_map/ppermute | solution.py:22
  72.4 12.7 %collective-permute-start.4 = (bf16[1024,128]{1,0:T(8,128)(2,1)S(1)}, bf16[1024,128]{1,0:T(8,128)(2,1)S(1)}, u32[]{:S(2)}, u32[]{:S(2)}) collective-permute-start(bf16[1024,128]{1,0:T(8,128)(2,1)S(1)} %collective-permute-done.3.refs_3_), channel_id=1, source_target_pairs={{0,1016},{8,16},{16,8},{24,32},{32,24},{40,48},{48,40},{56,64},{64... | collective-permute-start | bytes 786440 | tf_op jit(solution)/shard_map/ppermute | solution.py:31
  78.3 9.4 %collective-permute-start.2 = (bf16[1024,128]{1,0:T(8,128)(2,1)S(1)}, bf16[1024,128]{1,0:T(8,128)(2,1)S(1)}, u32[]{:S(2)}, u32[]{:S(2)}) collective-permute-start(bf16[1024,128]{1,0:T(8,128)(2,1)S(1)} %collective-permute-done.1.refs_3_), channel_id=1, source_target_pairs={{0,8},{8,0},{16,24},{24,16},{32,40},{40,32},{48,56},{56,48},{64,72... | collective-permute-start | bytes 786440 | tf_op jit(solution)/shard_map/ppermute | solution.py:31
  89.8 3.2 %collective-permute-start.6 = (bf16[512,128]{1,0:T(8,128)(2,1)S(1)}, bf16[512,128]{1,0:T(8,128)(2,1)S(1)}, u32[]{:S(2)}, u32[]{:S(2)}) collective-permute-start(bf16[512,128]{1,0:T(8,128)(2,1)S(1)} %last.1.own_ref), channel_id=1, source_target_pairs={{0,1},{1,0},{2,3},{3,2},{4,5},{5,4},{6,7},{7,6},{8,9},{9,8},{10,11... | collective-permute-start | bytes 393224 | tf_op jit(solution)/shard_map/ppermute | solution.py:22
  93.5 22.2 %copy-start.4 = (s32[1,128,4]{1,2,0:T(4,128)S(1)}, s32[1,128,4]{1,2,0:T(4,128)}, u32[]{:S(2)}) copy-start(s32[1,128,4]{1,2,0:T(4,128)} %param.11) | copy-start | bytes 6148
  106.0 27.0 %copy-start.5 = (bf16[2048,128]{1,0:T(8,128)(2,1)S(1)}, bf16[2048,128]{1,0:T(8,128)(2,1)}, u32[]{:S(2)}) copy-start(bf16[2048,128]{1,0:T(8,128)(2,1)} %param.8) | copy-start | bytes 1572868
  106.0 27.0 %copy-start.6 = (s32[2048]{0:T(1024)S(1)}, s32[2048]{0:T(1024)}, u32[]{:S(2)}) copy-start(s32[2048]{0:T(1024)} %param.10) | copy-start | bytes 24580
  106.7 26.3 %all-to-all-start.3 = ((bf16[128,4,128]{2,1,0:T(4,128)(2,1)}), bf16[128,4,128]{2,1,0:T(4,128)(2,1)S(1)}, u32[]{:S(2)}, u32[]{:S(2)}) async-start(bf16[128,4,128]{2,1,0:T(4,128)(2,1)} %bitcast.5), calls=%async_computation.3 | async-start | bytes 262144 | tf_op jit(solution)/shard_map/all_to_all | solution.py:18

commit v3 on v2

v3 whole, which is shorter than its diff:
```python
import jax
import jax.numpy as jnp
from jax import lax
from jax.experimental import pallas as pl
from jax.experimental.pallas import tpu as pltpu
from jax.sharding import Mesh
from jax.sharding import PartitionSpec as P

HEAD_DIM = 64
OFFSETS = (-2, -1, 1, 2)
CHUNK = 128
BF16 = jnp.bfloat16
F32 = jnp.float32
VMEM = pl.BlockSpec(memory_space=pltpu.VMEM)
PARAMS = pltpu.CompilerParams(vmem_limit_bytes=32 * 1024 * 1024)


def exchange(array, axis):
    return lax.all_to_all(array, axis, split_axis=0, concat_axis=0, tiled=True)


def other_core(value):
    return lax.ppermute(value, "core", [(0, 1), (1, 0)])


def swapped(value, axis, first):
    count, cores = lax.axis_size(axis), lax.axis_size("core")
    pairs = []
    for place in range(count):
        for core in range(cores):
            ahead = ((place + core) % 2 == 0) == first
            partner = (place + (1 if ahead else -1)) % count
            pairs.append((place * cores + core, partner * cores + core))
    return lax.ppermute(value, (axis, "core"), pairs)


def after(value, *earlier):
    return lax.optimization_barrier((value, *earlier))[0]


def feature_places():
    core, chip, chips = lax.axis_index("core"), lax.axis_index("x"), lax.axis_size("x")
    step = 1 - 2 * ((chip + core) & 1)
    wrap = lambda place: lax.rem(place + chips, chips)
    return core, (chip, wrap(chip + step), wrap(chip - step), wrap(chip + 2))


def block_product(blocks, gain_ref, w_ref, scaled_ref, rows_ref, put):
    rows, width = blocks[0][0].shape
    for i, (_, index) in enumerate(blocks):
        source = pl.ds(pl.multiple_of(index * width, width), width)
        for third in range(3):
            columns = slice(third * width, (third + 1) * width)
            rows_ref[i * width : (i + 1) * width, columns] = w_ref[third, source, :]

    def step(number, _):
        at = pl.ds(pl.multiple_of(number * CHUNK, CHUNK), CHUNK)
        total = jnp.zeros((CHUNK, width), F32)
        for i, (ref, index) in enumerate(blocks):
            value = ref[at, :].astype(F32)
            total = total + value * value
            gain = gain_ref[pl.ds(index, 1), :]
            scaled_ref[:, i * width : (i + 1) * width] = (value * gain).astype(BF16)
        put(at, total, jnp.dot(scaled_ref[...], rows_ref[...], preferred_element_type=F32))
        return 0

    lax.fori_loop(0, rows // CHUNK, step, 0)


def early_kernel(
    own_ref, first_ref, second_ref, gain_ref, w_ref, w_out_ref, square_ref, product_ref, sent_ref, *scratch
):
    core, (own, first, second, _) = feature_places()
    rows, width = own_ref.shape
    for i, ref in enumerate((own_ref, first_ref, second_ref)):
        sent_ref[i * rows : (i + 1) * rows, :] = ref[...]
    for i in range(gain_ref.shape[0]):
        sent_ref[4 * rows + i * width : 4 * rows + (i + 1) * width, :] = w_out_ref[:, i * width : (i + 1) * width]

    def put(at, square, product):
        square_ref[at, :] = square
        product_ref[at, :] = product

    blocks = [(own_ref, 2 * own + core), (first_ref, 2 * first + core), (second_ref, 2 * second + core)]
    block_product(blocks, gain_ref, w_ref, *scratch, put)


def middle_kernel(last_ref, gain_ref, w_ref, square0_ref, product0_ref, square_ref, product_ref, *scratch):
    core, (_, _, _, last) = feature_places()

    def put(at, square, product):
        square_ref[at, :] = square0_ref[at, :] + square
        product_ref[at, :] = product0_ref[at, :] + product

    block_product([(last_ref, 2 * last + core)], gain_ref, w_ref, *scratch, put)


def late_kernel(arrived_ref, gain_ref, w_ref, square0_ref, product0_ref, q_ref, kv_ref, *scratch):
    core, (own, first, second, last) = feature_places()
    rows, width = q_ref.shape
    features = gain_ref.shape[0] * width

    def put(at, square, product):
        mean = jnp.sum(square0_ref[at, :] + square, axis=-1, keepdims=True) / features
        factor = lax.rsqrt(mean + 1e-05)
        whole = ((product0_ref[at, :] + product) * factor).astype(BF16)
        q_ref[at, :] = whole[:, :width]
        kv_ref[at, :] = whole[:, width : 2 * width]
        kv_ref[pl.ds(pl.multiple_of(rows + at.start, CHUNK), CHUNK), :] = whole[:, 2 * width :]

    blocks = []
    for i, chip in enumerate((own, second, first, last)):
        blocks.append((arrived_ref.at[pl.ds(i * rows, rows)], 2 * chip + 1 - core))
    block_product(blocks, gain_ref, w_ref, *scratch, put)


def attend_block(q_ref, kv_ref, seen, before, put):
    rows, width = q_ref.shape
    chunk = 256
    heads = width // HEAD_DIM
    lane = lax.broadcasted_iota(jnp.int32, (1, width), 1)
    keys = kv_ref[pl.ds(0, rows), :]
    values = kv_ref[pl.ds(rows, rows), :]
    summed = []
    for head in range(heads):
        mine = lane // HEAD_DIM == head
        ones = jnp.broadcast_to(jnp.where(mine, 1.0, 0.0), values.shape).astype(BF16)
        summed.append(jnp.concatenate([jnp.where(mine, values, 0).astype(BF16), ones], axis=1))
    for start in range(0, rows, chunk):
        at = pl.ds(start, chunk)
        queries = q_ref[at, :] * HEAD_DIM ** (-0.5)
        if before is not None:
            tops = before[0][at, :]
        new_tops = jnp.zeros((chunk, width), F32)
        gained = jnp.zeros((chunk, 2 * width), F32)
        for head in range(heads):
            mine = lane // HEAD_DIM == head
            scores = lax.dot_general(
                jnp.where(mine, queries, 0).astype(BF16),
                keys,
                (((1,), (1,)), ((), ())),
                preferred_element_type=F32,
            )
            if seen is not None:
                scores = jnp.where(seen, scores, -1e30)
            top = jnp.max(scores, axis=-1, keepdims=True)
            if before is not None:
                top = jnp.maximum(top, tops[:, head * HEAD_DIM : head * HEAD_DIM + 1])
            expd = jnp.exp(scores - top).astype(BF16)
            gained = gained + jnp.dot(expd, summed[head], preferred_element_type=F32)
            new_tops = jnp.where(mine, top, new_tops)
        mixed, total = gained[:, :width], gained[:, width:]
        if before is not None:
            shrink = jnp.exp(tops - new_tops)
            mixed = before[2][at, :] * shrink + mixed
            total = before[1][at, :] * shrink + total
        put(at, new_tops, total, mixed)


def is_seen(turn, mask_ref):
    odd = (lax.axis_index("region") + lax.axis_index("core")) & 1
    offset = (1, -1, -2, 2)[turn]
    wanted = jnp.where(odd == 0, OFFSETS.index(offset), OFFSETS.index(-offset))
    mask = mask_ref[...]
    lane = lax.broadcasted_iota(jnp.int32, mask.shape, 1)
    return jnp.sum(jnp.where(lane == wanted, mask, 0), axis=-1, keepdims=True) > 0


def own_kernel(q_ref, kv_ref, *states):
    def put(at, *values):
        for ref, value in zip(states, values):
            ref[at, :] = value

    attend_block(q_ref, kv_ref, None, None, put)


def peer_kernel(turn, mask_ref, q_ref, kv_ref, *states):
    def put(at, *values):
        for ref, value in zip(states[3:], values):
            ref[at, :] = value

    attend_block(q_ref, kv_ref, is_seen(turn, mask_ref), states[:3], put)


def last_kernel(turn, mask_ref, q_ref, kv_ref, *refs):
    def put(at, top, total, mixed):
        refs[3][at, :] = (mixed / total).astype(BF16)

    attend_block(q_ref, kv_ref, is_seen(turn, mask_ref), refs[:3], put)


def column_share(chip, core, own_ref, other_ref, w_own_ref, arrived_ref):
    rows, width = own_ref.shape
    index = 2 * chip + core
    at = pl.ds(pl.multiple_of(index * width, width), width)
    both = jnp.concatenate([own_ref[...], other_ref[...]], axis=1)
    w_other = arrived_ref[pl.ds(pl.multiple_of(4 * rows + index * width, width), width), :]
    weight = jnp.concatenate([w_own_ref[:, at], w_other], axis=0)
    return jnp.dot(both, weight, preferred_element_type=F32)


def far_share_kernel(*refs):
    core, (_, _, _, last) = feature_places()
    refs[4][...] = column_share(last, core, *refs[:4]).astype(BF16)


def near_share_kernel(*refs):
    core, (own, first, second, _) = feature_places()
    ins, (base_ref, own_out, first_out, second_out) = refs[:4], refs[4:]
    second_out[...] = column_share(second, core, *ins).astype(BF16)
    first_out[...] = column_share(first, core, *ins)
    own_out[...] = base_ref[...].astype(F32) + column_share(own, core, *ins)


def add_kernel(share_ref, arrived_ref, out_ref):
    out_ref[...] = (share_ref[...] + arrived_ref[...].astype(F32)).astype(BF16)


def sum_kernel(base_ref, first_ref, second_ref, state_ref, back_ref):
    total = base_ref[...] + (first_ref[...].astype(F32) + second_ref[...].astype(F32))
    state_ref[...] = total
    back_ref[...] = total.astype(BF16)


def call(kernel, outs, name, scratch=(), flops=0, bytes_accessed=0, transcendentals=0):
    def run(*args):
        return pl.pallas_call(
            kernel,
            out_shape=outs,
            in_specs=[VMEM] * len(args),
            out_specs=jax.tree.map(lambda _: VMEM, outs),
            scratch_shapes=list(scratch),
            compiler_params=PARAMS,
            name=name,
            cost_estimate=pl.CostEstimate(
                flops=flops, bytes_accessed=bytes_accessed, transcendentals=transcendentals
            ),
        )(*args)

    return run


def on_device(grid, g2m_weight, g2m_slot, slot_node, peer_mask, norm_gain, w_qkv, w_out):
    regions = lax.axis_size("region")
    parts = lax.axis_size("x") * lax.axis_size("core")
    cap = slot_node.shape[2]
    slots = regions * cap
    rows = slots
    width = grid.shape[1]
    low = jax.ShapeDtypeStruct((rows, width), BF16)
    state = jax.ShapeDtypeStruct((rows, width), F32)

    scaled = (g2m_weight[:, None] * grid.astype(F32)).astype(BF16)
    slot_hot = (g2m_slot[None, :] == jnp.arange(slots, dtype=jnp.int32)[:, None]).astype(BF16)
    partial_value = jnp.dot(slot_hot, scaled, preferred_element_type=F32).astype(BF16)
    mesh_low = exchange(partial_value.reshape(regions, cap, width), "region").reshape(rows, width)

    first = swapped(mesh_low, "x", True)
    second = swapped(mesh_low, "x", False)
    last = swapped(first, "x", False)
    gain = norm_gain.reshape(parts, width)

    def product(kernel, outs, name, blocks, *args):
        depth = blocks * width
        return call(
            kernel,
            outs,
            name,
            scratch=[pltpu.VMEM((CHUNK, depth), BF16), pltpu.VMEM((depth, 3 * width), BF16)],
            flops=6 * rows * depth * width,
            bytes_accessed=2 << 20,
        )(*args)

    sums = (state, jax.ShapeDtypeStruct((rows, 3 * width), F32))
    sent = jax.ShapeDtypeStruct((4 * rows + parts * width, width), BF16)
    *so_far, sent = product(
        early_kernel, (*sums, sent), "early", 3, mesh_low, first, second, gain, w_qkv, w_out
    )
    arrived = other_core(lax.dynamic_update_slice(sent, last, (3 * rows, 0)))
    so_far = product(middle_kernel, sums, "middle", 1, last, gain, w_qkv, *so_far)
    kvs = jax.ShapeDtypeStruct((2 * rows, width), BF16)
    queries, kv = product(late_kernel, (low, kvs), "late", 4, arrived, gain, w_qkv, *so_far)

    cost = dict(flops=8 * rows * rows * width, transcendentals=2 * rows * rows)

    def attend(turn, *args):
        outs, kernel = (low, last_kernel) if turn == 3 else ((state,) * 3, peer_kernel)
        return call(lambda *refs: kernel(turn, *refs), outs, f"peer{turn}", **cost)(
            peer_mask, queries, *args
        )

    kv0 = swapped(kv, "region", True)
    kv1 = swapped(kv, "region", False)
    so_far = call(own_kernel, (state,) * 3, "own", **cost)(queries, kv)
    kv2 = swapped(after(kv0, so_far[0]), "region", False)
    kv3 = swapped(kv1, "region", True)
    so_far = attend(0, kv0, *so_far)
    so_far = attend(1, kv1, *so_far)
    so_far = attend(2, kv2, *so_far)
    attended = attend(3, kv3, *so_far)

    shared = (attended, other_core(attended), w_out, arrived)
    flops = 4 * rows * width * width
    far_share = call(far_share_kernel, low, "far_share", flops=flops)(*shared)
    relayed = swapped(far_share, "x", False)
    base, first_share, second_share = call(
        near_share_kernel, (state, state, low), "near_share", flops=3 * flops
    )(*shared, mesh_low)
    from_second = swapped(second_share, "x", False)
    passed_on = call(add_kernel, low, "add", bytes_accessed=1 << 19)(first_share, relayed)
    from_first = swapped(passed_on, "x", True)
    mesh_slots, mesh_back = call(sum_kernel, (state, low), "sum", bytes_accessed=1 << 20)(
        base, from_first, from_second
    )

    returned = exchange(mesh_back.reshape(regions, cap, width), "region").reshape(slots, width)
    flat_nodes = slot_node[0].reshape(-1)
    node_hot = (jnp.arange(rows, dtype=jnp.int32)[:, None] == flat_nodes[None, :]).astype(F32)
    mesh_state = jnp.dot(
        node_hot, mesh_slots, precision=lax.Precision.HIGHEST, preferred_element_type=F32
    )
    gathered = jnp.dot(slot_hot.T, returned, preferred_element_type=F32)
    grid_out = (grid.astype(F32) + gathered).astype(BF16)
    return (mesh_state, grid_out)


def solution(mesh):
    regions, model = mesh.devices.shape
    split = Mesh(mesh.devices.reshape(regions, model // 2, 2), ("region", "x", "core"))
    model = ("x", "core")
    return jax.shard_map(
        on_device,
        mesh=split,
        in_specs=(
            P("region", model),
            P("region"),
            P("region"),
            P("region", None, None),
            P("region", None),
            P(),
            P(None, None, model),
            P(model, None),
        ),
        out_specs=(P("region", model), P("region", model)),
        check_vma=False,
    )
```

time: 136 us -> 138 us (1.015)
  blocking collectives: 67 us -> 43.8 us
  starting transfers between devices: 26.9 us -> 41.9 us
  waiting for transfers between devices: 24.9 us -> 34 us
  Pallas kernels: 9.71 us -> 11.3 us
    all_to_all x3 -> x1, blocking collectives: 67 us -> 43.8 us  [exchange(): return lax.all_to_all(array, axis, split_axis=0, concat_axis=0, tiled=True)]
    ppermute x4 -> x10, starting transfers between devices: 12.2 us -> 29.4 us  [swapped(): return lax.ppermute(value, (axis, 'core'), pairs)]
    ppermute x4 -> x10, waiting for transfers between devices: 6.99 us -> 16.1 us  [swapped(): return lax.ppermute(value, (axis, 'core'), pairs)]
    pallas_call x9 -> x12, Pallas kernels: 9.71 us -> 11.3 us  [run(): pl.pallas_call(kernel, out_shape=outs, in_specs=[VMEM] * len(args), out_s...]
    ppermute x3 -> x2, starting transfers between devices: 5.75 us -> 4.48 us  [other_core(): return lax.ppermute(value, 'core', [(0, 1), (1, 0)])]
  transfers between devices with their start and end apart: 8 -> 13, of which waited for: 7 -> 13; matrix products, arithmetic and copies ran while one was open for 1% -> 1% of each run, Pallas kernels for 4% -> 6%
where the time goes in v3:
time: 138 us
  blocking collectives  43.8 us (32%)
  starting transfers between devices  41.9 us (30%)
  waiting for transfers between devices  34 us (25%)
  Pallas kernels  11.3 us (8%)
  matrix products  5.48 us (4%)
    all_to_all x1, blocking collectives, exchange(): return lax.all_to_all(array, axis, split_axis=0, concat_axis=0, tiled=True)  43.8 us
    ppermute x10, starting transfers between devices, swapped(): return lax.ppermute(value, (axis, 'core'), pairs)  29.4 us
    ppermute x10, waiting for transfers between devices, swapped(): return lax.ppermute(value, (axis, 'core'), pairs)  16.1 us
    all_to_all x1, waiting for transfers between devices, exchange(): return lax.all_to_all(array, axis, split_axis=0, concat_axis=0, tiled=True)  15.4 us
    pallas_call x12, Pallas kernels, run(): pl.pallas_call(kernel, out_shape=outs, in_specs=[VMEM] * len(args), out_s...  11.3 us
    all_to_all x1, starting transfers between devices, exchange(): return lax.all_to_all(array, axis, split_axis=0, concat_axis=0, tiled=True)  8.03 us
    ppermute x2, starting transfers between devices, other_core(): return lax.ppermute(value, 'core', [(0, 1), (1, 0)])  4.48 us
  transfers between devices with their start and end apart: 13, of which 13 were waited for; matrix products, arithmetic and copies ran while one was open for 1% of the time, Pallas kernels for 6%

profile of v3, /device:TPU:6, one launch (start us, length us, event | category | flops | bytes accessed | tf_op | source)
XLA Modules:
  0.0 137.6 jit_solution(16914510877193835403)
XLA Ops:
  0.7 2.1 %fusion.6 = bf16[512,128]{1,0:T(8,128)(2,1)S(1)} fusion(s32[2048]{0:T(1024)} %param.10, bf16[2048,128]{1,0:T(8,128)(2,1)} %param.8, f32[2048]{0:T(1024)} %param.9), kind=kOutput, calls=%fused_computation.8 | convolution fusion | flops 270336000 | bytes 671744 | tf_op jit(solution)/shard_map/dot_general | solution.py:255
  2.7 43.8 %all_to_all.10 = bf16[128,4,128]{2,1,0:T(4,128)(2,1)S(1)} all-to-all(bf16[128,4,128]{2,1,0:T(4,128)(2,1)S(1)} %bitcast.15), channel_id=1, replica_groups=mesh['region'=128,'x'=4,'core'=2] {'region'}, dimensions={0} | all-to-all | bytes 262144 | tf_op jit(solution)/shard_map/all_to_all | solution.py:19
  46.5 2.7 %collective-permute-start = (bf16[512,128]{1,0:T(8,128)(2,1)S(1)}, bf16[512,128]{1,0:T(8,128)(2,1)S(1)}, u32[]{:S(2)}, u32[]{:S(2)}) collective-permute-start(bf16[512,128]{1,0:T(8,128)(2,1)S(1)} %bitcast.7), channel_id=1, source_target_pairs={{0,2},{1,7},{2,0},{3,5},{4,6},{5,3},{6,4},{7,1},{8,10},{9,15},{10,... | collective-permute-start | bytes 393224 | tf_op jit(solution)/shard_map/ppermute | solution.py:34
  49.3 3.0 %collective-permute-start.1 = (bf16[512,128]{1,0:T(8,128)(2,1)S(1)}, bf16[512,128]{1,0:T(8,128)(2,1)S(1)}, u32[]{:S(2)}, u32[]{:S(2)}) collective-permute-start(bf16[512,128]{1,0:T(8,128)(2,1)S(1)} %bitcast.8), channel_id=1, source_target_pairs={{0,6},{1,3},{2,4},{3,1},{4,2},{5,7},{6,0},{7,5},{8,14},{9,11},{10,... | collective-permute-start | bytes 393224 | tf_op jit(solution)/shard_map/ppermute | solution.py:34
  52.3 1.1 collective-permute-done.first_ref
  53.4 3.1 %collective-permute-start.2 = (bf16[512,128]{1,0:T(8,128)(2,1)S(1)}, bf16[512,128]{1,0:T(8,128)(2,1)S(1)}, u32[]{:S(2)}, u32[]{:S(2)}) collective-permute-start(bf16[512,128]{1,0:T(8,128)(2,1)S(1)} %collective-permute-done.first_ref), channel_id=1, source_target_pairs={{0,6},{1,3},{2,4},{3,1},{4,2},{5,7},{6,0},{7,5},{8,14},{9,11},{10,... | collective-permute-start | bytes 393224 | tf_op jit(solution)/shard_map/ppermute | solution.py:34
  58.3 3.1 %collective-permute-done.2.last_ref = bf16[512,128]{1,0:T(8,128)(2,1)S(1)} collective-permute-done((bf16[512,128]{1,0:T(8,128)(2,1)S(1)}, bf16[512,128]{1,0:T(8,128)(2,1)S(1)}, u32[]{:S(2)}, u32[]{:S(2)}) %collective-permute-start.2) | collective-permute-done | bytes 131104 | tf_op jit(solution)/shard_map/ppermute | solution.py:34
  61.5 1.9 %collective-permute-start.3 = (bf16[3072,128]{1,0:T(8,128)(2,1)S(1)}, bf16[3072,128]{1,0:T(8,128)(2,1)S(1)}, u32[]{:S(2)}, u32[]{:S(2)}) collective-permute-start(bf16[3072,128]{1,0:T(8,128)(2,1)S(1)} %constant_dynamic-update-slice_fusion), channel_id=1, source_target_pairs={{0,1},{1,0},{2,3},{3,2},{4,5},{5,4},{6,7},{7,6},{8,9},{9,8},{10,11... | collective-permute-start | bytes 2359304 | tf_op jit(solution)/shard_map/ppermute | solution.py:23
  64.2 1.5 %collective-permute-done.3.arrived_ref.refs_3_ = bf16[3072,128]{1,0:T(8,128)(2,1)S(1)} collective-permute-done((bf16[3072,128]{1,0:T(8,128)(2,1)S(1)}, bf16[3072,128]{1,0:T(8,128)(2,1)S(1)}, u32[]{:S(2)}, u32[]{:S(2)}) %collective-permute-start.3) | collective-permute-done | bytes 786464 | tf_op jit(solution)/shard_map/ppermute | solution.py:23
  65.6 1.0 late.1
  66.7 2.9 %collective-permute-start.6 = (bf16[1024,128]{1,0:T(8,128)(2,1)S(1)}, bf16[1024,128]{1,0:T(8,128)(2,1)S(1)}, u32[]{:S(2)}, u32[]{:S(2)}) collective-permute-start(bf16[1024,128]{1,0:T(8,128)(2,1)S(1)} %get-tuple-element.33.kv_ref), channel_id=1, source_target_pairs={{0,8},{1,1017},{8,0},{9,17},{16,24},{17,9},{24,16},{25,33},{32,40}... | collective-permute-start | bytes 786440 | tf_op jit(solution)/shard_map/ppermute | solution.py:34
  69.6 2.6 %collective-permute-start.4 = (bf16[1024,128]{1,0:T(8,128)(2,1)S(1)}, bf16[1024,128]{1,0:T(8,128)(2,1)S(1)}, u32[]{:S(2)}, u32[]{:S(2)}) collective-permute-start(bf16[1024,128]{1,0:T(8,128)(2,1)S(1)} %get-tuple-element.33.kv_ref), channel_id=1, source_target_pairs={{0,1016},{1,9},{8,16},{9,1},{16,8},{17,25},{24,32},{25,17},{32,24}... | collective-permute-start | bytes 786440 | tf_op jit(solution)/shard_map/ppermute | solution.py:34
  72.1 1.2 own.1
  73.3 2.5 %collective-permute-done.6.refs_2_ = bf16[1024,128]{1,0:T(8,128)(2,1)S(1)} collective-permute-done((bf16[1024,128]{1,0:T(8,128)(2,1)S(1)}, bf16[1024,128]{1,0:T(8,128)(2,1)S(1)}, u32[]{:S(2)}, u32[]{:S(2)}) %collective-permute-start.6) | collective-permute-done | bytes 262176 | tf_op jit(solution)/shard_map/ppermute | solution.py:34
  75.8 4.1 %collective-permute-start.7 = (bf16[1024,128]{1,0:T(8,128)(2,1)S(1)}, bf16[1024,128]{1,0:T(8,128)(2,1)S(1)}, u32[]{:S(2)}, u32[]{:S(2)}) collective-permute-start(bf16[1024,128]{1,0:T(8,128)(2,1)S(1)} %collective-permute-done.6.refs_2_), channel_id=1, source_target_pairs={{0,1016},{1,9},{8,16},{9,1},{16,8},{17,25},{24,32},{25,17},{32,24}... | collective-permute-start | bytes 786440 | tf_op jit(solution)/shard_map/ppermute | solution.py:34
  79.9 1.2 collective-permute-done.4.refs_2_
  81.1 1.9 %collective-permute-start.5 = (bf16[1024,128]{1,0:T(8,128)(2,1)S(1)}, bf16[1024,128]{1,0:T(8,128)(2,1)S(1)}, u32[]{:S(2)}, u32[]{:S(2)}) collective-permute-start(bf16[1024,128]{1,0:T(8,128)(2,1)S(1)} %collective-permute-done.4.refs_2_), channel_id=1, source_target_pairs={{0,8},{1,1017},{8,0},{9,17},{16,24},{17,9},{24,16},{25,33},{32,40}... | collective-permute-start | bytes 786440 | tf_op jit(solution)/shard_map/ppermute | solution.py:34
  83.1 1.5 %peer0.1 = (f32[512,128]{1,0:T(8,128)S(1)}, f32[512,128]{1,0:T(8,128)S(1)}, f32[512,128]{1,0:T(8,128)S(1)}) custom-call(s32[1,4]{1,0:T(1,128)S(1)} %copy-done.3, bf16[512,128]{1,0:T(8,128)(2,1)S(1)} %get-tuple-element.32.q_ref.refs_1_, bf16[1024,128]{1,0:T(8,128)(2,1)S(1)} %collective-permute-done.6.refs_2_, f32[512,128]{1,0:T(8,128)S(1)} %get-tuple-element.34.refs_3_, ...), custom_call_target="tpu_custom_call" | custom-call | flops 268435456 | tf_op jit(solution)/shard_map/peer0/pallas_call | solution.py:227
  84.6 1.5 %peer1.1 = (f32[512,128]{1,0:T(8,128)S(1)}, f32[512,128]{1,0:T(8,128)S(1)}, f32[512,128]{1,0:T(8,128)S(1)}) custom-call(s32[1,4]{1,0:T(1,128)S(1)} %copy-done.3, bf16[512,128]{1,0:T(8,128)(2,1)S(1)} %get-tuple-element.32.q_ref.refs_1_, bf16[1024,128]{1,0:T(8,128)(2,1)S(1)} %collective-permute-done.4.refs_2_, f32[512,128]{1,0:T(8,128)S(1)} %get-tuple-element.38.refs_3_, ...), custom_call_target="tpu_custom_call" | custom-call | flops 268435456 | tf_op jit(solution)/shard_map/peer1/pallas_call | solution.py:227
  86.1 1.7 %collective-permute-done.7.refs_2_ = bf16[1024,128]{1,0:T(8,128)(2,1)S(1)} collective-permute-done((bf16[1024,128]{1,0:T(8,128)(2,1)S(1)}, bf16[1024,128]{1,0:T(8,128)(2,1)S(1)}, u32[]{:S(2)}, u32[]{:S(2)}) %collective-permute-start.7) | collective-permute-done | bytes 262176 | tf_op jit(solution)/shard_map/ppermute | solution.py:34
  87.8 1.5 %peer2.1 = (f32[512,128]{1,0:T(8,128)S(1)}, f32[512,128]{1,0:T(8,128)S(1)}, f32[512,128]{1,0:T(8,128)S(1)}) custom-call(s32[1,4]{1,0:T(1,128)S(1)} %copy-done.3, bf16[512,128]{1,0:T(8,128)(2,1)S(1)} %get-tuple-element.32.q_ref.refs_1_, bf16[1024,128]{1,0:T(8,128)(2,1)S(1)} %collective-permute-done.7.refs_2_, f32[512,128]{1,0:T(8,128)S(1)} %get-tuple-element.41.refs_3_, ...), custom_call_target="tpu_custom_call" | custom-call | flops 268435456 | tf_op jit(solution)/shard_map/peer2/pallas_call | solution.py:227
  89.4 1.5 %peer3.1.refs_0_ = bf16[512,128]{1,0:T(8,128)(2,1)S(1)} custom-call(s32[1,4]{1,0:T(1,128)S(1)} %copy-done.3, bf16[512,128]{1,0:T(8,128)(2,1)S(1)} %get-tuple-element.32.q_ref.refs_1_, bf16[1024,128]{1,0:T(8,128)(2,1)S(1)} %collective-permute-done.5.refs_2_, f32[512,128]{1,0:T(8,128)S(1)} %get-tuple-element.44.refs_3_, ...), custom_call_target="tpu_custom_call" | custom-call | flops 268435456 | tf_op jit(solution)/shard_map/peer3/pallas_call | solution.py:227
  90.9 2.6 %collective-permute-start.8 = (bf16[512,128]{1,0:T(8,128)(2,1)S(1)}, bf16[512,128]{1,0:T(8,128)(2,1)S(1)}, u32[]{:S(2)}, u32[]{:S(2)}) collective-permute-start(bf16[512,128]{1,0:T(8,128)(2,1)S(1)} %peer3.1.refs_0_), channel_id=1, source_target_pairs={{0,1},{1,0},{2,3},{3,2},{4,5},{5,4},{6,7},{7,6},{8,9},{9,8},{10,11... | collective-permute-start | bytes 393224 | tf_op jit(solution)/shard_map/ppermute | solution.py:23
  94.7 3.8 %collective-permute-start.9 = (bf16[512,128]{1,0:T(8,128)(2,1)S(1)}, bf16[512,128]{1,0:T(8,128)(2,1)S(1)}, u32[]{:S(2)}, u32[]{:S(2)}) collective-permute-start(bf16[512,128]{1,0:T(8,128)(2,1)S(1)} %far_share.1), channel_id=1, source_target_pairs={{0,6},{1,3},{2,4},{3,1},{4,2},{5,7},{6,0},{7,5},{8,14},{9,11},{10,... | collective-permute-start | bytes 393224 | tf_op jit(solution)/shard_map/ppermute | solution.py:34
  98.9 3.3 %collective-permute-start.11 = (bf16[512,128]{1,0:T(8,128)(2,1)S(1)}, bf16[512,128]{1,0:T(8,128)(2,1)S(1)}, u32[]{:S(2)}, u32[]{:S(2)}) collective-permute-start(bf16[512,128]{1,0:T(8,128)(2,1)S(1)} %get-tuple-element.49), channel_id=1, source_target_pairs={{0,6},{1,3},{2,4},{3,1},{4,2},{5,7},{6,0},{7,5},{8,14},{9,11},{10,... | collective-permute-start | bytes 393224 | tf_op jit(solution)/shard_map/ppermute | solution.py:34
  102.8 2.1 %collective-permute-start.10 = (bf16[512,128]{1,0:T(8,128)(2,1)S(1)}, bf16[512,128]{1,0:T(8,128)(2,1)S(1)}, u32[]{:S(2)}, u32[]{:S(2)}) collective-permute-start(bf16[512,128]{1,0:T(8,128)(2,1)S(1)} %add.8), channel_id=1, source_target_pairs={{0,2},{1,7},{2,0},{3,5},{4,6},{5,3},{6,4},{7,1},{8,10},{9,15},{10,... | collective-permute-start | bytes 393224 | tf_op jit(solution)/shard_map/ppermute | solution.py:34
  104.9 2.4 %collective-permute-done.11.second_ref = bf16[512,128]{1,0:T(8,128)(2,1)S(1)} collective-permute-done((bf16[512,128]{1,0:T(8,128)(2,1)S(1)}, bf16[512,128]{1,0:T(8,128)(2,1)S(1)}, u32[]{:S(2)}, u32[]{:S(2)}) %collective-permute-start.11) | collective-permute-done | bytes 131104 | tf_op jit(solution)/shard_map/ppermute | solution.py:34
  107.3 2.5 %collective-permute-done.10.first_ref = bf16[512,128]{1,0:T(8,128)(2,1)S(1)} collective-permute-done((bf16[512,128]{1,0:T(8,128)(2,1)S(1)}, bf16[512,128]{1,0:T(8,128)(2,1)S(1)}, u32[]{:S(2)}, u32[]{:S(2)}) %collective-permute-start.10) | collective-permute-done | bytes 131104 | tf_op jit(solution)/shard_map/ppermute | solution.py:34
  110.5 8.0 %all-to-all-start.1 = ((bf16[128,4,128]{2,1,0:T(4,128)(2,1)}), bf16[128,4,128]{2,1,0:T(4,128)(2,1)S(1)}, u32[]{:S(2)}, u32[]{:S(2)}) async-start(bf16[128,4,128]{2,1,0:T(4,128)(2,1)} %bitcast.3), calls=%async_computation.1 | async-start | bytes 262144 | tf_op jit(solution)/shard_map/all_to_all | solution.py:19
  118.8 1.3 fusion.8
  120.1 15.4 %all-to-all-done.1 = bf16[128,4,128]{2,1,0:T(4,128)(2,1)S(1)} async-done(((bf16[128,4,128]{2,1,0:T(4,128)(2,1)}), bf16[128,4,128]{2,1,0:T(4,128)(2,1)S(1)}, u32[]{:S(2)}, u32[]{:S(2)}) %all-to-all-start.1) | async-done | bytes 131104 | tf_op jit(solution)/shard_map/all_to_all | solution.py:19
  135.5 2.1 %fusion.3 = bf16[2048,128]{1,0:T(8,128)(2,1)} fusion(bf16[512,128]{1,0:T(8,128)(2,1)S(1)} %bitcast.14, s32[2048]{0:T(1024)S(1)} %copy-done.6, bf16[2048,128]{1,0:T(8,128)(2,1)S(1)} %copy-done.5), kind=kOutput, calls=%fused_computation.4 | convolution fusion | flops 270270464 | bytes 1187840 | tf_op jit(solution)/shard_map/dot_general | solution.py:322
  (27 shorter events, 5.9 us)
Async XLA Ops:
  0.6 56.7 %copy-start.2 = (f32[1024]{0:T(1024)S(1)}, f32[1024]{0:T(1024)}, u32[]{:S(2)}) copy-start(f32[1024]{0:T(1024)} %param.13) | copy-start | bytes 12292
  0.6 56.7 %copy-start = (bf16[3,1024,128]{2,1,0:T(8,128)(2,1)S(1)}, bf16[3,1024,128]{2,1,0:T(8,128)(2,1)}, u32[]{:S(2)}) copy-start(bf16[3,1024,128]{2,1,0:T(8,128)(2,1)} %w_ref.5) | copy-start | bytes 2359300
  0.7 56.7 %copy-start.1 = (bf16[128,1024]{1,0:T(8,128)(2,1)S(1)}, bf16[128,1024]{1,0:T(8,128)(2,1)}, u32[]{:S(2)}) copy-start(bf16[128,1024]{1,0:T(8,128)(2,1)} %refs_2_.3) | copy-start | bytes 786436
  46.5 6.8 %collective-permute-start = (bf16[512,128]{1,0:T(8,128)(2,1)S(1)}, bf16[512,128]{1,0:T(8,128)(2,1)S(1)}, u32[]{:S(2)}, u32[]{:S(2)}) collective-permute-start(bf16[512,128]{1,0:T(8,128)(2,1)S(1)} %bitcast.7), channel_id=1, source_target_pairs={{0,2},{1,7},{2,0},{3,5},{4,6},{5,3},{6,4},{7,1},{8,10},{9,15},{10,... | collective-permute-start | bytes 393224 | tf_op jit(solution)/shard_map/ppermute | solution.py:34
  49.3 8.1 %collective-permute-start.1 = (bf16[512,128]{1,0:T(8,128)(2,1)S(1)}, bf16[512,128]{1,0:T(8,128)(2,1)S(1)}, u32[]{:S(2)}, u32[]{:S(2)}) collective-permute-start(bf16[512,128]{1,0:T(8,128)(2,1)S(1)} %bitcast.8), channel_id=1, source_target_pairs={{0,6},{1,3},{2,4},{3,1},{4,2},{5,7},{6,0},{7,5},{8,14},{9,11},{10,... | collective-permute-start | bytes 393224 | tf_op jit(solution)/shard_map/ppermute | solution.py:34
  53.4 8.1 %collective-permute-start.2 = (bf16[512,128]{1,0:T(8,128)(2,1)S(1)}, bf16[512,128]{1,0:T(8,128)(2,1)S(1)}, u32[]{:S(2)}, u32[]{:S(2)}) collective-permute-start(bf16[512,128]{1,0:T(8,128)(2,1)S(1)} %collective-permute-done.first_ref), channel_id=1, source_target_pairs={{0,6},{1,3},{2,4},{3,1},{4,2},{5,7},{6,0},{7,5},{8,14},{9,11},{10,... | collective-permute-start | bytes 393224 | tf_op jit(solution)/shard_map/ppermute | solution.py:34
  61.5 4.2 %collective-permute-start.3 = (bf16[3072,128]{1,0:T(8,128)(2,1)S(1)}, bf16[3072,128]{1,0:T(8,128)(2,1)S(1)}, u32[]{:S(2)}, u32[]{:S(2)}) collective-permute-start(bf16[3072,128]{1,0:T(8,128)(2,1)S(1)} %constant_dynamic-update-slice_fusion), channel_id=1, source_target_pairs={{0,1},{1,0},{2,3},{3,2},{4,5},{5,4},{6,7},{7,6},{8,9},{9,8},{10,11... | collective-permute-start | bytes 2359304 | tf_op jit(solution)/shard_map/ppermute | solution.py:23
  66.7 16.4 %copy-start.3 = (s32[1,4]{1,0:T(1,128)S(1)}, s32[1,4]{1,0:T(1,128)}, u32[]{:S(2)}) copy-start(s32[1,4]{1,0:T(1,128)} %refs_0_.7) | copy-start | bytes 52
  66.7 9.2 %collective-permute-start.6 = (bf16[1024,128]{1,0:T(8,128)(2,1)S(1)}, bf16[1024,128]{1,0:T(8,128)(2,1)S(1)}, u32[]{:S(2)}, u32[]{:S(2)}) collective-permute-start(bf16[1024,128]{1,0:T(8,128)(2,1)S(1)} %get-tuple-element.33.kv_ref), channel_id=1, source_target_pairs={{0,8},{1,1017},{8,0},{9,17},{16,24},{17,9},{24,16},{25,33},{32,40}... | collective-permute-start | bytes 786440 | tf_op jit(solution)/shard_map/ppermute | solution.py:34
  69.6 11.6 %collective-permute-start.4 = (bf16[1024,128]{1,0:T(8,128)(2,1)S(1)}, bf16[1024,128]{1,0:T(8,128)(2,1)S(1)}, u32[]{:S(2)}, u32[]{:S(2)}) collective-permute-start(bf16[1024,128]{1,0:T(8,128)(2,1)S(1)} %get-tuple-element.33.kv_ref), channel_id=1, source_target_pairs={{0,1016},{1,9},{8,16},{9,1},{16,8},{17,25},{24,32},{25,17},{32,24}... | collective-permute-start | bytes 786440 | tf_op jit(solution)/shard_map/ppermute | solution.py:34
  75.8 11.9 %collective-permute-start.7 = (bf16[1024,128]{1,0:T(8,128)(2,1)S(1)}, bf16[1024,128]{1,0:T(8,128)(2,1)S(1)}, u32[]{:S(2)}, u32[]{:S(2)}) collective-permute-start(bf16[1024,128]{1,0:T(8,128)(2,1)S(1)} %collective-permute-done.6.refs_2_), channel_id=1, source_target_pairs={{0,1016},{1,9},{8,16},{9,1},{16,8},{17,25},{24,32},{25,17},{32,24}... | collective-permute-start | bytes 786440 | tf_op jit(solution)/shard_map/ppermute | solution.py:34
  81.1 8.3 %collective-permute-start.5 = (bf16[1024,128]{1,0:T(8,128)(2,1)S(1)}, bf16[1024,128]{1,0:T(8,128)(2,1)S(1)}, u32[]{:S(2)}, u32[]{:S(2)}) collective-permute-start(bf16[1024,128]{1,0:T(8,128)(2,1)S(1)} %collective-permute-done.4.refs_2_), channel_id=1, source_target_pairs={{0,8},{1,1017},{8,0},{9,17},{16,24},{17,9},{24,16},{25,33},{32,40}... | collective-permute-start | bytes 786440 | tf_op jit(solution)/shard_map/ppermute | solution.py:34
  90.9 3.5 %collective-permute-start.8 = (bf16[512,128]{1,0:T(8,128)(2,1)S(1)}, bf16[512,128]{1,0:T(8,128)(2,1)S(1)}, u32[]{:S(2)}, u32[]{:S(2)}) collective-permute-start(bf16[512,128]{1,0:T(8,128)(2,1)S(1)} %peer3.1.refs_0_), channel_id=1, source_target_pairs={{0,1},{1,0},{2,3},{3,2},{4,5},{5,4},{6,7},{7,6},{8,9},{9,8},{10,11... | collective-permute-start | bytes 393224 | tf_op jit(solution)/shard_map/ppermute | solution.py:23
  94.7 8.1 %collective-permute-start.9 = (bf16[512,128]{1,0:T(8,128)(2,1)S(1)}, bf16[512,128]{1,0:T(8,128)(2,1)S(1)}, u32[]{:S(2)}, u32[]{:S(2)}) collective-permute-start(bf16[512,128]{1,0:T(8,128)(2,1)S(1)} %far_share.1), channel_id=1, source_target_pairs={{0,6},{1,3},{2,4},{3,1},{4,2},{5,7},{6,0},{7,5},{8,14},{9,11},{10,... | collective-permute-start | bytes 393224 | tf_op jit(solution)/shard_map/ppermute | solution.py:34
  98.9 19.7 %copy-start.4 = (s32[1,128,4]{1,2,0:T(4,128)S(1)}, s32[1,128,4]{1,2,0:T(4,128)}, u32[]{:S(2)}) copy-start(s32[1,128,4]{1,2,0:T(4,128)} %param.11) | copy-start | bytes 6148
  98.9 8.4 %collective-permute-start.11 = (bf16[512,128]{1,0:T(8,128)(2,1)S(1)}, bf16[512,128]{1,0:T(8,128)(2,1)S(1)}, u32[]{:S(2)}, u32[]{:S(2)}) collective-permute-start(bf16[512,128]{1,0:T(8,128)(2,1)S(1)} %get-tuple-element.49), channel_id=1, source_target_pairs={{0,6},{1,3},{2,4},{3,1},{4,2},{5,7},{6,0},{7,5},{8,14},{9,11},{10,... | collective-permute-start | bytes 393224 | tf_op jit(solution)/shard_map/ppermute | solution.py:34
  102.8 32.7 %copy-start.5 = (bf16[2048,128]{1,0:T(8,128)(2,1)S(1)}, bf16[2048,128]{1,0:T(8,128)(2,1)}, u32[]{:S(2)}) copy-start(bf16[2048,128]{1,0:T(8,128)(2,1)} %param.8) | copy-start | bytes 1572868
  102.8 32.7 %copy-start.6 = (s32[2048]{0:T(1024)S(1)}, s32[2048]{0:T(1024)}, u32[]{:S(2)}) copy-start(s32[2048]{0:T(1024)} %param.10) | copy-start | bytes 24580
  102.8 7.0 %collective-permute-start.10 = (bf16[512,128]{1,0:T(8,128)(2,1)S(1)}, bf16[512,128]{1,0:T(8,128)(2,1)S(1)}, u32[]{:S(2)}, u32[]{:S(2)}) collective-permute-start(bf16[512,128]{1,0:T(8,128)(2,1)S(1)} %add.8), channel_id=1, source_target_pairs={{0,2},{1,7},{2,0},{3,5},{4,6},{5,3},{6,4},{7,1},{8,10},{9,15},{10,... | collective-permute-start | bytes 393224 | tf_op jit(solution)/shard_map/ppermute | solution.py:34
  110.5 25.0 %all-to-all-start.1 = ((bf16[128,4,128]{2,1,0:T(4,128)(2,1)}), bf16[128,4,128]{2,1,0:T(4,128)(2,1)S(1)}, u32[]{:S(2)}, u32[]{:S(2)}) async-start(bf16[128,4,128]{2,1,0:T(4,128)(2,1)} %bitcast.3), calls=%async_computation.1 | async-start | bytes 262144 | tf_op jit(solution)/shard_map/all_to_all | solution.py:19

commit v4 on v3

--- a/solution.py
+++ b/solution.py
@@ -36,13 +36,6 @@
 
 def after(value, *earlier):
     return lax.optimization_barrier((value, *earlier))[0]
-
-
-def feature_places():
-    core, chip, chips = lax.axis_index("core"), lax.axis_index("x"), lax.axis_size("x")
-    step = 1 - 2 * ((chip + core) & 1)
-    wrap = lambda place: lax.rem(place + chips, chips)
-    return core, (chip, wrap(chip + step), wrap(chip - step), wrap(chip + 2))
 
 
 def block_product(blocks, gain_ref, w_ref, scaled_ref, rows_ref, put):
@@ -67,36 +60,19 @@
     lax.fori_loop(0, rows // CHUNK, step, 0)
 
 
-def early_kernel(
-    own_ref, first_ref, second_ref, gain_ref, w_ref, w_out_ref, square_ref, product_ref, sent_ref, *scratch
-):
-    core, (own, first, second, _) = feature_places()
-    rows, width = own_ref.shape
-    for i, ref in enumerate((own_ref, first_ref, second_ref)):
-        sent_ref[i * rows : (i + 1) * rows, :] = ref[...]
-    for i in range(gain_ref.shape[0]):
-        sent_ref[4 * rows + i * width : 4 * rows + (i + 1) * width, :] = w_out_ref[:, i * width : (i + 1) * width]
+def own_half_kernel(own_ref, gain_ref, w_ref, square_ref, product_ref, *scratch):
+    core = lax.axis_index("core")
 
     def put(at, square, product):
         square_ref[at, :] = square
         product_ref[at, :] = product
 
-    blocks = [(own_ref, 2 * own + core), (first_ref, 2 * first + core), (second_ref, 2 * second + core)]
+    blocks = [(own_ref.at[chip], 2 * chip + core) for chip in range(own_ref.shape[0])]
     block_product(blocks, gain_ref, w_ref, *scratch, put)
 
 
-def middle_kernel(last_ref, gain_ref, w_ref, square0_ref, product0_ref, square_ref, product_ref, *scratch):
-    core, (_, _, _, last) = feature_places()
-
-    def put(at, square, product):
-        square_ref[at, :] = square0_ref[at, :] + square
-        product_ref[at, :] = product0_ref[at, :] + product
-
-    block_product([(last_ref, 2 * last + core)], gain_ref, w_ref, *scratch, put)
-
-
-def late_kernel(arrived_ref, gain_ref, w_ref, square0_ref, product0_ref, q_ref, kv_ref, *scratch):
-    core, (own, first, second, last) = feature_places()
+def other_half_kernel(other_ref, gain_ref, w_ref, square0_ref, product0_ref, q_ref, kv_ref, *scratch):
+    core = lax.axis_index("core")
     rows, width = q_ref.shape
     features = gain_ref.shape[0] * width
 
@@ -108,9 +84,7 @@
         kv_ref[at, :] = whole[:, width : 2 * width]
         kv_ref[pl.ds(pl.multiple_of(rows + at.start, CHUNK), CHUNK), :] = whole[:, 2 * width :]
 
-    blocks = []
-    for i, chip in enumerate((own, second, first, last)):
-        blocks.append((arrived_ref.at[pl.ds(i * rows, rows)], 2 * chip + 1 - core))
+    blocks = [(other_ref.at[chip], 2 * chip + 1 - core) for chip in range(other_ref.shape[0])]
     block_product(blocks, gain_ref, w_ref, *scratch, put)
 
 
@@ -189,35 +163,20 @@
     attend_block(q_ref, kv_ref, is_seen(turn, mask_ref), refs[:3], put)
 
 
-def column_share(chip, core, own_ref, other_ref, w_own_ref, arrived_ref):
-    rows, width = own_ref.shape
-    index = 2 * chip + core
-    at = pl.ds(pl.multiple_of(index * width, width), width)
+def share_kernel(own_ref, other_ref, w_own_ref, w_other_ref, out_ref):
+    blocks, _, width = out_ref.shape
+    core = lax.axis_index("core")
     both = jnp.concatenate([own_ref[...], other_ref[...]], axis=1)
-    w_other = arrived_ref[pl.ds(pl.multiple_of(4 * rows + index * width, width), width), :]
-    weight = jnp.concatenate([w_own_ref[:, at], w_other], axis=0)
-    return jnp.dot(both, weight, preferred_element_type=F32)
-
-
-def far_share_kernel(*refs):
-    core, (_, _, _, last) = feature_places()
-    refs[4][...] = column_share(last, core, *refs[:4]).astype(BF16)
-
-
-def near_share_kernel(*refs):
-    core, (own, first, second, _) = feature_places()
-    ins, (base_ref, own_out, first_out, second_out) = refs[:4], refs[4:]
-    second_out[...] = column_share(second, core, *ins).astype(BF16)
-    first_out[...] = column_share(first, core, *ins)
-    own_out[...] = base_ref[...].astype(F32) + column_share(own, core, *ins)
-
-
-def add_kernel(share_ref, arrived_ref, out_ref):
-    out_ref[...] = (share_ref[...] + arrived_ref[...].astype(F32)).astype(BF16)
-
-
-def sum_kernel(base_ref, first_ref, second_ref, state_ref, back_ref):
-    total = base_ref[...] + (first_ref[...].astype(F32) + second_ref[...].astype(F32))
+    for block in range(blocks):
+        at = pl.ds(pl.multiple_of((2 * block + core) * width, width), width)
+        weight = jnp.concatenate([w_own_ref[:, at], w_other_ref[:, at]], axis=0)
+        out_ref[block] = jnp.dot(both, weight, preferred_element_type=F32).astype(BF16)
+
+
+def sum_kernel(base_ref, parts_ref, state_ref, back_ref):
+    total = base_ref[...].astype(F32)
+    for block in range(parts_ref.shape[0]):
+        total = total + parts_ref[block].astype(F32)
     state_ref[...] = total
     back_ref[...] = total.astype(BF16)
 
@@ -242,7 +201,8 @@
 
 def on_device(grid, g2m_weight, g2m_slot, slot_node, peer_mask, norm_gain, w_qkv, w_out):
     regions = lax.axis_size("region")
-    parts = lax.axis_size("x") * lax.axis_size("core")
+    chips = lax.axis_size("x")
+    parts = chips * lax.axis_size("core")
     cap = slot_node.shape[2]
     slots = regions * cap
     rows = slots
@@ -255,9 +215,8 @@
     partial_value = jnp.dot(slot_hot, scaled, preferred_element_type=F32).astype(BF16)
     mesh_low = exchange(partial_value.reshape(regions, cap, width), "region").reshape(rows, width)
 
-    first = swapped(mesh_low, "x", True)
-    second = swapped(mesh_low, "x", False)
-    last = swapped(first, "x", False)
+    own = exchange(jnp.broadcast_to(mesh_low, (chips, rows, width)), "x")
+    other = other_core(own)
     gain = norm_gain.reshape(parts, width)
 
     def product(kernel, outs, name, blocks, *args):
@@ -272,14 +231,9 @@
         )(*args)
 
     sums = (state, jax.ShapeDtypeStruct((rows, 3 * width), F32))
-    sent = jax.ShapeDtypeStruct((4 * rows + parts * width, width), BF16)
-    *so_far, sent = product(
-        early_kernel, (*sums, sent), "early", 3, mesh_low, first, second, gain, w_qkv, w_out
-    )
-    arrived = other_core(lax.dynamic_update_slice(sent, last, (3 * rows, 0)))
-    so_far = product(middle_kernel, sums, "middle", 1, last, gain, w_qkv, *so_far)
     kvs = jax.ShapeDtypeStruct((2 * rows, width), BF16)
-    queries, kv = product(late_kernel, (low, kvs), "late", 4, arrived, gain, w_qkv, *so_far)
+    so_far = product(own_half_kernel, sums, "own_half", chips, own, gain, w_qkv)
+    queries, kv = product(other_half_kernel, (low, kvs), "other_half", chips, other, gain, w_qkv, *so_far)
 
     cost = dict(flops=8 * rows * rows * width, transcendentals=2 * rows * rows)
 
@@ -294,23 +248,20 @@
     so_far = call(own_kernel, (state,) * 3, "own", **cost)(queries, kv)
     kv2 = swapped(after(kv0, so_far[0]), "region", False)
     kv3 = swapped(kv1, "region", True)
+    w_other = other_core(after(w_out, so_far[0]))
     so_far = attend(0, kv0, *so_far)
-    so_far = attend(1, kv1, *so_far)
+    so_far = attend(1, kv1, after(so_far[0], w_other), *so_far[1:])
     so_far = attend(2, kv2, *so_far)
     attended = attend(3, kv3, *so_far)
 
-    shared = (attended, other_core(attended), w_out, arrived)
-    flops = 4 * rows * width * width
-    far_share = call(far_share_kernel, low, "far_share", flops=flops)(*shared)
-    relayed = swapped(far_share, "x", False)
-    base, first_share, second_share = call(
-        near_share_kernel, (state, state, low), "near_share", flops=3 * flops
-    )(*shared, mesh_low)
-    from_second = swapped(second_share, "x", False)
-    passed_on = call(add_kernel, low, "add", bytes_accessed=1 << 19)(first_share, relayed)
-    from_first = swapped(passed_on, "x", True)
+    summed = call(
+        share_kernel,
+        jax.ShapeDtypeStruct((chips, rows, width), BF16),
+        "share",
+        flops=4 * rows * width * chips * width,
+    )(attended, other_core(attended), w_out, w_other)
     mesh_slots, mesh_back = call(sum_kernel, (state, low), "sum", bytes_accessed=1 << 20)(
-        base, from_first, from_second
+        mesh_low, exchange(summed, "x")
     )
 
     returned = exchange(mesh_back.reshape(regions, cap, width), "region").reshape(slots, width)

time: 138 us -> 134 us (0.971)
  blocking collectives: 43.8 us -> 67.1 us
  starting transfers between devices: 41.9 us -> 28.2 us
  waiting for transfers between devices: 34 us -> 20.6 us
    all_to_all x1 -> x3, blocking collectives: 43.8 us -> 67.1 us  [exchange(): return lax.all_to_all(array, axis, split_axis=0, concat_axis=0, tiled=True)]
    ppermute x10 -> x4, starting transfers between devices: 29.4 us -> 12.9 us  [swapped(): return lax.ppermute(value, (axis, 'core'), pairs)]
    ppermute x10 -> x4, waiting for transfers between devices: 16.1 us -> 2.99 us  [swapped(): return lax.ppermute(value, (axis, 'core'), pairs)]
    ppermute x2 -> x3, starting transfers between devices: 4.48 us -> 6.03 us  [other_core(): return lax.ppermute(value, 'core', [(0, 1), (1, 0)])]
    pallas_call x12 -> x9, Pallas kernels: 11.3 us -> 10.4 us  [run(): pl.pallas_call(kernel, out_shape=outs, in_specs=[VMEM] * len(args), out_s...]
  transfers between devices with their start and end apart: 13 -> 8, of which waited for: 13 -> 6; matrix products, arithmetic and copies ran while one was open for 1% -> 1% of each run, Pallas kernels for 6% -> 5%
where the time goes in v4:
time: 134 us; the launch traced here: 133 us
  blocking collectives  67.1 us (50%)
  starting transfers between devices  28.2 us (21%)
  waiting for transfers between devices  20.6 us (15%)
  Pallas kernels  10.4 us (8%)
  matrix products  5.39 us (4%)
    all_to_all x3, blocking collectives, exchange(): return lax.all_to_all(array, axis, split_axis=0, concat_axis=0, tiled=True)  67.1 us
    all_to_all x1, waiting for transfers between devices, exchange(): return lax.all_to_all(array, axis, split_axis=0, concat_axis=0, tiled=True)  15.7 us
    ppermute x4, starting transfers between devices, swapped(): return lax.ppermute(value, (axis, 'core'), pairs)  12.9 us
    pallas_call x9, Pallas kernels, run(): pl.pallas_call(kernel, out_shape=outs, in_specs=[VMEM] * len(args), out_s...  10.4 us
    all_to_all x1, starting transfers between devices, exchange(): return lax.all_to_all(array, axis, split_axis=0, concat_axis=0, tiled=True)  9.26 us
    ppermute x3, starting transfers between devices, other_core(): return lax.ppermute(value, 'core', [(0, 1), (1, 0)])  6.03 us
    ppermute x4, waiting for transfers between devices, swapped(): return lax.ppermute(value, (axis, 'core'), pairs)  2.99 us
  transfers between devices with their start and end apart: 8, of which 6 were waited for; matrix products, arithmetic and copies ran while one was open for 1% of the time, Pallas kernels for 5%

profile of v4, /device:TPU:6, one launch (start us, length us, event | category | flops | bytes accessed | tf_op | source)
XLA Modules:
  0.0 132.8 jit_solution(3662760537395792693)
XLA Ops:
  0.6 2.0 %fusion.6 = bf16[512,128]{1,0:T(8,128)(2,1)S(1)} fusion(s32[2048]{0:T(1024)} %param.10, bf16[2048,128]{1,0:T(8,128)(2,1)} %param.8, f32[2048]{0:T(1024)} %param.9), kind=kOutput, calls=%fused_computation.8 | convolution fusion | flops 270336000 | bytes 671744 | tf_op jit(solution)/shard_map/dot_general | solution.py:215
  2.6 43.8 %all_to_all.20 = bf16[128,4,128]{2,1,0:T(4,128)(2,1)S(1)} all-to-all(bf16[128,4,128]{2,1,0:T(4,128)(2,1)S(1)} %bitcast.12), channel_id=1, replica_groups=mesh['region'=128,'x'=4,'core'=2] {'region'}, dimensions={0} | all-to-all | bytes 262144 | tf_op jit(solution)/shard_map/all_to_all | solution.py:19
  46.4 0.1 broadcast_in_dim.2
  46.5 10.7 %all_to_all.21.own_ref = bf16[4,512,128]{2,1,0:T(8,128)(2,1)S(1)} all-to-all(bf16[4,512,128]{2,1,0:T(8,128)(2,1)S(1)} %broadcast_in_dim.2), channel_id=1, replica_groups=mesh['region'=128,'x'=4,'core'=2] {'x'}, dimensions={0} | all-to-all | bytes 1048576 | tf_op jit(solution)/shard_map/all_to_all | solution.py:19
  57.2 1.9 %collective-permute-start = (bf16[4,512,128]{2,1,0:T(8,128)(2,1)S(1)}, bf16[4,512,128]{2,1,0:T(8,128)(2,1)S(1)}, u32[]{:S(2)}, u32[]{:S(2)}) collective-permute-start(bf16[4,512,128]{2,1,0:T(8,128)(2,1)S(1)} %all_to_all.21.own_ref), channel_id=1, source_target_pairs={{0,1},{1,0},{2,3},{3,2},{4,5},{5,4},{6,7},{7,6},{8,9},{9,8},{10,11... | collective-permute-start | bytes 1572872 | tf_op jit(solution)/shard_map/ppermute | solution.py:23
  59.1 1.0 own_half.1
  60.2 0.8 collective-permute-done.other_ref
  61.0 1.0 other_half.1
  62.0 3.0 %collective-permute-start.3 = (bf16[1024,128]{1,0:T(8,128)(2,1)S(1)}, bf16[1024,128]{1,0:T(8,128)(2,1)S(1)}, u32[]{:S(2)}, u32[]{:S(2)}) collective-permute-start(bf16[1024,128]{1,0:T(8,128)(2,1)S(1)} %get-tuple-element.26.kv_ref), channel_id=1, source_target_pairs={{0,8},{1,1017},{8,0},{9,17},{16,24},{17,9},{24,16},{25,33},{32,40}... | collective-permute-start | bytes 786440 | tf_op jit(solution)/shard_map/ppermute | solution.py:34
  65.1 2.4 %collective-permute-start.1 = (bf16[1024,128]{1,0:T(8,128)(2,1)S(1)}, bf16[1024,128]{1,0:T(8,128)(2,1)S(1)}, u32[]{:S(2)}, u32[]{:S(2)}) collective-permute-start(bf16[1024,128]{1,0:T(8,128)(2,1)S(1)} %get-tuple-element.26.kv_ref), channel_id=1, source_target_pairs={{0,1016},{1,9},{8,16},{9,1},{16,8},{17,25},{24,32},{25,17},{32,24}... | collective-permute-start | bytes 786440 | tf_op jit(solution)/shard_map/ppermute | solution.py:34
  67.4 1.2 own.1
  68.6 1.9 %collective-permute-start.5 = (bf16[128,1024]{1,0:T(8,128)(2,1)S(1)}, bf16[128,1024]{1,0:T(8,128)(2,1)S(1)}, u32[]{:S(2)}, u32[]{:S(2)}) collective-permute-start(bf16[128,1024]{1,0:T(8,128)(2,1)S(1)} %copy-done.1), channel_id=1, source_target_pairs={{0,1},{1,0},{2,3},{3,2},{4,5},{5,4},{6,7},{7,6},{8,9},{9,8},{10,11... | collective-permute-start | bytes 786440 | tf_op jit(solution)/shard_map/ppermute | solution.py:23
  70.5 1.2 collective-permute-done.3.refs_2_
  71.7 5.6 %collective-permute-start.4 = (bf16[1024,128]{1,0:T(8,128)(2,1)S(1)}, bf16[1024,128]{1,0:T(8,128)(2,1)S(1)}, u32[]{:S(2)}, u32[]{:S(2)}) collective-permute-start(bf16[1024,128]{1,0:T(8,128)(2,1)S(1)} %collective-permute-done.3.refs_2_), channel_id=1, source_target_pairs={{0,1016},{1,9},{8,16},{9,1},{16,8},{17,25},{24,32},{25,17},{32,24}... | collective-permute-start | bytes 786440 | tf_op jit(solution)/shard_map/ppermute | solution.py:34
  77.4 1.9 %collective-permute-start.2 = (bf16[1024,128]{1,0:T(8,128)(2,1)S(1)}, bf16[1024,128]{1,0:T(8,128)(2,1)S(1)}, u32[]{:S(2)}, u32[]{:S(2)}) collective-permute-start(bf16[1024,128]{1,0:T(8,128)(2,1)S(1)} %collective-permute-done.1.refs_2_), channel_id=1, source_target_pairs={{0,8},{1,1017},{8,0},{9,17},{16,24},{17,9},{24,16},{25,33},{32,40}... | collective-permute-start | bytes 786440 | tf_op jit(solution)/shard_map/ppermute | solution.py:34
  79.3 1.5 %peer0.1 = (f32[512,128]{1,0:T(8,128)S(1)}, f32[512,128]{1,0:T(8,128)S(1)}, f32[512,128]{1,0:T(8,128)S(1)}) custom-call(s32[1,4]{1,0:T(1,128)S(1)} %copy-done.3, bf16[512,128]{1,0:T(8,128)(2,1)S(1)} %get-tuple-element.25.q_ref.refs_1_, bf16[1024,128]{1,0:T(8,128)(2,1)S(1)} %collective-permute-done.3.refs_2_, f32[512,128]{1,0:T(8,128)S(1)} %get-tuple-element.27.refs_3_, ...), custom_call_target="tpu_custom_call" | custom-call | flops 268435456 | tf_op jit(solution)/shard_map/peer0/pallas_call | solution.py:186
  80.8 1.5 %peer1.1 = (f32[512,128]{1,0:T(8,128)S(1)}, f32[512,128]{1,0:T(8,128)S(1)}, f32[512,128]{1,0:T(8,128)S(1)}) custom-call(s32[1,4]{1,0:T(1,128)S(1)} %copy-done.3, bf16[512,128]{1,0:T(8,128)(2,1)S(1)} %get-tuple-element.25.q_ref.refs_1_, bf16[1024,128]{1,0:T(8,128)(2,1)S(1)} %collective-permute-done.1.refs_2_, f32[512,128]{1,0:T(8,128)S(1)} %get-tuple-element.33.refs_3_, ...), custom_call_target="tpu_custom_call" | custom-call | flops 268435456 | tf_op jit(solution)/shard_map/peer1/pallas_call | solution.py:186
  82.3 1.7 %collective-permute-done.4.refs_2_ = bf16[1024,128]{1,0:T(8,128)(2,1)S(1)} collective-permute-done((bf16[1024,128]{1,0:T(8,128)(2,1)S(1)}, bf16[1024,128]{1,0:T(8,128)(2,1)S(1)}, u32[]{:S(2)}, u32[]{:S(2)}) %collective-permute-start.4) | collective-permute-done | bytes 262176 | tf_op jit(solution)/shard_map/ppermute | solution.py:34
  84.0 1.5 %peer2.1 = (f32[512,128]{1,0:T(8,128)S(1)}, f32[512,128]{1,0:T(8,128)S(1)}, f32[512,128]{1,0:T(8,128)S(1)}) custom-call(s32[1,4]{1,0:T(1,128)S(1)} %copy-done.3, bf16[512,128]{1,0:T(8,128)(2,1)S(1)} %get-tuple-element.25.q_ref.refs_1_, bf16[1024,128]{1,0:T(8,128)(2,1)S(1)} %collective-permute-done.4.refs_2_, f32[512,128]{1,0:T(8,128)S(1)} %get-tuple-element.36.refs_3_, ...), custom_call_target="tpu_custom_call" | custom-call | flops 268435456 | tf_op jit(solution)/shard_map/peer2/pallas_call | solution.py:186
  85.5 0.1 collective-permute-done.2.refs_2_
  85.6 1.5 %peer3.1.own_ref = bf16[512,128]{1,0:T(8,128)(2,1)S(1)} custom-call(s32[1,4]{1,0:T(1,128)S(1)} %copy-done.3, bf16[512,128]{1,0:T(8,128)(2,1)S(1)} %get-tuple-element.25.q_ref.refs_1_, bf16[1024,128]{1,0:T(8,128)(2,1)S(1)} %collective-permute-done.2.refs_2_, f32[512,128]{1,0:T(8,128)S(1)} %get-tuple-element.39.refs_3_, ...), custom_call_target="tpu_custom_call" | custom-call | flops 268435456 | tf_op jit(solution)/shard_map/peer3/pallas_call | solution.py:186
  87.1 2.2 %collective-permute-start.6 = (bf16[512,128]{1,0:T(8,128)(2,1)S(1)}, bf16[512,128]{1,0:T(8,128)(2,1)S(1)}, u32[]{:S(2)}, u32[]{:S(2)}) collective-permute-start(bf16[512,128]{1,0:T(8,128)(2,1)S(1)} %peer3.1.own_ref), channel_id=1, source_target_pairs={{0,1},{1,0},{2,3},{3,2},{4,5},{5,4},{6,7},{7,6},{8,9},{9,8},{10,11... | collective-permute-start | bytes 393224 | tf_op jit(solution)/shard_map/ppermute | solution.py:23
  89.3 1.0 collective-permute-done.6.other_ref
  90.4 0.4 share.1
  90.8 12.6 %all_to_all.22.parts_ref = bf16[4,512,128]{2,1,0:T(8,128)(2,1)S(1)} all-to-all(bf16[4,512,128]{2,1,0:T(8,128)(2,1)S(1)} %share.1), channel_id=1, replica_groups=mesh['region'=128,'x'=4,'core'=2] {'x'}, dimensions={0} | all-to-all | bytes 1048576 | tf_op jit(solution)/shard_map/all_to_all | solution.py:19
  103.5 0.7 sum.1
  104.2 9.3 %all-to-all-start.3 = ((bf16[128,4,128]{2,1,0:T(4,128)(2,1)}), bf16[128,4,128]{2,1,0:T(4,128)(2,1)S(1)}, u32[]{:S(2)}, u32[]{:S(2)}) async-start(bf16[128,4,128]{2,1,0:T(4,128)(2,1)} %bitcast.3), calls=%async_computation.3 | async-start | bytes 262144 | tf_op jit(solution)/shard_map/all_to_all | solution.py:19
  113.5 0.1 copy.10
  113.6 0.1 eq.29
  113.7 1.3 fusion.8
  115.0 15.7 %all-to-all-done.3 = bf16[128,4,128]{2,1,0:T(4,128)(2,1)S(1)} async-done(((bf16[128,4,128]{2,1,0:T(4,128)(2,1)}), bf16[128,4,128]{2,1,0:T(4,128)(2,1)S(1)}, u32[]{:S(2)}, u32[]{:S(2)}) %all-to-all-start.3) | async-done | bytes 131104 | tf_op jit(solution)/shard_map/all_to_all | solution.py:19
  130.7 2.1 %fusion.3 = bf16[2048,128]{1,0:T(8,128)(2,1)} fusion(bf16[512,128]{1,0:T(8,128)(2,1)S(1)} %bitcast.11, s32[2048]{0:T(1024)S(1)} %copy-done.6, bf16[2048,128]{1,0:T(8,128)(2,1)S(1)} %copy-done.5), kind=kOutput, calls=%fused_computation.4 | convolution fusion | flops 270270464 | bytes 1187840 | tf_op jit(solution)/shard_map/dot_general | solution.py:273
  (16 shorter events, 0.0 us)
Async XLA Ops:
  46.4 12.7 %copy-start = (bf16[3,1024,128]{2,1,0:T(8,128)(2,1)S(1)}, bf16[3,1024,128]{2,1,0:T(8,128)(2,1)}, u32[]{:S(2)}) copy-start(bf16[3,1024,128]{2,1,0:T(8,128)(2,1)} %w_ref.3) | copy-start | bytes 2359300
  46.4 12.7 %copy-start.2 = (f32[1024]{0:T(1024)S(1)}, f32[1024]{0:T(1024)}, u32[]{:S(2)}) copy-start(f32[1024]{0:T(1024)} %param.13) | copy-start | bytes 12292
  57.2 3.8 %collective-permute-start = (bf16[4,512,128]{2,1,0:T(8,128)(2,1)S(1)}, bf16[4,512,128]{2,1,0:T(8,128)(2,1)S(1)}, u32[]{:S(2)}, u32[]{:S(2)}) collective-permute-start(bf16[4,512,128]{2,1,0:T(8,128)(2,1)S(1)} %all_to_all.21.own_ref), channel_id=1, source_target_pairs={{0,1},{1,0},{2,3},{3,2},{4,5},{5,4},{6,7},{7,6},{8,9},{9,8},{10,11... | collective-permute-start | bytes 1572872 | tf_op jit(solution)/shard_map/ppermute | solution.py:23
  62.0 6.6 %copy-start.1 = (bf16[128,1024]{1,0:T(8,128)(2,1)S(1)}, bf16[128,1024]{1,0:T(8,128)(2,1)}, u32[]{:S(2)}) copy-start(bf16[128,1024]{1,0:T(8,128)(2,1)} %w_own_ref.1) | copy-start | bytes 786436
  62.0 17.3 %copy-start.3 = (s32[1,4]{1,0:T(1,128)S(1)}, s32[1,4]{1,0:T(1,128)}, u32[]{:S(2)}) copy-start(s32[1,4]{1,0:T(1,128)} %refs_0_.7) | copy-start | bytes 52
  62.0 9.7 %collective-permute-start.3 = (bf16[1024,128]{1,0:T(8,128)(2,1)S(1)}, bf16[1024,128]{1,0:T(8,128)(2,1)S(1)}, u32[]{:S(2)}, u32[]{:S(2)}) collective-permute-start(bf16[1024,128]{1,0:T(8,128)(2,1)S(1)} %get-tuple-element.26.kv_ref), channel_id=1, source_target_pairs={{0,8},{1,1017},{8,0},{9,17},{16,24},{17,9},{24,16},{25,33},{32,40}... | collective-permute-start | bytes 786440 | tf_op jit(solution)/shard_map/ppermute | solution.py:34
  65.1 12.3 %collective-permute-start.1 = (bf16[1024,128]{1,0:T(8,128)(2,1)S(1)}, bf16[1024,128]{1,0:T(8,128)(2,1)S(1)}, u32[]{:S(2)}, u32[]{:S(2)}) collective-permute-start(bf16[1024,128]{1,0:T(8,128)(2,1)S(1)} %get-tuple-element.26.kv_ref), channel_id=1, source_target_pairs={{0,1016},{1,9},{8,16},{9,1},{16,8},{17,25},{24,32},{25,17},{32,24}... | collective-permute-start | bytes 786440 | tf_op jit(solution)/shard_map/ppermute | solution.py:34
  68.6 12.2 %collective-permute-start.5 = (bf16[128,1024]{1,0:T(8,128)(2,1)S(1)}, bf16[128,1024]{1,0:T(8,128)(2,1)S(1)}, u32[]{:S(2)}, u32[]{:S(2)}) collective-permute-start(bf16[128,1024]{1,0:T(8,128)(2,1)S(1)} %copy-done.1), channel_id=1, source_target_pairs={{0,1},{1,0},{2,3},{3,2},{4,5},{5,4},{6,7},{7,6},{8,9},{9,8},{10,11... | collective-permute-start | bytes 786440 | tf_op jit(solution)/shard_map/ppermute | solution.py:23
  71.7 12.3 %collective-permute-start.4 = (bf16[1024,128]{1,0:T(8,128)(2,1)S(1)}, bf16[1024,128]{1,0:T(8,128)(2,1)S(1)}, u32[]{:S(2)}, u32[]{:S(2)}) collective-permute-start(bf16[1024,128]{1,0:T(8,128)(2,1)S(1)} %collective-permute-done.3.refs_2_), channel_id=1, source_target_pairs={{0,1016},{1,9},{8,16},{9,1},{16,8},{17,25},{24,32},{25,17},{32,24}... | collective-permute-start | bytes 786440 | tf_op jit(solution)/shard_map/ppermute | solution.py:34
  77.4 8.3 %collective-permute-start.2 = (bf16[1024,128]{1,0:T(8,128)(2,1)S(1)}, bf16[1024,128]{1,0:T(8,128)(2,1)S(1)}, u32[]{:S(2)}, u32[]{:S(2)}) collective-permute-start(bf16[1024,128]{1,0:T(8,128)(2,1)S(1)} %collective-permute-done.1.refs_2_), channel_id=1, source_target_pairs={{0,8},{1,1017},{8,0},{9,17},{16,24},{17,9},{24,16},{25,33},{32,40}... | collective-permute-start | bytes 786440 | tf_op jit(solution)/shard_map/ppermute | solution.py:34
  87.1 3.2 %collective-permute-start.6 = (bf16[512,128]{1,0:T(8,128)(2,1)S(1)}, bf16[512,128]{1,0:T(8,128)(2,1)S(1)}, u32[]{:S(2)}, u32[]{:S(2)}) collective-permute-start(bf16[512,128]{1,0:T(8,128)(2,1)S(1)} %peer3.1.own_ref), channel_id=1, source_target_pairs={{0,1},{1,0},{2,3},{3,2},{4,5},{5,4},{6,7},{7,6},{8,9},{9,8},{10,11... | collective-permute-start | bytes 393224 | tf_op jit(solution)/shard_map/ppermute | solution.py:23
  90.8 22.6 %copy-start.4 = (s32[1,128,4]{1,2,0:T(4,128)S(1)}, s32[1,128,4]{1,2,0:T(4,128)}, u32[]{:S(2)}) copy-start(s32[1,128,4]{1,2,0:T(4,128)} %param.11) | copy-start | bytes 6148
  103.4 27.3 %copy-start.5 = (bf16[2048,128]{1,0:T(8,128)(2,1)S(1)}, bf16[2048,128]{1,0:T(8,128)(2,1)}, u32[]{:S(2)}) copy-start(bf16[2048,128]{1,0:T(8,128)(2,1)} %param.8) | copy-start | bytes 1572868
  103.4 27.3 %copy-start.6 = (s32[2048]{0:T(1024)S(1)}, s32[2048]{0:T(1024)}, u32[]{:S(2)}) copy-start(s32[2048]{0:T(1024)} %param.10) | copy-start | bytes 24580
  104.2 26.5 %all-to-all-start.3 = ((bf16[128,4,128]{2,1,0:T(4,128)(2,1)}), bf16[128,4,128]{2,1,0:T(4,128)(2,1)S(1)}, u32[]{:S(2)}, u32[]{:S(2)}) async-start(bf16[128,4,128]{2,1,0:T(4,128)(2,1)} %bitcast.3), calls=%async_computation.3 | async-start | bytes 262144 | tf_op jit(solution)/shard_map/all_to_all | solution.py:19

commit v5 on v4

--- a/solution.py
+++ b/solution.py
@@ -38,12 +38,12 @@
     return lax.optimization_barrier((value, *earlier))[0]
 
 
-def block_product(blocks, gain_ref, w_ref, scaled_ref, rows_ref, put):
+def block_product(blocks, thirds, gain_ref, w_ref, scaled_ref, rows_ref, put):
     rows, width = blocks[0][0].shape
     for i, (_, index) in enumerate(blocks):
         source = pl.ds(pl.multiple_of(index * width, width), width)
-        for third in range(3):
-            columns = slice(third * width, (third + 1) * width)
+        for at, third in enumerate(thirds):
+            columns = slice(at * width, (at + 1) * width)
             rows_ref[i * width : (i + 1) * width, columns] = w_ref[third, source, :]
 
     def step(number, _):
@@ -68,24 +68,39 @@
         product_ref[at, :] = product
 
     blocks = [(own_ref.at[chip], 2 * chip + core) for chip in range(own_ref.shape[0])]
-    block_product(blocks, gain_ref, w_ref, *scratch, put)
-
-
-def other_half_kernel(other_ref, gain_ref, w_ref, square0_ref, product0_ref, q_ref, kv_ref, *scratch):
+    block_product(blocks, (0, 1, 2), gain_ref, w_ref, *scratch, put)
+
+
+def finish(thirds, other_ref, gain_ref, w_ref, square0_ref, product0_ref, scratch, put):
     core = lax.axis_index("core")
-    rows, width = q_ref.shape
+    width = gain_ref.shape[1]
     features = gain_ref.shape[0] * width
-
-    def put(at, square, product):
+    columns = slice(thirds[0] * width, (thirds[-1] + 1) * width)
+
+    def add(at, square, product):
         mean = jnp.sum(square0_ref[at, :] + square, axis=-1, keepdims=True) / features
         factor = lax.rsqrt(mean + 1e-05)
-        whole = ((product0_ref[at, :] + product) * factor).astype(BF16)
-        q_ref[at, :] = whole[:, :width]
-        kv_ref[at, :] = whole[:, width : 2 * width]
-        kv_ref[pl.ds(pl.multiple_of(rows + at.start, CHUNK), CHUNK), :] = whole[:, 2 * width :]
+        put(at, ((product0_ref[at, columns] + product) * factor).astype(BF16))
 
     blocks = [(other_ref.at[chip], 2 * chip + 1 - core) for chip in range(other_ref.shape[0])]
-    block_product(blocks, gain_ref, w_ref, *scratch, put)
+    block_product(blocks, thirds, gain_ref, w_ref, *scratch, add)
+
+
+def kv_kernel(other_ref, gain_ref, w_ref, square0_ref, product0_ref, kv_ref, *scratch):
+    rows, width = square0_ref.shape
+
+    def put(at, both):
+        kv_ref[at, :] = both[:, :width]
+        kv_ref[pl.ds(pl.multiple_of(rows + at.start, CHUNK), CHUNK), :] = both[:, width:]
+
+    finish((1, 2), other_ref, gain_ref, w_ref, square0_ref, product0_ref, scratch, put)
+
+
+def q_kernel(other_ref, gain_ref, w_ref, square0_ref, product0_ref, q_ref, *scratch):
+    def put(at, queries):
+        q_ref[at, :] = queries
+
+    finish((0,), other_ref, gain_ref, w_ref, square0_ref, product0_ref, scratch, put)
 
 
 def attend_block(q_ref, kv_ref, seen, before, put):
@@ -181,6 +196,24 @@
     back_ref[...] = total.astype(BF16)
 
 
+def down(row):
+    return jnp.broadcast_to(row, (row.shape[1], row.shape[1])).T
+
+
+def decode_kernel(slot_ref, returned_ref, grid_ref, out_ref):
+    step = pl.program_id(0)
+    points, lanes = grid_ref.shape
+    slots = returned_ref.shape[0]
+    pieces = points // lanes
+    for i in range(pieces):
+        slot = down(slot_ref[pl.ds(step * pieces + i, 1), :])
+        number = lax.broadcasted_iota(jnp.int32, (lanes, slots), 1)
+        hot = jnp.where(number == jnp.concatenate([slot] * (slots // lanes), axis=1), 1.0, 0.0)
+        rows = slice(i * lanes, (i + 1) * lanes)
+        back = jnp.dot(hot.astype(BF16), returned_ref[...], preferred_element_type=F32)
+        out_ref[rows, :] = (grid_ref[rows, :].astype(F32) + back).astype(BF16)
+
+
 def call(kernel, outs, name, scratch=(), flops=0, bytes_accessed=0, transcendentals=0):
     def run(*args):
         return pl.pallas_call(
@@ -210,30 +243,38 @@
     low = jax.ShapeDtypeStruct((rows, width), BF16)
     state = jax.ShapeDtypeStruct((rows, width), F32)
 
+    points = grid.shape[0]
+    by_lane = pl.BlockSpec((points // width, width), lambda i: (0, 0))
+    by_slot = pl.BlockSpec((slots, width), lambda i: (0, 0))
+    by_step = pl.BlockSpec((points // 4, width), lambda i: (i, 0))
+    slot_rows = g2m_slot.reshape(-1, width)
     scaled = (g2m_weight[:, None] * grid.astype(F32)).astype(BF16)
     slot_hot = (g2m_slot[None, :] == jnp.arange(slots, dtype=jnp.int32)[:, None]).astype(BF16)
     partial_value = jnp.dot(slot_hot, scaled, preferred_element_type=F32).astype(BF16)
+    w_other = other_core(w_out)
     mesh_low = exchange(partial_value.reshape(regions, cap, width), "region").reshape(rows, width)
 
+    mesh_low = after(mesh_low, w_other)
     own = exchange(jnp.broadcast_to(mesh_low, (chips, rows, width)), "x")
     other = other_core(own)
     gain = norm_gain.reshape(parts, width)
 
-    def product(kernel, outs, name, blocks, *args):
-        depth = blocks * width
+    def product(kernel, outs, name, thirds, *args):
+        depth = chips * width
         return call(
             kernel,
             outs,
             name,
-            scratch=[pltpu.VMEM((CHUNK, depth), BF16), pltpu.VMEM((depth, 3 * width), BF16)],
-            flops=6 * rows * depth * width,
+            scratch=[pltpu.VMEM((CHUNK, depth), BF16), pltpu.VMEM((depth, thirds * width), BF16)],
+            flops=2 * thirds * rows * depth * width,
             bytes_accessed=2 << 20,
         )(*args)
 
     sums = (state, jax.ShapeDtypeStruct((rows, 3 * width), F32))
     kvs = jax.ShapeDtypeStruct((2 * rows, width), BF16)
-    so_far = product(own_half_kernel, sums, "own_half", chips, own, gain, w_qkv)
-    queries, kv = product(other_half_kernel, (low, kvs), "other_half", chips, other, gain, w_qkv, *so_far)
+    so_far = product(own_half_kernel, sums, "own_half", 3, own, gain, w_qkv)
+    kv = product(kv_kernel, kvs, "kv", 2, other, gain, w_qkv, *so_far)
+    queries = product(q_kernel, low, "q", 1, other, gain, w_qkv, *so_far)
 
     cost = dict(flops=8 * rows * rows * width, transcendentals=2 * rows * rows)
 
@@ -248,9 +289,8 @@
     so_far = call(own_kernel, (state,) * 3, "own", **cost)(queries, kv)
     kv2 = swapped(after(kv0, so_far[0]), "region", False)
     kv3 = swapped(kv1, "region", True)
-    w_other = other_core(after(w_out, so_far[0]))
     so_far = attend(0, kv0, *so_far)
-    so_far = attend(1, kv1, after(so_far[0], w_other), *so_far[1:])
+    so_far = attend(1, kv1, *so_far)
     so_far = attend(2, kv2, *so_far)
     attended = attend(3, kv3, *so_far)
 
@@ -270,8 +310,15 @@
     mesh_state = jnp.dot(
         node_hot, mesh_slots, precision=lax.Precision.HIGHEST, preferred_element_type=F32
     )
-    gathered = jnp.dot(slot_hot.T, returned, preferred_element_type=F32)
-    grid_out = (grid.astype(F32) + gathered).astype(BF16)
+    grid_out = pl.pallas_call(
+        decode_kernel,
+        grid=(4,),
+        out_shape=jax.ShapeDtypeStruct(grid.shape, BF16),
+        in_specs=[by_lane, by_slot, by_step],
+        out_specs=by_step,
+        compiler_params=PARAMS,
+        name="decode",
+    )(slot_rows, returned, grid)
     return (mesh_state, grid_out)
 
 

time: 134 us -> 134 us (level)
  blocking collectives: 67.1 us -> 23.4 us
  starting transfers between devices: 28.2 us -> 51.8 us
  waiting for transfers between devices: 20.6 us -> 38.9 us
  Pallas kernels: 10.4 us -> 13.3 us
  matrix products: 5.39 us -> 4.01 us
    all_to_all x3 -> x2, blocking collectives: 67.1 us -> 23.4 us  [exchange(): return lax.all_to_all(array, axis, split_axis=0, concat_axis=0, tiled=True)]
    all_to_all x1 -> x2, starting transfers between devices: 9.26 us -> 34.3 us  [exchange(): return lax.all_to_all(array, axis, split_axis=0, concat_axis=0, tiled=True)]
    all_to_all x1 -> x2, waiting for transfers between devices: 15.7 us -> 30.1 us  [exchange(): return lax.all_to_all(array, axis, split_axis=0, concat_axis=0, tiled=True)]
    ppermute x4, waiting for transfers between devices: 2.99 us -> 5.48 us  [swapped(): return lax.ppermute(value, (axis, 'core'), pairs)]
    pallas_call x0 -> x1, Pallas kernels: none -> 2.36 us  [on_device(): pl.pallas_call(decode_kernel, grid=(4,), out_shape=jax.ShapeDtypeStruct(g...]
    dot_general x1 -> x0, matrix products: 2.09 us -> none  [on_device(): gathered = jnp.dot(slot_hot.T, returned, preferred_element_type=F32)]
    ppermute x4, starting transfers between devices: 12.9 us -> 11.4 us  [swapped(): return lax.ppermute(value, (axis, 'core'), pairs)]
    ppermute x3, waiting for transfers between devices: 1.89 us -> 3.34 us  [other_core(): return lax.ppermute(value, 'core', [(0, 1), (1, 0)])]
  transfers between devices with their start and end apart: 8 -> 9, of which waited for: 6 -> 8; matrix products, arithmetic and copies ran while one was open for 1% -> 1% of each run, Pallas kernels for 5% -> 6%
where the time goes in v5:
time: 134 us; the launch traced here: 133 us
  starting transfers between devices  51.8 us (39%)
  waiting for transfers between devices  38.9 us (29%)
  blocking collectives  23.4 us (17%)
  Pallas kernels  13.3 us (10%)
  matrix products  4.01 us (3%)
    all_to_all x2, starting transfers between devices, exchange(): return lax.all_to_all(array, axis, split_axis=0, concat_axis=0, tiled=True)  34.3 us
    all_to_all x2, waiting for transfers between devices, exchange(): return lax.all_to_all(array, axis, split_axis=0, concat_axis=0, tiled=True)  30.1 us
    all_to_all x2, blocking collectives, exchange(): return lax.all_to_all(array, axis, split_axis=0, concat_axis=0, tiled=True)  23.4 us
    ppermute x4, starting transfers between devices, swapped(): return lax.ppermute(value, (axis, 'core'), pairs)  11.4 us
    pallas_call x10, Pallas kernels, run(): pl.pallas_call(kernel, out_shape=outs, in_specs=[VMEM] * len(args), out_s...  11 us
    ppermute x3, starting transfers between devices, other_core(): return lax.ppermute(value, 'core', [(0, 1), (1, 0)])  6.07 us
    ppermute x4, waiting for transfers between devices, swapped(): return lax.ppermute(value, (axis, 'core'), pairs)  5.48 us
    ppermute x3, waiting for transfers between devices, other_core(): return lax.ppermute(value, 'core', [(0, 1), (1, 0)])  3.34 us
  transfers between devices with their start and end apart: 9, of which 8 were waited for; matrix products, arithmetic and copies ran while one was open for 1% of the time, Pallas kernels for 6%

profile of v5, /device:TPU:6, one launch (start us, length us, event | category | flops | bytes accessed | tf_op | source)
XLA Modules:
  0.0 132.5 jit_solution(2226936611694728680)
XLA Ops:
  0.6 2.7 %fusion.2 = bf16[512,128]{1,0:T(8,128)(2,1)} fusion(s32[2048]{0:T(1024)} %param.10, bf16[2048,128]{1,0:T(8,128)(2,1)} %grid_ref.1, f32[2048]{0:T(1024)} %param.9), kind=kOutput, calls=%fused_computation.3 | convolution fusion | flops 270336000 | bytes 671744 | tf_op jit(solution)/shard_map/dot_general | solution.py:253
  3.3 26.3 %all-to-all-start = ((bf16[128,4,128]{2,1,0:T(4,128)(2,1)}), bf16[128,4,128]{2,1,0:T(4,128)(2,1)S(1)}, u32[]{:S(2)}, u32[]{:S(2)}) async-start(bf16[128,4,128]{2,1,0:T(4,128)(2,1)} %bitcast), calls=%async_computation | async-start | bytes 262144 | tf_op jit(solution)/shard_map/all_to_all | solution.py:19
  29.6 1.9 %collective-permute-start = (bf16[128,1024]{1,0:T(8,128)(2,1)S(1)}, bf16[128,1024]{1,0:T(8,128)(2,1)S(1)}, u32[]{:S(2)}, u32[]{:S(2)}) collective-permute-start(bf16[128,1024]{1,0:T(8,128)(2,1)S(1)} %copy-done.2), channel_id=1, source_target_pairs={{0,1},{1,0},{2,3},{3,2},{4,5},{5,4},{6,7},{7,6},{8,9},{9,8},{10,11... | collective-permute-start | bytes 786440 | tf_op jit(solution)/shard_map/ppermute | solution.py:23
  31.5 1.5 %collective-permute-done.w_other_ref = bf16[128,1024]{1,0:T(8,128)(2,1)S(1)} collective-permute-done((bf16[128,1024]{1,0:T(8,128)(2,1)S(1)}, bf16[128,1024]{1,0:T(8,128)(2,1)S(1)}, u32[]{:S(2)}, u32[]{:S(2)}) %collective-permute-start) | collective-permute-done | bytes 262176 | tf_op jit(solution)/shard_map/ppermute | solution.py:23
  33.0 14.3 %all-to-all-done = bf16[128,4,128]{2,1,0:T(4,128)(2,1)S(1)} async-done(((bf16[128,4,128]{2,1,0:T(4,128)(2,1)}), bf16[128,4,128]{2,1,0:T(4,128)(2,1)S(1)}, u32[]{:S(2)}, u32[]{:S(2)}) %all-to-all-start) | async-done | bytes 131104 | tf_op jit(solution)/shard_map/all_to_all | solution.py:19
  47.4 10.7 %all_to_all.20.own_ref = bf16[4,512,128]{2,1,0:T(8,128)(2,1)S(1)} all-to-all(bf16[4,512,128]{2,1,0:T(8,128)(2,1)S(1)} %broadcast_in_dim.2), channel_id=1, replica_groups=mesh['region'=128,'x'=4,'core'=2] {'x'}, dimensions={0} | all-to-all | bytes 1048576 | tf_op jit(solution)/shard_map/all_to_all | solution.py:19
  58.2 1.9 %collective-permute-start.1 = (bf16[4,512,128]{2,1,0:T(8,128)(2,1)S(1)}, bf16[4,512,128]{2,1,0:T(8,128)(2,1)S(1)}, u32[]{:S(2)}, u32[]{:S(2)}) collective-permute-start(bf16[4,512,128]{2,1,0:T(8,128)(2,1)S(1)} %all_to_all.20.own_ref), channel_id=1, source_target_pairs={{0,1},{1,0},{2,3},{3,2},{4,5},{5,4},{6,7},{7,6},{8,9},{9,8},{10,11... | collective-permute-start | bytes 1572872 | tf_op jit(solution)/shard_map/ppermute | solution.py:23
  60.1 1.0 own_half.1
  61.1 0.8 collective-permute-done.1.other_ref
  61.9 0.9 kv.1.kv_ref
  62.8 2.8 %collective-permute-start.4 = (bf16[1024,128]{1,0:T(8,128)(2,1)S(1)}, bf16[1024,128]{1,0:T(8,128)(2,1)S(1)}, u32[]{:S(2)}, u32[]{:S(2)}) collective-permute-start(bf16[1024,128]{1,0:T(8,128)(2,1)S(1)} %kv.1.kv_ref), channel_id=1, source_target_pairs={{0,8},{1,1017},{8,0},{9,17},{16,24},{17,9},{24,16},{25,33},{32,40}... | collective-permute-start | bytes 786440 | tf_op jit(solution)/shard_map/ppermute | solution.py:34
  65.6 2.3 %collective-permute-start.2 = (bf16[1024,128]{1,0:T(8,128)(2,1)S(1)}, bf16[1024,128]{1,0:T(8,128)(2,1)S(1)}, u32[]{:S(2)}, u32[]{:S(2)}) collective-permute-start(bf16[1024,128]{1,0:T(8,128)(2,1)S(1)} %kv.1.kv_ref), channel_id=1, source_target_pairs={{0,1016},{1,9},{8,16},{9,1},{16,8},{17,25},{24,32},{25,17},{32,24}... | collective-permute-start | bytes 786440 | tf_op jit(solution)/shard_map/ppermute | solution.py:34
  68.0 0.8 q.1.q_ref.refs_1_
  68.8 1.2 own.1
  69.9 2.5 %collective-permute-done.4.refs_2_ = bf16[1024,128]{1,0:T(8,128)(2,1)S(1)} collective-permute-done((bf16[1024,128]{1,0:T(8,128)(2,1)S(1)}, bf16[1024,128]{1,0:T(8,128)(2,1)S(1)}, u32[]{:S(2)}, u32[]{:S(2)}) %collective-permute-start.4) | collective-permute-done | bytes 262176 | tf_op jit(solution)/shard_map/ppermute | solution.py:34
  72.4 4.4 %collective-permute-start.5 = (bf16[1024,128]{1,0:T(8,128)(2,1)S(1)}, bf16[1024,128]{1,0:T(8,128)(2,1)S(1)}, u32[]{:S(2)}, u32[]{:S(2)}) collective-permute-start(bf16[1024,128]{1,0:T(8,128)(2,1)S(1)} %collective-permute-done.4.refs_2_), channel_id=1, source_target_pairs={{0,1016},{1,9},{8,16},{9,1},{16,8},{17,25},{24,32},{25,17},{32,24}... | collective-permute-start | bytes 786440 | tf_op jit(solution)/shard_map/ppermute | solution.py:34
  76.8 0.4 collective-permute-done.2.refs_2_
  77.2 1.9 %collective-permute-start.3 = (bf16[1024,128]{1,0:T(8,128)(2,1)S(1)}, bf16[1024,128]{1,0:T(8,128)(2,1)S(1)}, u32[]{:S(2)}, u32[]{:S(2)}) collective-permute-start(bf16[1024,128]{1,0:T(8,128)(2,1)S(1)} %collective-permute-done.2.refs_2_), channel_id=1, source_target_pairs={{0,8},{1,1017},{8,0},{9,17},{16,24},{17,9},{24,16},{25,33},{32,40}... | collective-permute-start | bytes 786440 | tf_op jit(solution)/shard_map/ppermute | solution.py:34
  79.2 1.5 %peer0.1 = (f32[512,128]{1,0:T(8,128)S(1)}, f32[512,128]{1,0:T(8,128)S(1)}, f32[512,128]{1,0:T(8,128)S(1)}) custom-call(s32[1,4]{1,0:T(1,128)S(1)} %copy-done.5, bf16[512,128]{1,0:T(8,128)(2,1)S(1)} %q.1.q_ref.refs_1_, bf16[1024,128]{1,0:T(8,128)(2,1)S(1)} %collective-permute-done.4.refs_2_, f32[512,128]{1,0:T(8,128)S(1)} %get-tuple-element.23.refs_3_, ...), custom_call_target="tpu_custom_call" | custom-call | flops 268435456 | tf_op jit(solution)/shard_map/peer0/pallas_call | solution.py:219
  80.7 1.5 %peer1.1 = (f32[512,128]{1,0:T(8,128)S(1)}, f32[512,128]{1,0:T(8,128)S(1)}, f32[512,128]{1,0:T(8,128)S(1)}) custom-call(s32[1,4]{1,0:T(1,128)S(1)} %copy-done.5, bf16[512,128]{1,0:T(8,128)(2,1)S(1)} %q.1.q_ref.refs_1_, bf16[1024,128]{1,0:T(8,128)(2,1)S(1)} %collective-permute-done.2.refs_2_, f32[512,128]{1,0:T(8,128)S(1)} %get-tuple-element.27.refs_3_, ...), custom_call_target="tpu_custom_call" | custom-call | flops 268435456 | tf_op jit(solution)/shard_map/peer1/pallas_call | solution.py:219
  82.2 2.6 %collective-permute-done.5.refs_2_ = bf16[1024,128]{1,0:T(8,128)(2,1)S(1)} collective-permute-done((bf16[1024,128]{1,0:T(8,128)(2,1)S(1)}, bf16[1024,128]{1,0:T(8,128)(2,1)S(1)}, u32[]{:S(2)}, u32[]{:S(2)}) %collective-permute-start.5) | collective-permute-done | bytes 262176 | tf_op jit(solution)/shard_map/ppermute | solution.py:34
  84.7 1.5 %peer2.1 = (f32[512,128]{1,0:T(8,128)S(1)}, f32[512,128]{1,0:T(8,128)S(1)}, f32[512,128]{1,0:T(8,128)S(1)}) custom-call(s32[1,4]{1,0:T(1,128)S(1)} %copy-done.5, bf16[512,128]{1,0:T(8,128)(2,1)S(1)} %q.1.q_ref.refs_1_, bf16[1024,128]{1,0:T(8,128)(2,1)S(1)} %collective-permute-done.5.refs_2_, f32[512,128]{1,0:T(8,128)S(1)} %get-tuple-element.30.refs_3_, ...), custom_call_target="tpu_custom_call" | custom-call | flops 268435456 | tf_op jit(solution)/shard_map/peer2/pallas_call | solution.py:219
  86.3 1.5 %peer3.1.own_ref = bf16[512,128]{1,0:T(8,128)(2,1)S(1)} custom-call(s32[1,4]{1,0:T(1,128)S(1)} %copy-done.5, bf16[512,128]{1,0:T(8,128)(2,1)S(1)} %q.1.q_ref.refs_1_, bf16[1024,128]{1,0:T(8,128)(2,1)S(1)} %collective-permute-done.3.refs_2_, f32[512,128]{1,0:T(8,128)S(1)} %get-tuple-element.33.refs_3_, f32[512,128]{1,0:T(8,128)S(1)} %get-tuple-element.34.refs_4_, ...), custom_call_target="tpu_custom_call" | custom-call | flops 268435456 | tf_op jit(solution)/shard_map/peer3/pallas_call | solution.py:219
  87.8 2.2 %collective-permute-start.6 = (bf16[512,128]{1,0:T(8,128)(2,1)S(1)}, bf16[512,128]{1,0:T(8,128)(2,1)S(1)}, u32[]{:S(2)}, u32[]{:S(2)}) collective-permute-start(bf16[512,128]{1,0:T(8,128)(2,1)S(1)} %peer3.1.own_ref), channel_id=1, source_target_pairs={{0,1},{1,0},{2,3},{3,2},{4,5},{5,4},{6,7},{7,6},{8,9},{9,8},{10,11... | collective-permute-start | bytes 393224 | tf_op jit(solution)/shard_map/ppermute | solution.py:23
  90.0 1.0 collective-permute-done.6.other_ref
  91.0 0.4 share.1
  91.5 12.7 %all_to_all.21.parts_ref = bf16[4,512,128]{2,1,0:T(8,128)(2,1)S(1)} all-to-all(bf16[4,512,128]{2,1,0:T(8,128)(2,1)S(1)} %share.1), channel_id=1, replica_groups=mesh['region'=128,'x'=4,'core'=2] {'x'}, dimensions={0} | all-to-all | bytes 1048576 | tf_op jit(solution)/shard_map/all_to_all | solution.py:19
  104.1 0.7 sum.1
  104.9 8.0 %all-to-all-start.3 = ((bf16[128,4,128]{2,1,0:T(4,128)(2,1)}), bf16[128,4,128]{2,1,0:T(4,128)(2,1)S(1)}, u32[]{:S(2)}, u32[]{:S(2)}) async-start(bf16[128,4,128]{2,1,0:T(4,128)(2,1)} %bitcast.4), calls=%async_computation.3 | async-start | bytes 262144 | tf_op jit(solution)/shard_map/all_to_all | solution.py:19
  113.1 1.3 fusion.3
  114.4 15.7 %all-to-all-done.3 = bf16[128,4,128]{2,1,0:T(4,128)(2,1)S(1)} async-done(((bf16[128,4,128]{2,1,0:T(4,128)(2,1)}), bf16[128,4,128]{2,1,0:T(4,128)(2,1)S(1)}, u32[]{:S(2)}, u32[]{:S(2)}) %all-to-all-start.3) | async-done | bytes 131104 | tf_op jit(solution)/shard_map/all_to_all | solution.py:19
  130.2 2.4 %decode.1 = bf16[2048,128]{1,0:T(8,128)(2,1)} custom-call(s32[16,128]{1,0:T(8,128)S(1)} %bitcast.13, bf16[512,128]{1,0:T(8,128)(2,1)S(1)} %bitcast.9, bf16[2048,128]{1,0:T(8,128)(2,1)S(1)} %copy-done.1), custom_call_target="tpu_custom_call" | custom-call | tf_op jit(solution)/shard_map/decode/pallas_call | solution.py:313
  (18 shorter events, 0.3 us)
Async XLA Ops:
  0.6 29.0 %copy-start.2 = (bf16[128,1024]{1,0:T(8,128)(2,1)S(1)}, bf16[128,1024]{1,0:T(8,128)(2,1)}, u32[]{:S(2)}) copy-start(bf16[128,1024]{1,0:T(8,128)(2,1)} %w_own_ref.1) | copy-start | bytes 786436
  3.3 44.0 %all-to-all-start = ((bf16[128,4,128]{2,1,0:T(4,128)(2,1)}), bf16[128,4,128]{2,1,0:T(4,128)(2,1)S(1)}, u32[]{:S(2)}, u32[]{:S(2)}) async-start(bf16[128,4,128]{2,1,0:T(4,128)(2,1)} %bitcast), calls=%async_computation | async-start | bytes 262144 | tf_op jit(solution)/shard_map/all_to_all | solution.py:19
  29.6 3.4 %collective-permute-start = (bf16[128,1024]{1,0:T(8,128)(2,1)S(1)}, bf16[128,1024]{1,0:T(8,128)(2,1)S(1)}, u32[]{:S(2)}, u32[]{:S(2)}) collective-permute-start(bf16[128,1024]{1,0:T(8,128)(2,1)S(1)} %copy-done.2), channel_id=1, source_target_pairs={{0,1},{1,0},{2,3},{3,2},{4,5},{5,4},{6,7},{7,6},{8,9},{9,8},{10,11... | collective-permute-start | bytes 786440 | tf_op jit(solution)/shard_map/ppermute | solution.py:23
  47.4 12.7 %copy-start = (bf16[3,1024,128]{2,1,0:T(8,128)(2,1)S(1)}, bf16[3,1024,128]{2,1,0:T(8,128)(2,1)}, u32[]{:S(2)}) copy-start(bf16[3,1024,128]{2,1,0:T(8,128)(2,1)} %w_ref.5) | copy-start | bytes 2359300
  47.4 12.7 %copy-start.3 = (f32[1024]{0:T(1024)S(1)}, f32[1024]{0:T(1024)}, u32[]{:S(2)}) copy-start(f32[1024]{0:T(1024)} %param.13) | copy-start | bytes 12292
  58.2 3.8 %collective-permute-start.1 = (bf16[4,512,128]{2,1,0:T(8,128)(2,1)S(1)}, bf16[4,512,128]{2,1,0:T(8,128)(2,1)S(1)}, u32[]{:S(2)}, u32[]{:S(2)}) collective-permute-start(bf16[4,512,128]{2,1,0:T(8,128)(2,1)S(1)} %all_to_all.20.own_ref), channel_id=1, source_target_pairs={{0,1},{1,0},{2,3},{3,2},{4,5},{5,4},{6,7},{7,6},{8,9},{9,8},{10,11... | collective-permute-start | bytes 1572872 | tf_op jit(solution)/shard_map/ppermute | solution.py:23
  62.8 9.6 %collective-permute-start.4 = (bf16[1024,128]{1,0:T(8,128)(2,1)S(1)}, bf16[1024,128]{1,0:T(8,128)(2,1)S(1)}, u32[]{:S(2)}, u32[]{:S(2)}) collective-permute-start(bf16[1024,128]{1,0:T(8,128)(2,1)S(1)} %kv.1.kv_ref), channel_id=1, source_target_pairs={{0,8},{1,1017},{8,0},{9,17},{16,24},{17,9},{24,16},{25,33},{32,40}... | collective-permute-start | bytes 786440 | tf_op jit(solution)/shard_map/ppermute | solution.py:34
  65.6 11.6 %collective-permute-start.2 = (bf16[1024,128]{1,0:T(8,128)(2,1)S(1)}, bf16[1024,128]{1,0:T(8,128)(2,1)S(1)}, u32[]{:S(2)}, u32[]{:S(2)}) collective-permute-start(bf16[1024,128]{1,0:T(8,128)(2,1)S(1)} %kv.1.kv_ref), channel_id=1, source_target_pairs={{0,1016},{1,9},{8,16},{9,1},{16,8},{17,25},{24,32},{25,17},{32,24}... | collective-permute-start | bytes 786440 | tf_op jit(solution)/shard_map/ppermute | solution.py:34
  68.7 10.4 %copy-start.5 = (s32[1,4]{1,0:T(1,128)S(1)}, s32[1,4]{1,0:T(1,128)}, u32[]{:S(2)}) copy-start(s32[1,4]{1,0:T(1,128)} %refs_0_.7) | copy-start | bytes 52
  72.4 12.4 %collective-permute-start.5 = (bf16[1024,128]{1,0:T(8,128)(2,1)S(1)}, bf16[1024,128]{1,0:T(8,128)(2,1)S(1)}, u32[]{:S(2)}, u32[]{:S(2)}) collective-permute-start(bf16[1024,128]{1,0:T(8,128)(2,1)S(1)} %collective-permute-done.4.refs_2_), channel_id=1, source_target_pairs={{0,1016},{1,9},{8,16},{9,1},{16,8},{17,25},{24,32},{25,17},{32,24}... | collective-permute-start | bytes 786440 | tf_op jit(solution)/shard_map/ppermute | solution.py:34
  77.2 9.0 %collective-permute-start.3 = (bf16[1024,128]{1,0:T(8,128)(2,1)S(1)}, bf16[1024,128]{1,0:T(8,128)(2,1)S(1)}, u32[]{:S(2)}, u32[]{:S(2)}) collective-permute-start(bf16[1024,128]{1,0:T(8,128)(2,1)S(1)} %collective-permute-done.2.refs_2_), channel_id=1, source_target_pairs={{0,8},{1,1017},{8,0},{9,17},{16,24},{17,9},{24,16},{25,33},{32,40}... | collective-permute-start | bytes 786440 | tf_op jit(solution)/shard_map/ppermute | solution.py:34
  87.8 3.2 %collective-permute-start.6 = (bf16[512,128]{1,0:T(8,128)(2,1)S(1)}, bf16[512,128]{1,0:T(8,128)(2,1)S(1)}, u32[]{:S(2)}, u32[]{:S(2)}) collective-permute-start(bf16[512,128]{1,0:T(8,128)(2,1)S(1)} %peer3.1.own_ref), channel_id=1, source_target_pairs={{0,1},{1,0},{2,3},{3,2},{4,5},{5,4},{6,7},{7,6},{8,9},{9,8},{10,11... | collective-permute-start | bytes 393224 | tf_op jit(solution)/shard_map/ppermute | solution.py:23
  91.5 21.4 %copy-start.6 = (s32[1,128,4]{1,2,0:T(4,128)S(1)}, s32[1,128,4]{1,2,0:T(4,128)}, u32[]{:S(2)}) copy-start(s32[1,128,4]{1,2,0:T(4,128)} %param.11) | copy-start | bytes 6148
  104.1 26.0 %copy-start.1 = (bf16[2048,128]{1,0:T(8,128)(2,1)S(1)}, bf16[2048,128]{1,0:T(8,128)(2,1)}, u32[]{:S(2)}) copy-start(bf16[2048,128]{1,0:T(8,128)(2,1)} %grid_ref.1) | copy-start | bytes 1572868
  104.1 26.0 %copy-start.4 = (s32[2048]{0:T(1024)S(1)}, s32[2048]{0:T(1024)}, u32[]{:S(2)}) copy-start(s32[2048]{0:T(1024)} %param.10) | copy-start | bytes 24580
  104.9 25.3 %all-to-all-start.3 = ((bf16[128,4,128]{2,1,0:T(4,128)(2,1)}), bf16[128,4,128]{2,1,0:T(4,128)(2,1)S(1)}, u32[]{:S(2)}, u32[]{:S(2)}) async-start(bf16[128,4,128]{2,1,0:T(4,128)(2,1)} %bitcast.4), calls=%async_computation.3 | async-start | bytes 262144 | tf_op jit(solution)/shard_map/all_to_all | solution.py:19

commit v6 on v5

--- a/solution.py
+++ b/solution.py
@@ -171,20 +171,27 @@
     attend_block(q_ref, kv_ref, is_seen(turn, mask_ref), states[:3], put)
 
 
-def last_kernel(turn, mask_ref, q_ref, kv_ref, *refs):
+def last_kernel(turn, mask_ref, q_ref, kv_ref, top_ref, total_ref, mixed_ref, w_ref, out_ref):
+    rows, width = q_ref.shape
+
     def put(at, top, total, mixed):
-        refs[3][at, :] = (mixed / total).astype(BF16)
-
-    attend_block(q_ref, kv_ref, is_seen(turn, mask_ref), refs[:3], put)
-
-
-def share_kernel(own_ref, other_ref, w_own_ref, w_other_ref, out_ref):
-    blocks, _, width = out_ref.shape
+        out_ref[at, :] = (mixed / total).astype(BF16)
+
+    attend_block(q_ref, kv_ref, is_seen(turn, mask_ref), (top_ref, total_ref, mixed_ref), put)
+    part = 1 - lax.axis_index("core")
+    for block in range(w_ref.shape[1] // (2 * width)):
+        at = pl.ds(pl.multiple_of((2 * block + part) * width, width), width)
+        out_ref[rows + block * width : rows + (block + 1) * width, :] = w_ref[:, at]
+
+
+def share_kernel(chip_ref, w_ref, out_ref):
+    blocks, rows, width = out_ref.shape
     core = lax.axis_index("core")
-    both = jnp.concatenate([own_ref[...], other_ref[...]], axis=1)
+    both = jnp.concatenate([chip_ref[core, :rows, :], chip_ref[1 - core, :rows, :]], axis=1)
     for block in range(blocks):
         at = pl.ds(pl.multiple_of((2 * block + core) * width, width), width)
-        weight = jnp.concatenate([w_own_ref[:, at], w_other_ref[:, at]], axis=0)
+        w_other = chip_ref[1 - core, rows + block * width : rows + (block + 1) * width, :]
+        weight = jnp.concatenate([w_ref[:, at], w_other], axis=0)
         out_ref[block] = jnp.dot(both, weight, preferred_element_type=F32).astype(BF16)
 
 
@@ -194,24 +201,6 @@
         total = total + parts_ref[block].astype(F32)
     state_ref[...] = total
     back_ref[...] = total.astype(BF16)
-
-
-def down(row):
-    return jnp.broadcast_to(row, (row.shape[1], row.shape[1])).T
-
-
-def decode_kernel(slot_ref, returned_ref, grid_ref, out_ref):
-    step = pl.program_id(0)
-    points, lanes = grid_ref.shape
-    slots = returned_ref.shape[0]
-    pieces = points // lanes
-    for i in range(pieces):
-        slot = down(slot_ref[pl.ds(step * pieces + i, 1), :])
-        number = lax.broadcasted_iota(jnp.int32, (lanes, slots), 1)
-        hot = jnp.where(number == jnp.concatenate([slot] * (slots // lanes), axis=1), 1.0, 0.0)
-        rows = slice(i * lanes, (i + 1) * lanes)
-        back = jnp.dot(hot.astype(BF16), returned_ref[...], preferred_element_type=F32)
-        out_ref[rows, :] = (grid_ref[rows, :].astype(F32) + back).astype(BF16)
 
 
 def call(kernel, outs, name, scratch=(), flops=0, bytes_accessed=0, transcendentals=0):
@@ -243,18 +232,11 @@
     low = jax.ShapeDtypeStruct((rows, width), BF16)
     state = jax.ShapeDtypeStruct((rows, width), F32)
 
-    points = grid.shape[0]
-    by_lane = pl.BlockSpec((points // width, width), lambda i: (0, 0))
-    by_slot = pl.BlockSpec((slots, width), lambda i: (0, 0))
-    by_step = pl.BlockSpec((points // 4, width), lambda i: (i, 0))
-    slot_rows = g2m_slot.reshape(-1, width)
     scaled = (g2m_weight[:, None] * grid.astype(F32)).astype(BF16)
     slot_hot = (g2m_slot[None, :] == jnp.arange(slots, dtype=jnp.int32)[:, None]).astype(BF16)
     partial_value = jnp.dot(slot_hot, scaled, preferred_element_type=F32).astype(BF16)
-    w_other = other_core(w_out)
     mesh_low = exchange(partial_value.reshape(regions, cap, width), "region").reshape(rows, width)
 
-    mesh_low = after(mesh_low, w_other)
     own = exchange(jnp.broadcast_to(mesh_low, (chips, rows, width)), "x")
     other = other_core(own)
     gain = norm_gain.reshape(parts, width)
@@ -279,7 +261,8 @@
     cost = dict(flops=8 * rows * rows * width, transcendentals=2 * rows * rows)
 
     def attend(turn, *args):
-        outs, kernel = (low, last_kernel) if turn == 3 else ((state,) * 3, peer_kernel)
+        lasts = jax.ShapeDtypeStruct((rows + chips * width, width), BF16)
+        outs, kernel = (lasts, last_kernel) if turn == 3 else ((state,) * 3, peer_kernel)
         return call(lambda *refs: kernel(turn, *refs), outs, f"peer{turn}", **cost)(
             peer_mask, queries, *args
         )
@@ -292,14 +275,14 @@
     so_far = attend(0, kv0, *so_far)
     so_far = attend(1, kv1, *so_far)
     so_far = attend(2, kv2, *so_far)
-    attended = attend(3, kv3, *so_far)
+    attended = attend(3, kv3, *so_far, w_out)
 
     summed = call(
         share_kernel,
         jax.ShapeDtypeStruct((chips, rows, width), BF16),
         "share",
         flops=4 * rows * width * chips * width,
-    )(attended, other_core(attended), w_out, w_other)
+    )(lax.all_gather(attended, "core"), w_out)
     mesh_slots, mesh_back = call(sum_kernel, (state, low), "sum", bytes_accessed=1 << 20)(
         mesh_low, exchange(summed, "x")
     )
@@ -310,15 +293,8 @@
     mesh_state = jnp.dot(
         node_hot, mesh_slots, precision=lax.Precision.HIGHEST, preferred_element_type=F32
     )
-    grid_out = pl.pallas_call(
-        decode_kernel,
-        grid=(4,),
-        out_shape=jax.ShapeDtypeStruct(grid.shape, BF16),
-        in_specs=[by_lane, by_slot, by_step],
-        out_specs=by_step,
-        compiler_params=PARAMS,
-        name="decode",
-    )(slot_rows, returned, grid)
+    gathered = jnp.dot(slot_hot.T, returned, preferred_element_type=F32)
+    grid_out = (grid.astype(F32) + gathered).astype(BF16)
     return (mesh_state, grid_out)
 
 

time: 134 us -> 132 us (0.985)
  blocking collectives: 23.4 us -> 69.4 us
  starting transfers between devices: 51.8 us -> 21.6 us
  waiting for transfers between devices: 38.9 us -> 21.8 us
  Pallas kernels: 13.3 us -> 11 us
  matrix products: 4.01 us -> 5.39 us
    all_to_all x2 -> x3, blocking collectives: 23.4 us -> 67.2 us  [exchange(): return lax.all_to_all(array, axis, split_axis=0, concat_axis=0, tiled=True)]
    all_to_all x2 -> x1, starting transfers between devices: 34.3 us -> 8.09 us  [exchange(): return lax.all_to_all(array, axis, split_axis=0, concat_axis=0, tiled=True)]
    all_to_all x2 -> x1, waiting for transfers between devices: 30.1 us -> 15.7 us  [exchange(): return lax.all_to_all(array, axis, split_axis=0, concat_axis=0, tiled=True)]
    ppermute x3 -> x1, starting transfers between devices: 6.07 us -> 1.91 us  [other_core(): return lax.ppermute(value, 'core', [(0, 1), (1, 0)])]
    ppermute x3 -> x1, waiting for transfers between devices: 3.34 us -> 0.85 us  [other_core(): return lax.ppermute(value, 'core', [(0, 1), (1, 0)])]
    pallas_call x1 -> x0, Pallas kernels: 2.36 us -> none  [on_device(): pl.pallas_call(decode_kernel, grid=(4,), out_shape=jax.ShapeDtypeStruct(g...]
    all_gather x0 -> x1, blocking collectives: none -> 2.18 us  [on_device(): lax.all_gather(attended, 'core')]
    dot_general x0 -> x1, matrix products: none -> 2.09 us  [on_device(): gathered = jnp.dot(slot_hot.T, returned, preferred_element_type=F32)]
  transfers between devices with their start and end apart: 9 -> 6, of which waited for: 8 -> 5; matrix products, arithmetic and copies ran while one was open for 1% -> 1% of each run, Pallas kernels for 6% -> 6%
where the time goes in v6:
time: 132 us; the launch traced here: 130 us
  blocking collectives  69.4 us (53%)
  waiting for transfers between devices  21.8 us (17%)
  starting transfers between devices  21.6 us (16%)
  Pallas kernels  11 us (8%)
  matrix products  5.39 us (4%)
    all_to_all x3, blocking collectives, exchange(): return lax.all_to_all(array, axis, split_axis=0, concat_axis=0, tiled=True)  67.2 us
    all_to_all x1, waiting for transfers between devices, exchange(): return lax.all_to_all(array, axis, split_axis=0, concat_axis=0, tiled=True)  15.7 us
    ppermute x4, starting transfers between devices, swapped(): return lax.ppermute(value, (axis, 'core'), pairs)  11.6 us
    pallas_call x10, Pallas kernels, run(): pl.pallas_call(kernel, out_shape=outs, in_specs=[VMEM] * len(args), out_s...  11 us
    all_to_all x1, starting transfers between devices, exchange(): return lax.all_to_all(array, axis, split_axis=0, concat_axis=0, tiled=True)  8.09 us
    ppermute x4, waiting for transfers between devices, swapped(): return lax.ppermute(value, (axis, 'core'), pairs)  5.18 us
  transfers between devices with their start and end apart: 6, of which 5 were waited for; matrix products, arithmetic and copies ran while one was open for 1% of the time, Pallas kernels for 6%

profile of v6, /device:TPU:6, one launch (start us, length us, event | category | flops | bytes accessed | tf_op | source)
XLA Modules:
  0.0 130.3 jit_solution(6585523392582199016)
XLA Ops:
  0.6 2.0 %fusion.6 = bf16[512,128]{1,0:T(8,128)(2,1)S(1)} fusion(s32[2048]{0:T(1024)} %param.10, bf16[2048,128]{1,0:T(8,128)(2,1)} %param.8, f32[2048]{0:T(1024)} %param.9), kind=kOutput, calls=%fused_computation.8 | convolution fusion | flops 270336000 | bytes 671744 | tf_op jit(solution)/shard_map/dot_general | solution.py:237
  2.6 43.8 %all_to_all.20 = bf16[128,4,128]{2,1,0:T(4,128)(2,1)S(1)} all-to-all(bf16[128,4,128]{2,1,0:T(4,128)(2,1)S(1)} %bitcast.15), channel_id=1, replica_groups=mesh['region'=128,'x'=4,'core'=2] {'region'}, dimensions={0} | all-to-all | bytes 262144 | tf_op jit(solution)/shard_map/all_to_all | solution.py:19
  46.4 0.1 broadcast_in_dim.2
  46.5 10.7 %all_to_all.21.own_ref = bf16[4,512,128]{2,1,0:T(8,128)(2,1)S(1)} all-to-all(bf16[4,512,128]{2,1,0:T(8,128)(2,1)S(1)} %broadcast_in_dim.2), channel_id=1, replica_groups=mesh['region'=128,'x'=4,'core'=2] {'x'}, dimensions={0} | all-to-all | bytes 1048576 | tf_op jit(solution)/shard_map/all_to_all | solution.py:19
  57.2 1.9 %collective-permute-start = (bf16[4,512,128]{2,1,0:T(8,128)(2,1)S(1)}, bf16[4,512,128]{2,1,0:T(8,128)(2,1)S(1)}, u32[]{:S(2)}, u32[]{:S(2)}) collective-permute-start(bf16[4,512,128]{2,1,0:T(8,128)(2,1)S(1)} %all_to_all.21.own_ref), channel_id=1, source_target_pairs={{0,1},{1,0},{2,3},{3,2},{4,5},{5,4},{6,7},{7,6},{8,9},{9,8},{10,11... | collective-permute-start | bytes 1572872 | tf_op jit(solution)/shard_map/ppermute | solution.py:23
  59.1 1.0 own_half.1
  60.2 0.8 collective-permute-done.other_ref
  61.0 0.9 kv.1.kv_ref
  61.9 2.9 %collective-permute-start.3 = (bf16[1024,128]{1,0:T(8,128)(2,1)S(1)}, bf16[1024,128]{1,0:T(8,128)(2,1)S(1)}, u32[]{:S(2)}, u32[]{:S(2)}) collective-permute-start(bf16[1024,128]{1,0:T(8,128)(2,1)S(1)} %kv.1.kv_ref), channel_id=1, source_target_pairs={{0,8},{1,1017},{8,0},{9,17},{16,24},{17,9},{24,16},{25,33},{32,40}... | collective-permute-start | bytes 786440 | tf_op jit(solution)/shard_map/ppermute | solution.py:34
  64.7 2.4 %collective-permute-start.1 = (bf16[1024,128]{1,0:T(8,128)(2,1)S(1)}, bf16[1024,128]{1,0:T(8,128)(2,1)S(1)}, u32[]{:S(2)}, u32[]{:S(2)}) collective-permute-start(bf16[1024,128]{1,0:T(8,128)(2,1)S(1)} %kv.1.kv_ref), channel_id=1, source_target_pairs={{0,1016},{1,9},{8,16},{9,1},{16,8},{17,25},{24,32},{25,17},{32,24}... | collective-permute-start | bytes 786440 | tf_op jit(solution)/shard_map/ppermute | solution.py:34
  67.1 0.8 q.1.q_ref.refs_1_
  67.9 1.2 own.1
  69.1 2.3 %collective-permute-done.3.refs_2_ = bf16[1024,128]{1,0:T(8,128)(2,1)S(1)} collective-permute-done((bf16[1024,128]{1,0:T(8,128)(2,1)S(1)}, bf16[1024,128]{1,0:T(8,128)(2,1)S(1)}, u32[]{:S(2)}, u32[]{:S(2)}) %collective-permute-start.3) | collective-permute-done | bytes 262176 | tf_op jit(solution)/shard_map/ppermute | solution.py:34
  71.4 4.5 %collective-permute-start.4 = (bf16[1024,128]{1,0:T(8,128)(2,1)S(1)}, bf16[1024,128]{1,0:T(8,128)(2,1)S(1)}, u32[]{:S(2)}, u32[]{:S(2)}) collective-permute-start(bf16[1024,128]{1,0:T(8,128)(2,1)S(1)} %collective-permute-done.3.refs_2_), channel_id=1, source_target_pairs={{0,1016},{1,9},{8,16},{9,1},{16,8},{17,25},{24,32},{25,17},{32,24}... | collective-permute-start | bytes 786440 | tf_op jit(solution)/shard_map/ppermute | solution.py:34
  75.9 0.4 collective-permute-done.1.refs_2_
  76.3 1.9 %collective-permute-start.2 = (bf16[1024,128]{1,0:T(8,128)(2,1)S(1)}, bf16[1024,128]{1,0:T(8,128)(2,1)S(1)}, u32[]{:S(2)}, u32[]{:S(2)}) collective-permute-start(bf16[1024,128]{1,0:T(8,128)(2,1)S(1)} %collective-permute-done.1.refs_2_), channel_id=1, source_target_pairs={{0,8},{1,1017},{8,0},{9,17},{16,24},{17,9},{24,16},{25,33},{32,40}... | collective-permute-start | bytes 786440 | tf_op jit(solution)/shard_map/ppermute | solution.py:34
  78.3 1.5 %peer0.1 = (f32[512,128]{1,0:T(8,128)S(1)}, f32[512,128]{1,0:T(8,128)S(1)}, f32[512,128]{1,0:T(8,128)S(1)}) custom-call(s32[1,4]{1,0:T(1,128)S(1)} %copy-done.3, bf16[512,128]{1,0:T(8,128)(2,1)S(1)} %q.1.q_ref.refs_1_, bf16[1024,128]{1,0:T(8,128)(2,1)S(1)} %collective-permute-done.3.refs_2_, f32[512,128]{1,0:T(8,128)S(1)} %get-tuple-element.21.refs_3_, ...), custom_call_target="tpu_custom_call" | custom-call | flops 268435456 | tf_op jit(solution)/shard_map/peer0/pallas_call | solution.py:208
  79.8 1.5 %peer1.1 = (f32[512,128]{1,0:T(8,128)S(1)}, f32[512,128]{1,0:T(8,128)S(1)}, f32[512,128]{1,0:T(8,128)S(1)}) custom-call(s32[1,4]{1,0:T(1,128)S(1)} %copy-done.3, bf16[512,128]{1,0:T(8,128)(2,1)S(1)} %q.1.q_ref.refs_1_, bf16[1024,128]{1,0:T(8,128)(2,1)S(1)} %collective-permute-done.1.refs_2_, f32[512,128]{1,0:T(8,128)S(1)} %get-tuple-element.25.refs_3_, ...), custom_call_target="tpu_custom_call" | custom-call | flops 268435456 | tf_op jit(solution)/shard_map/peer1/pallas_call | solution.py:208
  81.3 2.4 %collective-permute-done.4.refs_2_ = bf16[1024,128]{1,0:T(8,128)(2,1)S(1)} collective-permute-done((bf16[1024,128]{1,0:T(8,128)(2,1)S(1)}, bf16[1024,128]{1,0:T(8,128)(2,1)S(1)}, u32[]{:S(2)}, u32[]{:S(2)}) %collective-permute-start.4) | collective-permute-done | bytes 262176 | tf_op jit(solution)/shard_map/ppermute | solution.py:34
  83.7 1.5 %peer2.1 = (f32[512,128]{1,0:T(8,128)S(1)}, f32[512,128]{1,0:T(8,128)S(1)}, f32[512,128]{1,0:T(8,128)S(1)}) custom-call(s32[1,4]{1,0:T(1,128)S(1)} %copy-done.3, bf16[512,128]{1,0:T(8,128)(2,1)S(1)} %q.1.q_ref.refs_1_, bf16[1024,128]{1,0:T(8,128)(2,1)S(1)} %collective-permute-done.4.refs_2_, f32[512,128]{1,0:T(8,128)S(1)} %get-tuple-element.28.refs_3_, ...), custom_call_target="tpu_custom_call" | custom-call | flops 268435456 | tf_op jit(solution)/shard_map/peer2/pallas_call | solution.py:208
  85.2 1.5 %peer3.1 = bf16[1024,128]{1,0:T(8,128)(2,1)S(1)} custom-call(s32[1,4]{1,0:T(1,128)S(1)} %copy-done.3, bf16[512,128]{1,0:T(8,128)(2,1)S(1)} %q.1.q_ref.refs_1_, bf16[1024,128]{1,0:T(8,128)(2,1)S(1)} %collective-permute-done.2.refs_2_, f32[512,128]{1,0:T(8,128)S(1)} %get-tuple-element.31.refs_3_, f32[512,128]{1,0:T(8,128)S(1)} %get-tuple-element.32.refs_4_, ...), custom_call_target="tpu_custom_call" | custom-call | flops 268435456 | tf_op jit(solution)/shard_map/peer3/pallas_call | solution.py:208
  86.7 2.2 %all-gather = bf16[2048,128]{1,0:T(8,128)(2,1)S(1)} all-gather(bf16[1024,128]{1,0:T(8,128)(2,1)S(1)} %peer3.1), channel_id=2, replica_groups=mesh['region'=128,'x'=4,'core'=2] {'core'}, dimensions={0}, use_global_device_ids=true | all-gather | bytes 786432 | tf_op jit(solution)/shard_map/all_gather | solution.py:285
  88.9 0.4 share.1
  89.4 0.0 copy-start.4
  89.4 12.7 %all_to_all.22.parts_ref = bf16[4,512,128]{2,1,0:T(8,128)(2,1)S(1)} all-to-all(bf16[4,512,128]{2,1,0:T(8,128)(2,1)S(1)} %share.1), channel_id=1, replica_groups=mesh['region'=128,'x'=4,'core'=2] {'x'}, dimensions={0} | all-to-all | bytes 1048576 | tf_op jit(solution)/shard_map/all_to_all | solution.py:19
  102.1 0.7 sum.1
  102.8 8.1 %all-to-all-start.3 = ((bf16[128,4,128]{2,1,0:T(4,128)(2,1)}), bf16[128,4,128]{2,1,0:T(4,128)(2,1)S(1)}, u32[]{:S(2)}, u32[]{:S(2)}) async-start(bf16[128,4,128]{2,1,0:T(4,128)(2,1)} %bitcast.4), calls=%async_computation.3 | async-start | bytes 262144 | tf_op jit(solution)/shard_map/all_to_all | solution.py:19
  110.9 0.1 copy.10
  111.1 0.1 eq.29
  111.2 1.3 %fusion.8 = f32[512,128]{1,0:T(8,128)} fusion(f32[512,128]{1,0:T(8,128)S(1)} %get-tuple-element.34, s32[512]{0:T(512)S(1)} %eq.29), kind=kOutput, calls=%fused_computation.11 | convolution fusion | flops 402915328 | bytes 526336 | tf_op jit(solution)/shard_map/dot_general | solution.py:293
  112.5 15.7 %all-to-all-done.3 = bf16[128,4,128]{2,1,0:T(4,128)(2,1)S(1)} async-done(((bf16[128,4,128]{2,1,0:T(4,128)(2,1)}), bf16[128,4,128]{2,1,0:T(4,128)(2,1)S(1)}, u32[]{:S(2)}, u32[]{:S(2)}) %all-to-all-start.3) | async-done | bytes 131104 | tf_op jit(solution)/shard_map/all_to_all | solution.py:19
  128.2 2.1 %fusion.3 = bf16[2048,128]{1,0:T(8,128)(2,1)} fusion(bf16[512,128]{1,0:T(8,128)(2,1)S(1)} %bitcast.14, s32[2048]{0:T(1024)S(1)} %copy-done.6, bf16[2048,128]{1,0:T(8,128)(2,1)S(1)} %copy-done.5), kind=kOutput, calls=%fused_computation.4 | convolution fusion | flops 270270464 | bytes 1187840 | tf_op jit(solution)/shard_map/dot_general | solution.py:296
  (14 shorter events, 0.0 us)
Async XLA Ops:
  46.4 12.7 %copy-start = (bf16[3,1024,128]{2,1,0:T(8,128)(2,1)S(1)}, bf16[3,1024,128]{2,1,0:T(8,128)(2,1)}, u32[]{:S(2)}) copy-start(bf16[3,1024,128]{2,1,0:T(8,128)(2,1)} %w_ref.6) | copy-start | bytes 2359300
  46.4 12.7 %copy-start.2 = (f32[1024]{0:T(1024)S(1)}, f32[1024]{0:T(1024)}, u32[]{:S(2)}) copy-start(f32[1024]{0:T(1024)} %param.13) | copy-start | bytes 12292
  57.2 3.8 %collective-permute-start = (bf16[4,512,128]{2,1,0:T(8,128)(2,1)S(1)}, bf16[4,512,128]{2,1,0:T(8,128)(2,1)S(1)}, u32[]{:S(2)}, u32[]{:S(2)}) collective-permute-start(bf16[4,512,128]{2,1,0:T(8,128)(2,1)S(1)} %all_to_all.21.own_ref), channel_id=1, source_target_pairs={{0,1},{1,0},{2,3},{3,2},{4,5},{5,4},{6,7},{7,6},{8,9},{9,8},{10,11... | collective-permute-start | bytes 1572872 | tf_op jit(solution)/shard_map/ppermute | solution.py:23
  61.9 9.5 %collective-permute-start.3 = (bf16[1024,128]{1,0:T(8,128)(2,1)S(1)}, bf16[1024,128]{1,0:T(8,128)(2,1)S(1)}, u32[]{:S(2)}, u32[]{:S(2)}) collective-permute-start(bf16[1024,128]{1,0:T(8,128)(2,1)S(1)} %kv.1.kv_ref), channel_id=1, source_target_pairs={{0,8},{1,1017},{8,0},{9,17},{16,24},{17,9},{24,16},{25,33},{32,40}... | collective-permute-start | bytes 786440 | tf_op jit(solution)/shard_map/ppermute | solution.py:34
  64.7 11.6 %collective-permute-start.1 = (bf16[1024,128]{1,0:T(8,128)(2,1)S(1)}, bf16[1024,128]{1,0:T(8,128)(2,1)S(1)}, u32[]{:S(2)}, u32[]{:S(2)}) collective-permute-start(bf16[1024,128]{1,0:T(8,128)(2,1)S(1)} %kv.1.kv_ref), channel_id=1, source_target_pairs={{0,1016},{1,9},{8,16},{9,1},{16,8},{17,25},{24,32},{25,17},{32,24}... | collective-permute-start | bytes 786440 | tf_op jit(solution)/shard_map/ppermute | solution.py:34
  67.9 10.3 %copy-start.3 = (s32[1,4]{1,0:T(1,128)S(1)}, s32[1,4]{1,0:T(1,128)}, u32[]{:S(2)}) copy-start(s32[1,4]{1,0:T(1,128)} %refs_0_.7) | copy-start | bytes 52
  71.4 12.3 %collective-permute-start.4 = (bf16[1024,128]{1,0:T(8,128)(2,1)S(1)}, bf16[1024,128]{1,0:T(8,128)(2,1)S(1)}, u32[]{:S(2)}, u32[]{:S(2)}) collective-permute-start(bf16[1024,128]{1,0:T(8,128)(2,1)S(1)} %collective-permute-done.3.refs_2_), channel_id=1, source_target_pairs={{0,1016},{1,9},{8,16},{9,1},{16,8},{17,25},{24,32},{25,17},{32,24}... | collective-permute-start | bytes 786440 | tf_op jit(solution)/shard_map/ppermute | solution.py:34
  76.3 8.9 %collective-permute-start.2 = (bf16[1024,128]{1,0:T(8,128)(2,1)S(1)}, bf16[1024,128]{1,0:T(8,128)(2,1)S(1)}, u32[]{:S(2)}, u32[]{:S(2)}) collective-permute-start(bf16[1024,128]{1,0:T(8,128)(2,1)S(1)} %collective-permute-done.1.refs_2_), channel_id=1, source_target_pairs={{0,8},{1,1017},{8,0},{9,17},{16,24},{17,9},{24,16},{25,33},{32,40}... | collective-permute-start | bytes 786440 | tf_op jit(solution)/shard_map/ppermute | solution.py:34
  81.3 4.0 %copy-start.1 = (bf16[128,1024]{1,0:T(8,128)(2,1)S(1)}, bf16[128,1024]{1,0:T(8,128)(2,1)}, u32[]{:S(2)}) copy-start(bf16[128,1024]{1,0:T(8,128)(2,1)} %w_ref.7) | copy-start | bytes 786436
  89.4 21.6 %copy-start.4 = (s32[1,128,4]{1,2,0:T(4,128)S(1)}, s32[1,128,4]{1,2,0:T(4,128)}, u32[]{:S(2)}) copy-start(s32[1,128,4]{1,2,0:T(4,128)} %param.11) | copy-start | bytes 6148
  102.1 26.1 %copy-start.5 = (bf16[2048,128]{1,0:T(8,128)(2,1)S(1)}, bf16[2048,128]{1,0:T(8,128)(2,1)}, u32[]{:S(2)}) copy-start(bf16[2048,128]{1,0:T(8,128)(2,1)} %param.8) | copy-start | bytes 1572868
  102.1 26.1 %copy-start.6 = (s32[2048]{0:T(1024)S(1)}, s32[2048]{0:T(1024)}, u32[]{:S(2)}) copy-start(s32[2048]{0:T(1024)} %param.10) | copy-start | bytes 24580
  102.8 25.4 %all-to-all-start.3 = ((bf16[128,4,128]{2,1,0:T(4,128)(2,1)}), bf16[128,4,128]{2,1,0:T(4,128)(2,1)S(1)}, u32[]{:S(2)}, u32[]{:S(2)}) async-start(bf16[128,4,128]{2,1,0:T(4,128)(2,1)} %bitcast.4), calls=%async_computation.3 | async-start | bytes 262144 | tf_op jit(solution)/shard_map/all_to_all | solution.py:19

commit v7 on v6

--- a/solution.py
+++ b/solution.py
@@ -8,7 +8,7 @@
 
 HEAD_DIM = 64
 OFFSETS = (-2, -1, 1, 2)
-CHUNK = 128
+CHUNK = 256
 BF16 = jnp.bfloat16
 F32 = jnp.float32
 VMEM = pl.BlockSpec(memory_space=pltpu.VMEM)
@@ -203,6 +203,20 @@
     back_ref[...] = total.astype(BF16)
 
 
+def hot_kernel(slot_ref, hot_ref):
+    lanes, slots = slot_ref.shape[1], hot_ref.shape[1]
+    number = lax.broadcasted_iota(jnp.int32, (lanes, slots), 1)
+    for i in range(slot_ref.shape[0]):
+        down = jnp.broadcast_to(slot_ref[i : i + 1, :], (lanes, lanes)).T
+        wanted = jnp.concatenate([down] * (slots // lanes), axis=1)
+        hot_ref[i * lanes : (i + 1) * lanes, :] = jnp.where(number == wanted, 1.0, 0.0).astype(BF16)
+
+
+def decode_kernel(hot_ref, returned_ref, grid_ref, out_ref):
+    back = jnp.dot(hot_ref[...], returned_ref[...], preferred_element_type=F32)
+    out_ref[...] = (grid_ref[...].astype(F32) + back).astype(BF16)
+
+
 def call(kernel, outs, name, scratch=(), flops=0, bytes_accessed=0, transcendentals=0):
     def run(*args):
         return pl.pallas_call(
@@ -293,8 +307,11 @@
     mesh_state = jnp.dot(
         node_hot, mesh_slots, precision=lax.Precision.HIGHEST, preferred_element_type=F32
     )
-    gathered = jnp.dot(slot_hot.T, returned, preferred_element_type=F32)
-    grid_out = (grid.astype(F32) + gathered).astype(BF16)
+    hots = jax.ShapeDtypeStruct((grid.shape[0], slots), BF16)
+    slot_rows = after(g2m_slot.reshape(-1, width), mesh_back)
+    hot = call(hot_kernel, hots, "hot", bytes_accessed=1 << 21)(slot_rows)
+    outs = jax.ShapeDtypeStruct(grid.shape, BF16)
+    grid_out = call(decode_kernel, outs, "decode")(hot, returned, grid)
     return (mesh_state, grid_out)
 
 

time: 132 us -> 130 us (0.985)
  matrix products: 5.39 us -> 3.38 us
    dot_general x1 -> x0, matrix products: 2.09 us -> none  [on_device(): gathered = jnp.dot(slot_hot.T, returned, preferred_element_type=F32)]
    pallas_call x10 -> x12, Pallas kernels: 11 us -> 12 us  [run(): pl.pallas_call(kernel, out_shape=outs, in_specs=[VMEM] * len(args), out_s...]
where the time goes in v7:
time: 130 us; the launch traced here: 129 us
  blocking collectives  69.3 us (53%)
  waiting for transfers between devices  22.2 us (17%)
  starting transfers between devices  21 us (16%)
  Pallas kernels  12 us (9%)
  matrix products  3.38 us (3%)
    all_to_all x3, blocking collectives, exchange(): return lax.all_to_all(array, axis, split_axis=0, concat_axis=0, tiled=True)  67.1 us
    all_to_all x1, waiting for transfers between devices, exchange(): return lax.all_to_all(array, axis, split_axis=0, concat_axis=0, tiled=True)  15.3 us
    pallas_call x12, Pallas kernels, run(): pl.pallas_call(kernel, out_shape=outs, in_specs=[VMEM] * len(args), out_s...  12 us
    ppermute x4, starting transfers between devices, swapped(): return lax.ppermute(value, (axis, 'core'), pairs)  11.3 us
    all_to_all x1, starting transfers between devices, exchange(): return lax.all_to_all(array, axis, split_axis=0, concat_axis=0, tiled=True)  7.72 us
    ppermute x4, waiting for transfers between devices, swapped(): return lax.ppermute(value, (axis, 'core'), pairs)  5.73 us
  transfers between devices with their start and end apart: 6, of which 5 were waited for; matrix products, arithmetic and copies ran while one was open for 1% of the time, Pallas kernels for 6%

profile of v7, /device:TPU:6, one launch (start us, length us, event | category | flops | bytes accessed | tf_op | source)
XLA Modules:
  0.0 129.0 jit_solution(729680703903709324)
XLA Ops:
  0.7 2.1 %fusion.2 = bf16[512,128]{1,0:T(8,128)(2,1)S(1)} fusion(s32[2048]{0:T(1024)} %param.10, bf16[2048,128]{1,0:T(8,128)(2,1)} %grid_ref.1, f32[2048]{0:T(1024)} %param.9), kind=kOutput, calls=%fused_computation.3 | convolution fusion | flops 270336000 | bytes 671744 | tf_op jit(solution)/shard_map/dot_general | solution.py:251
  2.7 43.8 %all_to_all.20 = bf16[128,4,128]{2,1,0:T(4,128)(2,1)S(1)} all-to-all(bf16[128,4,128]{2,1,0:T(4,128)(2,1)S(1)} %bitcast.16), channel_id=1, replica_groups=mesh['region'=128,'x'=4,'core'=2] {'region'}, dimensions={0} | all-to-all | bytes 262144 | tf_op jit(solution)/shard_map/all_to_all | solution.py:19
  46.5 0.1 broadcast_in_dim.2
  46.6 10.6 %all_to_all.21.own_ref = bf16[4,512,128]{2,1,0:T(8,128)(2,1)S(1)} all-to-all(bf16[4,512,128]{2,1,0:T(8,128)(2,1)S(1)} %broadcast_in_dim.2), channel_id=1, replica_groups=mesh['region'=128,'x'=4,'core'=2] {'x'}, dimensions={0} | all-to-all | bytes 1048576 | tf_op jit(solution)/shard_map/all_to_all | solution.py:19
  57.2 1.9 %collective-permute-start = (bf16[4,512,128]{2,1,0:T(8,128)(2,1)S(1)}, bf16[4,512,128]{2,1,0:T(8,128)(2,1)S(1)}, u32[]{:S(2)}, u32[]{:S(2)}) collective-permute-start(bf16[4,512,128]{2,1,0:T(8,128)(2,1)S(1)} %all_to_all.21.own_ref), channel_id=1, source_target_pairs={{0,1},{1,0},{2,3},{3,2},{4,5},{5,4},{6,7},{7,6},{8,9},{9,8},{10,11... | collective-permute-start | bytes 1572872 | tf_op jit(solution)/shard_map/ppermute | solution.py:23
  59.1 0.7 own_half.1
  59.8 1.2 collective-permute-done.other_ref
  61.0 0.6 kv.1.kv_ref
  61.5 2.9 %collective-permute-start.3 = (bf16[1024,128]{1,0:T(8,128)(2,1)S(1)}, bf16[1024,128]{1,0:T(8,128)(2,1)S(1)}, u32[]{:S(2)}, u32[]{:S(2)}) collective-permute-start(bf16[1024,128]{1,0:T(8,128)(2,1)S(1)} %kv.1.kv_ref), channel_id=1, source_target_pairs={{0,8},{1,1017},{8,0},{9,17},{16,24},{17,9},{24,16},{25,33},{32,40}... | collective-permute-start | bytes 786440 | tf_op jit(solution)/shard_map/ppermute | solution.py:34
  64.4 2.4 %collective-permute-start.1 = (bf16[1024,128]{1,0:T(8,128)(2,1)S(1)}, bf16[1024,128]{1,0:T(8,128)(2,1)S(1)}, u32[]{:S(2)}, u32[]{:S(2)}) collective-permute-start(bf16[1024,128]{1,0:T(8,128)(2,1)S(1)} %kv.1.kv_ref), channel_id=1, source_target_pairs={{0,1016},{1,9},{8,16},{9,1},{16,8},{17,25},{24,32},{25,17},{32,24}... | collective-permute-start | bytes 786440 | tf_op jit(solution)/shard_map/ppermute | solution.py:34
  66.8 0.5 q.1.q_ref.refs_1_
  67.3 1.2 own.1
  68.5 2.6 %collective-permute-done.3.refs_2_ = bf16[1024,128]{1,0:T(8,128)(2,1)S(1)} collective-permute-done((bf16[1024,128]{1,0:T(8,128)(2,1)S(1)}, bf16[1024,128]{1,0:T(8,128)(2,1)S(1)}, u32[]{:S(2)}, u32[]{:S(2)}) %collective-permute-start.3) | collective-permute-done | bytes 262176 | tf_op jit(solution)/shard_map/ppermute | solution.py:34
  71.1 4.2 %collective-permute-start.4 = (bf16[1024,128]{1,0:T(8,128)(2,1)S(1)}, bf16[1024,128]{1,0:T(8,128)(2,1)S(1)}, u32[]{:S(2)}, u32[]{:S(2)}) collective-permute-start(bf16[1024,128]{1,0:T(8,128)(2,1)S(1)} %collective-permute-done.3.refs_2_), channel_id=1, source_target_pairs={{0,1016},{1,9},{8,16},{9,1},{16,8},{17,25},{24,32},{25,17},{32,24}... | collective-permute-start | bytes 786440 | tf_op jit(solution)/shard_map/ppermute | solution.py:34
  75.3 0.7 collective-permute-done.1.refs_2_
  76.0 1.9 %collective-permute-start.2 = (bf16[1024,128]{1,0:T(8,128)(2,1)S(1)}, bf16[1024,128]{1,0:T(8,128)(2,1)S(1)}, u32[]{:S(2)}, u32[]{:S(2)}) collective-permute-start(bf16[1024,128]{1,0:T(8,128)(2,1)S(1)} %collective-permute-done.1.refs_2_), channel_id=1, source_target_pairs={{0,8},{1,1017},{8,0},{9,17},{16,24},{17,9},{24,16},{25,33},{32,40}... | collective-permute-start | bytes 786440 | tf_op jit(solution)/shard_map/ppermute | solution.py:34
  77.9 1.5 %peer0.1 = (f32[512,128]{1,0:T(8,128)S(1)}, f32[512,128]{1,0:T(8,128)S(1)}, f32[512,128]{1,0:T(8,128)S(1)}) custom-call(s32[1,4]{1,0:T(1,128)S(1)} %copy-done.4, bf16[512,128]{1,0:T(8,128)(2,1)S(1)} %q.1.q_ref.refs_1_, bf16[1024,128]{1,0:T(8,128)(2,1)S(1)} %collective-permute-done.3.refs_2_, f32[512,128]{1,0:T(8,128)S(1)} %get-tuple-element.22.refs_3_, ...), custom_call_target="tpu_custom_call" | custom-call | flops 268435456 | tf_op jit(solution)/shard_map/peer0/pallas_call | solution.py:222
  79.4 1.5 %peer1.1 = (f32[512,128]{1,0:T(8,128)S(1)}, f32[512,128]{1,0:T(8,128)S(1)}, f32[512,128]{1,0:T(8,128)S(1)}) custom-call(s32[1,4]{1,0:T(1,128)S(1)} %copy-done.4, bf16[512,128]{1,0:T(8,128)(2,1)S(1)} %q.1.q_ref.refs_1_, bf16[1024,128]{1,0:T(8,128)(2,1)S(1)} %collective-permute-done.1.refs_2_, f32[512,128]{1,0:T(8,128)S(1)} %get-tuple-element.26.refs_3_, ...), custom_call_target="tpu_custom_call" | custom-call | flops 268435456 | tf_op jit(solution)/shard_map/peer1/pallas_call | solution.py:222
  80.9 2.4 %collective-permute-done.4.refs_2_ = bf16[1024,128]{1,0:T(8,128)(2,1)S(1)} collective-permute-done((bf16[1024,128]{1,0:T(8,128)(2,1)S(1)}, bf16[1024,128]{1,0:T(8,128)(2,1)S(1)}, u32[]{:S(2)}, u32[]{:S(2)}) %collective-permute-start.4) | collective-permute-done | bytes 262176 | tf_op jit(solution)/shard_map/ppermute | solution.py:34
  83.3 1.5 %peer2.1 = (f32[512,128]{1,0:T(8,128)S(1)}, f32[512,128]{1,0:T(8,128)S(1)}, f32[512,128]{1,0:T(8,128)S(1)}) custom-call(s32[1,4]{1,0:T(1,128)S(1)} %copy-done.4, bf16[512,128]{1,0:T(8,128)(2,1)S(1)} %q.1.q_ref.refs_1_, bf16[1024,128]{1,0:T(8,128)(2,1)S(1)} %collective-permute-done.4.refs_2_, f32[512,128]{1,0:T(8,128)S(1)} %get-tuple-element.29.refs_3_, ...), custom_call_target="tpu_custom_call" | custom-call | flops 268435456 | tf_op jit(solution)/shard_map/peer2/pallas_call | solution.py:222
  84.9 1.5 %peer3.1 = bf16[1024,128]{1,0:T(8,128)(2,1)S(1)} custom-call(s32[1,4]{1,0:T(1,128)S(1)} %copy-done.4, bf16[512,128]{1,0:T(8,128)(2,1)S(1)} %q.1.q_ref.refs_1_, bf16[1024,128]{1,0:T(8,128)(2,1)S(1)} %collective-permute-done.2.refs_2_, f32[512,128]{1,0:T(8,128)S(1)} %get-tuple-element.32.refs_3_, f32[512,128]{1,0:T(8,128)S(1)} %get-tuple-element.33.refs_4_, ...), custom_call_target="tpu_custom_call" | custom-call | flops 268435456 | tf_op jit(solution)/shard_map/peer3/pallas_call | solution.py:222
  86.4 2.2 %all-gather = bf16[2048,128]{1,0:T(8,128)(2,1)S(1)} all-gather(bf16[1024,128]{1,0:T(8,128)(2,1)S(1)} %peer3.1), channel_id=2, replica_groups=mesh['region'=128,'x'=4,'core'=2] {'core'}, dimensions={0}, use_global_device_ids=true | all-gather | bytes 786432 | tf_op jit(solution)/shard_map/all_gather | solution.py:299
  88.6 0.4 share.1
  89.1 12.7 %all_to_all.22.parts_ref = bf16[4,512,128]{2,1,0:T(8,128)(2,1)S(1)} all-to-all(bf16[4,512,128]{2,1,0:T(8,128)(2,1)S(1)} %share.1), channel_id=1, replica_groups=mesh['region'=128,'x'=4,'core'=2] {'x'}, dimensions={0} | all-to-all | bytes 1048576 | tf_op jit(solution)/shard_map/all_to_all | solution.py:19
  101.8 0.7 sum.1
  102.5 7.7 %all-to-all-start.3 = ((bf16[128,4,128]{2,1,0:T(4,128)(2,1)}), bf16[128,4,128]{2,1,0:T(4,128)(2,1)S(1)}, u32[]{:S(2)}, u32[]{:S(2)}) async-start(bf16[128,4,128]{2,1,0:T(4,128)(2,1)} %bitcast.5), calls=%async_computation.3 | async-start | bytes 262144 | tf_op jit(solution)/shard_map/all_to_all | solution.py:19
  110.2 0.1 copy.10
  110.4 0.1 eq.29
  110.5 0.4 hot.1.hot_ref
  110.9 1.3 %fusion.3 = f32[512,128]{1,0:T(8,128)} fusion(f32[512,128]{1,0:T(8,128)S(1)} %get-tuple-element.35, s32[512]{0:T(512)S(1)} %eq.29), kind=kOutput, calls=%fused_computation.6 | convolution fusion | flops 402915328 | bytes 526336 | tf_op jit(solution)/shard_map/dot_general | solution.py:307
  112.2 15.3 %all-to-all-done.3 = bf16[128,4,128]{2,1,0:T(4,128)(2,1)S(1)} async-done(((bf16[128,4,128]{2,1,0:T(4,128)(2,1)}), bf16[128,4,128]{2,1,0:T(4,128)(2,1)S(1)}, u32[]{:S(2)}, u32[]{:S(2)}) %all-to-all-start.3) | async-done | bytes 131104 | tf_op jit(solution)/shard_map/all_to_all | solution.py:19
  127.5 1.5 %decode.1 = bf16[2048,128]{1,0:T(8,128)(2,1)} custom-call(bf16[2048,512]{1,0:T(8,128)(2,1)S(1)} %hot.1.hot_ref, bf16[512,128]{1,0:T(8,128)(2,1)S(1)} %bitcast.11, bf16[2048,128]{1,0:T(8,128)(2,1)S(1)} %copy-done.2), custom_call_target="tpu_custom_call" | custom-call | tf_op jit(solution)/shard_map/decode/pallas_call | solution.py:222
  (15 shorter events, 0.0 us)
Async XLA Ops:
  0.6 58.4 %copy-start = (bf16[3,1024,128]{2,1,0:T(8,128)(2,1)S(1)}, bf16[3,1024,128]{2,1,0:T(8,128)(2,1)}, u32[]{:S(2)}) copy-start(bf16[3,1024,128]{2,1,0:T(8,128)(2,1)} %w_ref.6) | copy-start | bytes 2359300
  0.6 58.4 %copy-start.3 = (f32[1024]{0:T(1024)S(1)}, f32[1024]{0:T(1024)}, u32[]{:S(2)}) copy-start(f32[1024]{0:T(1024)} %param.13) | copy-start | bytes 12292
  57.2 3.8 %collective-permute-start = (bf16[4,512,128]{2,1,0:T(8,128)(2,1)S(1)}, bf16[4,512,128]{2,1,0:T(8,128)(2,1)S(1)}, u32[]{:S(2)}, u32[]{:S(2)}) collective-permute-start(bf16[4,512,128]{2,1,0:T(8,128)(2,1)S(1)} %all_to_all.21.own_ref), channel_id=1, source_target_pairs={{0,1},{1,0},{2,3},{3,2},{4,5},{5,4},{6,7},{7,6},{8,9},{9,8},{10,11... | collective-permute-start | bytes 1572872 | tf_op jit(solution)/shard_map/ppermute | solution.py:23
  61.5 16.4 %copy-start.4 = (s32[1,4]{1,0:T(1,128)S(1)}, s32[1,4]{1,0:T(1,128)}, u32[]{:S(2)}) copy-start(s32[1,4]{1,0:T(1,128)} %refs_0_.7) | copy-start | bytes 52
  61.5 9.5 %collective-permute-start.3 = (bf16[1024,128]{1,0:T(8,128)(2,1)S(1)}, bf16[1024,128]{1,0:T(8,128)(2,1)S(1)}, u32[]{:S(2)}, u32[]{:S(2)}) collective-permute-start(bf16[1024,128]{1,0:T(8,128)(2,1)S(1)} %kv.1.kv_ref), channel_id=1, source_target_pairs={{0,8},{1,1017},{8,0},{9,17},{16,24},{17,9},{24,16},{25,33},{32,40}... | collective-permute-start | bytes 786440 | tf_op jit(solution)/shard_map/ppermute | solution.py:34
  64.4 11.6 %collective-permute-start.1 = (bf16[1024,128]{1,0:T(8,128)(2,1)S(1)}, bf16[1024,128]{1,0:T(8,128)(2,1)S(1)}, u32[]{:S(2)}, u32[]{:S(2)}) collective-permute-start(bf16[1024,128]{1,0:T(8,128)(2,1)S(1)} %kv.1.kv_ref), channel_id=1, source_target_pairs={{0,1016},{1,9},{8,16},{9,1},{16,8},{17,25},{24,32},{25,17},{32,24}... | collective-permute-start | bytes 786440 | tf_op jit(solution)/shard_map/ppermute | solution.py:34
  67.3 17.6 %copy-start.1 = (bf16[128,1024]{1,0:T(8,128)(2,1)S(1)}, bf16[128,1024]{1,0:T(8,128)(2,1)}, u32[]{:S(2)}) copy-start(bf16[128,1024]{1,0:T(8,128)(2,1)} %w_ref.7) | copy-start | bytes 786436
  71.1 12.3 %collective-permute-start.4 = (bf16[1024,128]{1,0:T(8,128)(2,1)S(1)}, bf16[1024,128]{1,0:T(8,128)(2,1)S(1)}, u32[]{:S(2)}, u32[]{:S(2)}) collective-permute-start(bf16[1024,128]{1,0:T(8,128)(2,1)S(1)} %collective-permute-done.3.refs_2_), channel_id=1, source_target_pairs={{0,1016},{1,9},{8,16},{9,1},{16,8},{17,25},{24,32},{25,17},{32,24}... | collective-permute-start | bytes 786440 | tf_op jit(solution)/shard_map/ppermute | solution.py:34
  76.0 8.9 %collective-permute-start.2 = (bf16[1024,128]{1,0:T(8,128)(2,1)S(1)}, bf16[1024,128]{1,0:T(8,128)(2,1)S(1)}, u32[]{:S(2)}, u32[]{:S(2)}) collective-permute-start(bf16[1024,128]{1,0:T(8,128)(2,1)S(1)} %collective-permute-done.1.refs_2_), channel_id=1, source_target_pairs={{0,8},{1,1017},{8,0},{9,17},{16,24},{17,9},{24,16},{25,33},{32,40}... | collective-permute-start | bytes 786440 | tf_op jit(solution)/shard_map/ppermute | solution.py:34
  86.4 23.8 %copy-start.6 = (s32[1,128,4]{1,2,0:T(4,128)S(1)}, s32[1,128,4]{1,2,0:T(4,128)}, u32[]{:S(2)}) copy-start(s32[1,128,4]{1,2,0:T(4,128)} %param.11) | copy-start | bytes 6148
  86.4 24.1 %copy-start.5 = (s32[2048]{0:T(1024)S(1)}, s32[2048]{0:T(1024)}, u32[]{:S(2)}) copy-start(s32[2048]{0:T(1024)} %param.10) | copy-start | bytes 24580
  101.8 25.7 %copy-start.2 = (bf16[2048,128]{1,0:T(8,128)(2,1)S(1)}, bf16[2048,128]{1,0:T(8,128)(2,1)}, u32[]{:S(2)}) copy-start(bf16[2048,128]{1,0:T(8,128)(2,1)} %grid_ref.1) | copy-start | bytes 1572868
  102.5 25.0 %all-to-all-start.3 = ((bf16[128,4,128]{2,1,0:T(4,128)(2,1)}), bf16[128,4,128]{2,1,0:T(4,128)(2,1)S(1)}, u32[]{:S(2)}, u32[]{:S(2)}) async-start(bf16[128,4,128]{2,1,0:T(4,128)(2,1)} %bitcast.5), calls=%async_computation.3 | async-start | bytes 262144 | tf_op jit(solution)/shard_map/all_to_all | solution.py:19

commit v8 on v7

--- a/solution.py
+++ b/solution.py
@@ -212,9 +212,17 @@
         hot_ref[i * lanes : (i + 1) * lanes, :] = jnp.where(number == wanted, 1.0, 0.0).astype(BF16)
 
 
-def decode_kernel(hot_ref, returned_ref, grid_ref, out_ref):
-    back = jnp.dot(hot_ref[...], returned_ref[...], preferred_element_type=F32)
-    out_ref[...] = (grid_ref[...].astype(F32) + back).astype(BF16)
+def decode_kernel(hot_ref, returned_ref, grid_ref, out_ref, part_ref, sems):
+    parts, rows, _ = part_ref.shape
+    copies = []
+    for i in range(parts):
+        at = pl.ds(i * rows, rows)
+        back = jnp.dot(hot_ref[at, :], returned_ref[...], preferred_element_type=F32)
+        part_ref[i] = (grid_ref[at, :].astype(F32) + back).astype(BF16)
+        copies.append(pltpu.make_async_copy(part_ref.at[i], out_ref.at[at], sems.at[i]))
+        copies[i].start()
+    for copy in copies:
+        copy.wait()
 
 
 def call(kernel, outs, name, scratch=(), flops=0, bytes_accessed=0, transcendentals=0):
@@ -310,8 +318,18 @@
     hots = jax.ShapeDtypeStruct((grid.shape[0], slots), BF16)
     slot_rows = after(g2m_slot.reshape(-1, width), mesh_back)
     hot = call(hot_kernel, hots, "hot", bytes_accessed=1 << 21)(slot_rows)
-    outs = jax.ShapeDtypeStruct(grid.shape, BF16)
-    grid_out = call(decode_kernel, outs, "decode")(hot, returned, grid)
+    grid_out = pl.pallas_call(
+        decode_kernel,
+        out_shape=jax.ShapeDtypeStruct(grid.shape, BF16),
+        in_specs=[VMEM] * 3,
+        out_specs=pl.BlockSpec(memory_space=pl.ANY),
+        scratch_shapes=[
+            pltpu.VMEM((4, grid.shape[0] // 4, width), BF16),
+            pltpu.SemaphoreType.DMA((4,)),
+        ],
+        compiler_params=PARAMS,
+        name="decode",
+    )(hot, returned, grid)
     return (mesh_state, grid_out)
 
 

time: 130 us -> 130 us (level)
    pallas_call x12 -> x11, Pallas kernels: 12 us -> 10.5 us  [run(): pl.pallas_call(kernel, out_shape=outs, in_specs=[VMEM] * len(args), out_s...]
    pallas_call x0 -> x1, Pallas kernels: none -> 1.41 us  [on_device(): pl.pallas_call(decode_kernel, out_shape=jax.ShapeDtypeStruct(grid.shape,...]
where the time goes in v8:
time: 130 us; the launch traced here: 129 us
  blocking collectives  69.3 us (53%)
  waiting for transfers between devices  22.2 us (17%)
  starting transfers between devices  21 us (16%)
  Pallas kernels  11.9 us (9%)
  matrix products  3.38 us (3%)
    all_to_all x3, blocking collectives, exchange(): return lax.all_to_all(array, axis, split_axis=0, concat_axis=0, tiled=True)  67.1 us
    all_to_all x1, waiting for transfers between devices, exchange(): return lax.all_to_all(array, axis, split_axis=0, concat_axis=0, tiled=True)  15.3 us
    ppermute x4, starting transfers between devices, swapped(): return lax.ppermute(value, (axis, 'core'), pairs)  11.3 us
    pallas_call x11, Pallas kernels, run(): pl.pallas_call(kernel, out_shape=outs, in_specs=[VMEM] * len(args), out_s...  10.5 us
    all_to_all x1, starting transfers between devices, exchange(): return lax.all_to_all(array, axis, split_axis=0, concat_axis=0, tiled=True)  7.72 us
    ppermute x4, waiting for transfers between devices, swapped(): return lax.ppermute(value, (axis, 'core'), pairs)  5.73 us
  transfers between devices with their start and end apart: 6, of which 5 were waited for; matrix products, arithmetic and copies ran while one was open for 1% of the time, Pallas kernels for 6%

profile of v8, /device:TPU:6, one launch (start us, length us, event | category | flops | bytes accessed | tf_op | source)
XLA Modules:
  0.0 129.1 jit_solution(17381897754164354252)
XLA Ops:
  0.7 2.1 %fusion.2 = bf16[512,128]{1,0:T(8,128)(2,1)S(1)} fusion(s32[2048]{0:T(1024)} %param.10, bf16[2048,128]{1,0:T(8,128)(2,1)} %grid_ref.1, f32[2048]{0:T(1024)} %param.9), kind=kOutput, calls=%fused_computation.3 | convolution fusion | flops 270336000 | bytes 671744 | tf_op jit(solution)/shard_map/dot_general | solution.py:259
  2.7 43.8 %all_to_all.20 = bf16[128,4,128]{2,1,0:T(4,128)(2,1)S(1)} all-to-all(bf16[128,4,128]{2,1,0:T(4,128)(2,1)S(1)} %bitcast.16), channel_id=1, replica_groups=mesh['region'=128,'x'=4,'core'=2] {'region'}, dimensions={0} | all-to-all | bytes 262144 | tf_op jit(solution)/shard_map/all_to_all | solution.py:19
  46.5 0.1 broadcast_in_dim.2
  46.6 10.6 %all_to_all.21.own_ref = bf16[4,512,128]{2,1,0:T(8,128)(2,1)S(1)} all-to-all(bf16[4,512,128]{2,1,0:T(8,128)(2,1)S(1)} %broadcast_in_dim.2), channel_id=1, replica_groups=mesh['region'=128,'x'=4,'core'=2] {'x'}, dimensions={0} | all-to-all | bytes 1048576 | tf_op jit(solution)/shard_map/all_to_all | solution.py:19
  57.2 1.9 %collective-permute-start = (bf16[4,512,128]{2,1,0:T(8,128)(2,1)S(1)}, bf16[4,512,128]{2,1,0:T(8,128)(2,1)S(1)}, u32[]{:S(2)}, u32[]{:S(2)}) collective-permute-start(bf16[4,512,128]{2,1,0:T(8,128)(2,1)S(1)} %all_to_all.21.own_ref), channel_id=1, source_target_pairs={{0,1},{1,0},{2,3},{3,2},{4,5},{5,4},{6,7},{7,6},{8,9},{9,8},{10,11... | collective-permute-start | bytes 1572872 | tf_op jit(solution)/shard_map/ppermute | solution.py:23
  59.1 0.7 own_half.1
  59.8 1.2 collective-permute-done.other_ref
  61.0 0.6 kv.1.kv_ref
  61.5 2.9 %collective-permute-start.3 = (bf16[1024,128]{1,0:T(8,128)(2,1)S(1)}, bf16[1024,128]{1,0:T(8,128)(2,1)S(1)}, u32[]{:S(2)}, u32[]{:S(2)}) collective-permute-start(bf16[1024,128]{1,0:T(8,128)(2,1)S(1)} %kv.1.kv_ref), channel_id=1, source_target_pairs={{0,8},{1,1017},{8,0},{9,17},{16,24},{17,9},{24,16},{25,33},{32,40}... | collective-permute-start | bytes 786440 | tf_op jit(solution)/shard_map/ppermute | solution.py:34
  64.4 2.4 %collective-permute-start.1 = (bf16[1024,128]{1,0:T(8,128)(2,1)S(1)}, bf16[1024,128]{1,0:T(8,128)(2,1)S(1)}, u32[]{:S(2)}, u32[]{:S(2)}) collective-permute-start(bf16[1024,128]{1,0:T(8,128)(2,1)S(1)} %kv.1.kv_ref), channel_id=1, source_target_pairs={{0,1016},{1,9},{8,16},{9,1},{16,8},{17,25},{24,32},{25,17},{32,24}... | collective-permute-start | bytes 786440 | tf_op jit(solution)/shard_map/ppermute | solution.py:34
  66.8 0.5 q.1.q_ref.refs_1_
  67.3 1.2 own.1
  68.5 2.6 %collective-permute-done.3.refs_2_ = bf16[1024,128]{1,0:T(8,128)(2,1)S(1)} collective-permute-done((bf16[1024,128]{1,0:T(8,128)(2,1)S(1)}, bf16[1024,128]{1,0:T(8,128)(2,1)S(1)}, u32[]{:S(2)}, u32[]{:S(2)}) %collective-permute-start.3) | collective-permute-done | bytes 262176 | tf_op jit(solution)/shard_map/ppermute | solution.py:34
  71.1 4.2 %collective-permute-start.4 = (bf16[1024,128]{1,0:T(8,128)(2,1)S(1)}, bf16[1024,128]{1,0:T(8,128)(2,1)S(1)}, u32[]{:S(2)}, u32[]{:S(2)}) collective-permute-start(bf16[1024,128]{1,0:T(8,128)(2,1)S(1)} %collective-permute-done.3.refs_2_), channel_id=1, source_target_pairs={{0,1016},{1,9},{8,16},{9,1},{16,8},{17,25},{24,32},{25,17},{32,24}... | collective-permute-start | bytes 786440 | tf_op jit(solution)/shard_map/ppermute | solution.py:34
  75.3 0.7 collective-permute-done.1.refs_2_
  76.0 1.9 %collective-permute-start.2 = (bf16[1024,128]{1,0:T(8,128)(2,1)S(1)}, bf16[1024,128]{1,0:T(8,128)(2,1)S(1)}, u32[]{:S(2)}, u32[]{:S(2)}) collective-permute-start(bf16[1024,128]{1,0:T(8,128)(2,1)S(1)} %collective-permute-done.1.refs_2_), channel_id=1, source_target_pairs={{0,8},{1,1017},{8,0},{9,17},{16,24},{17,9},{24,16},{25,33},{32,40}... | collective-permute-start | bytes 786440 | tf_op jit(solution)/shard_map/ppermute | solution.py:34
  77.9 1.5 %peer0.1 = (f32[512,128]{1,0:T(8,128)S(1)}, f32[512,128]{1,0:T(8,128)S(1)}, f32[512,128]{1,0:T(8,128)S(1)}) custom-call(s32[1,4]{1,0:T(1,128)S(1)} %copy-done.4, bf16[512,128]{1,0:T(8,128)(2,1)S(1)} %q.1.q_ref.refs_1_, bf16[1024,128]{1,0:T(8,128)(2,1)S(1)} %collective-permute-done.3.refs_2_, f32[512,128]{1,0:T(8,128)S(1)} %get-tuple-element.22.refs_3_, ...), custom_call_target="tpu_custom_call" | custom-call | flops 268435456 | tf_op jit(solution)/shard_map/peer0/pallas_call | solution.py:230
  79.4 1.5 %peer1.1 = (f32[512,128]{1,0:T(8,128)S(1)}, f32[512,128]{1,0:T(8,128)S(1)}, f32[512,128]{1,0:T(8,128)S(1)}) custom-call(s32[1,4]{1,0:T(1,128)S(1)} %copy-done.4, bf16[512,128]{1,0:T(8,128)(2,1)S(1)} %q.1.q_ref.refs_1_, bf16[1024,128]{1,0:T(8,128)(2,1)S(1)} %collective-permute-done.1.refs_2_, f32[512,128]{1,0:T(8,128)S(1)} %get-tuple-element.26.refs_3_, ...), custom_call_target="tpu_custom_call" | custom-call | flops 268435456 | tf_op jit(solution)/shard_map/peer1/pallas_call | solution.py:230
  80.9 2.4 %collective-permute-done.4.refs_2_ = bf16[1024,128]{1,0:T(8,128)(2,1)S(1)} collective-permute-done((bf16[1024,128]{1,0:T(8,128)(2,1)S(1)}, bf16[1024,128]{1,0:T(8,128)(2,1)S(1)}, u32[]{:S(2)}, u32[]{:S(2)}) %collective-permute-start.4) | collective-permute-done | bytes 262176 | tf_op jit(solution)/shard_map/ppermute | solution.py:34
  83.3 1.5 %peer2.1 = (f32[512,128]{1,0:T(8,128)S(1)}, f32[512,128]{1,0:T(8,128)S(1)}, f32[512,128]{1,0:T(8,128)S(1)}) custom-call(s32[1,4]{1,0:T(1,128)S(1)} %copy-done.4, bf16[512,128]{1,0:T(8,128)(2,1)S(1)} %q.1.q_ref.refs_1_, bf16[1024,128]{1,0:T(8,128)(2,1)S(1)} %collective-permute-done.4.refs_2_, f32[512,128]{1,0:T(8,128)S(1)} %get-tuple-element.29.refs_3_, ...), custom_call_target="tpu_custom_call" | custom-call | flops 268435456 | tf_op jit(solution)/shard_map/peer2/pallas_call | solution.py:230
  84.9 1.5 %peer3.1 = bf16[1024,128]{1,0:T(8,128)(2,1)S(1)} custom-call(s32[1,4]{1,0:T(1,128)S(1)} %copy-done.4, bf16[512,128]{1,0:T(8,128)(2,1)S(1)} %q.1.q_ref.refs_1_, bf16[1024,128]{1,0:T(8,128)(2,1)S(1)} %collective-permute-done.2.refs_2_, f32[512,128]{1,0:T(8,128)S(1)} %get-tuple-element.32.refs_3_, f32[512,128]{1,0:T(8,128)S(1)} %get-tuple-element.33.refs_4_, ...), custom_call_target="tpu_custom_call" | custom-call | flops 268435456 | tf_op jit(solution)/shard_map/peer3/pallas_call | solution.py:230
  86.4 2.2 %all-gather = bf16[2048,128]{1,0:T(8,128)(2,1)S(1)} all-gather(bf16[1024,128]{1,0:T(8,128)(2,1)S(1)} %peer3.1), channel_id=2, replica_groups=mesh['region'=128,'x'=4,'core'=2] {'core'}, dimensions={0}, use_global_device_ids=true | all-gather | bytes 786432 | tf_op jit(solution)/shard_map/all_gather | solution.py:307
  88.6 0.4 share.1
  89.1 12.7 %all_to_all.22.parts_ref = bf16[4,512,128]{2,1,0:T(8,128)(2,1)S(1)} all-to-all(bf16[4,512,128]{2,1,0:T(8,128)(2,1)S(1)} %share.1), channel_id=1, replica_groups=mesh['region'=128,'x'=4,'core'=2] {'x'}, dimensions={0} | all-to-all | bytes 1048576 | tf_op jit(solution)/shard_map/all_to_all | solution.py:19
  101.8 0.7 sum.1
  102.5 7.7 %all-to-all-start.3 = ((bf16[128,4,128]{2,1,0:T(4,128)(2,1)}), bf16[128,4,128]{2,1,0:T(4,128)(2,1)S(1)}, u32[]{:S(2)}, u32[]{:S(2)}) async-start(bf16[128,4,128]{2,1,0:T(4,128)(2,1)} %bitcast.5), calls=%async_computation.3 | async-start | bytes 262144 | tf_op jit(solution)/shard_map/all_to_all | solution.py:19
  110.2 0.1 copy.10
  110.4 0.1 eq.29
  110.5 0.4 hot.1.hot_ref
  110.9 1.3 %fusion.3 = f32[512,128]{1,0:T(8,128)} fusion(f32[512,128]{1,0:T(8,128)S(1)} %get-tuple-element.35, s32[512]{0:T(512)S(1)} %eq.29), kind=kOutput, calls=%fused_computation.6 | convolution fusion | flops 402915328 | bytes 526336 | tf_op jit(solution)/shard_map/dot_general | solution.py:315
  112.2 15.3 %all-to-all-done.3 = bf16[128,4,128]{2,1,0:T(4,128)(2,1)S(1)} async-done(((bf16[128,4,128]{2,1,0:T(4,128)(2,1)}), bf16[128,4,128]{2,1,0:T(4,128)(2,1)S(1)}, u32[]{:S(2)}, u32[]{:S(2)}) %all-to-all-start.3) | async-done | bytes 131104 | tf_op jit(solution)/shard_map/all_to_all | solution.py:19
  127.5 1.4 %decode.1 = bf16[2048,128]{1,0:T(8,128)(2,1)} custom-call(bf16[2048,512]{1,0:T(8,128)(2,1)S(1)} %hot.1.hot_ref, bf16[512,128]{1,0:T(8,128)(2,1)S(1)} %bitcast.11, bf16[2048,128]{1,0:T(8,128)(2,1)S(1)} %copy-done.2), custom_call_target="tpu_custom_call" | custom-call | tf_op jit(solution)/shard_map/decode/pallas_call | solution.py:321
  (15 shorter events, 0.0 us)
Async XLA Ops:
  0.6 58.4 %copy-start = (bf16[3,1024,128]{2,1,0:T(8,128)(2,1)S(1)}, bf16[3,1024,128]{2,1,0:T(8,128)(2,1)}, u32[]{:S(2)}) copy-start(bf16[3,1024,128]{2,1,0:T(8,128)(2,1)} %w_ref.6) | copy-start | bytes 2359300
  0.6 58.4 %copy-start.3 = (f32[1024]{0:T(1024)S(1)}, f32[1024]{0:T(1024)}, u32[]{:S(2)}) copy-start(f32[1024]{0:T(1024)} %param.13) | copy-start | bytes 12292
  57.2 3.8 %collective-permute-start = (bf16[4,512,128]{2,1,0:T(8,128)(2,1)S(1)}, bf16[4,512,128]{2,1,0:T(8,128)(2,1)S(1)}, u32[]{:S(2)}, u32[]{:S(2)}) collective-permute-start(bf16[4,512,128]{2,1,0:T(8,128)(2,1)S(1)} %all_to_all.21.own_ref), channel_id=1, source_target_pairs={{0,1},{1,0},{2,3},{3,2},{4,5},{5,4},{6,7},{7,6},{8,9},{9,8},{10,11... | collective-permute-start | bytes 1572872 | tf_op jit(solution)/shard_map/ppermute | solution.py:23
  61.5 16.4 %copy-start.4 = (s32[1,4]{1,0:T(1,128)S(1)}, s32[1,4]{1,0:T(1,128)}, u32[]{:S(2)}) copy-start(s32[1,4]{1,0:T(1,128)} %refs_0_.7) | copy-start | bytes 52
  61.5 9.5 %collective-permute-start.3 = (bf16[1024,128]{1,0:T(8,128)(2,1)S(1)}, bf16[1024,128]{1,0:T(8,128)(2,1)S(1)}, u32[]{:S(2)}, u32[]{:S(2)}) collective-permute-start(bf16[1024,128]{1,0:T(8,128)(2,1)S(1)} %kv.1.kv_ref), channel_id=1, source_target_pairs={{0,8},{1,1017},{8,0},{9,17},{16,24},{17,9},{24,16},{25,33},{32,40}... | collective-permute-start | bytes 786440 | tf_op jit(solution)/shard_map/ppermute | solution.py:34
  64.4 11.6 %collective-permute-start.1 = (bf16[1024,128]{1,0:T(8,128)(2,1)S(1)}, bf16[1024,128]{1,0:T(8,128)(2,1)S(1)}, u32[]{:S(2)}, u32[]{:S(2)}) collective-permute-start(bf16[1024,128]{1,0:T(8,128)(2,1)S(1)} %kv.1.kv_ref), channel_id=1, source_target_pairs={{0,1016},{1,9},{8,16},{9,1},{16,8},{17,25},{24,32},{25,17},{32,24}... | collective-permute-start | bytes 786440 | tf_op jit(solution)/shard_map/ppermute | solution.py:34
  67.3 17.6 %copy-start.1 = (bf16[128,1024]{1,0:T(8,128)(2,1)S(1)}, bf16[128,1024]{1,0:T(8,128)(2,1)}, u32[]{:S(2)}) copy-start(bf16[128,1024]{1,0:T(8,128)(2,1)} %w_ref.7) | copy-start | bytes 786436
  71.1 12.3 %collective-permute-start.4 = (bf16[1024,128]{1,0:T(8,128)(2,1)S(1)}, bf16[1024,128]{1,0:T(8,128)(2,1)S(1)}, u32[]{:S(2)}, u32[]{:S(2)}) collective-permute-start(bf16[1024,128]{1,0:T(8,128)(2,1)S(1)} %collective-permute-done.3.refs_2_), channel_id=1, source_target_pairs={{0,1016},{1,9},{8,16},{9,1},{16,8},{17,25},{24,32},{25,17},{32,24}... | collective-permute-start | bytes 786440 | tf_op jit(solution)/shard_map/ppermute | solution.py:34
  76.0 8.9 %collective-permute-start.2 = (bf16[1024,128]{1,0:T(8,128)(2,1)S(1)}, bf16[1024,128]{1,0:T(8,128)(2,1)S(1)}, u32[]{:S(2)}, u32[]{:S(2)}) collective-permute-start(bf16[1024,128]{1,0:T(8,128)(2,1)S(1)} %collective-permute-done.1.refs_2_), channel_id=1, source_target_pairs={{0,8},{1,1017},{8,0},{9,17},{16,24},{17,9},{24,16},{25,33},{32,40}... | collective-permute-start | bytes 786440 | tf_op jit(solution)/shard_map/ppermute | solution.py:34
  86.4 23.8 %copy-start.6 = (s32[1,128,4]{1,2,0:T(4,128)S(1)}, s32[1,128,4]{1,2,0:T(4,128)}, u32[]{:S(2)}) copy-start(s32[1,128,4]{1,2,0:T(4,128)} %param.11) | copy-start | bytes 6148
  86.4 24.1 %copy-start.5 = (s32[2048]{0:T(1024)S(1)}, s32[2048]{0:T(1024)}, u32[]{:S(2)}) copy-start(s32[2048]{0:T(1024)} %param.10) | copy-start | bytes 24580
  101.8 25.7 %copy-start.2 = (bf16[2048,128]{1,0:T(8,128)(2,1)S(1)}, bf16[2048,128]{1,0:T(8,128)(2,1)}, u32[]{:S(2)}) copy-start(bf16[2048,128]{1,0:T(8,128)(2,1)} %grid_ref.1) | copy-start | bytes 1572868
  102.5 25.0 %all-to-all-start.3 = ((bf16[128,4,128]{2,1,0:T(4,128)(2,1)}), bf16[128,4,128]{2,1,0:T(4,128)(2,1)S(1)}, u32[]{:S(2)}, u32[]{:S(2)}) async-start(bf16[128,4,128]{2,1,0:T(4,128)(2,1)} %bitcast.5), calls=%async_computation.3 | async-start | bytes 262144 | tf_op jit(solution)/shard_map/all_to_all | solution.py:19
